TPU v7x, 32 devices: a whole 2x2x4 slice. The times are simulated.
32 devices in a mesh: tmpl: 1, freq: 32 (over z, y, x, core).
Axes of the slice: x: 2, y: 2, z: 4, core: 2. Of those that a mesh axis runs over, the one named last changes fastest.
Arguments:
- strain: float32 [512, 512], P('freq'), may hold values from -6 to 6
- inv_asd: float32 [512, 512], P('freq'), may hold values from 0.25 to 4
- spectra: bfloat16 [512, 4, 2, 512], P('freq', 'tmpl'), may hold values from -6 to 6
- cutoff: int32 [4], P('tmpl'), may hold values from 64 to 256
Outputs:
- filter_series: float32 [4, 2, 512, 512], P('tmpl', None, 'freq')
- peak_power: float32 [512, 512], P('freq')
All inputs are finite; a program needn't handle non-finite values.
Results may differ from a plain program's by a relative error of at most 0.0051.
Values may be sent and summed in bfloat16 or wider, within the bound.
No kernel may reach another device: no remote copies, remote signals or barrier semaphores. Data moves between devices by JAX's collectives and lax.ppermute only.
A program may use at most 64 MiB of HBM per device.

v0:
```python
import math

import jax
import jax.numpy as jnp
from jax import lax
from jax.sharding import PartitionSpec as P


def angle_table(left, right, modulus):
    product = left[:, None] * right[None, :] % modulus
    return 2.0 * math.pi / modulus * product.astype(jnp.float32)


def exact_dot(left, right):
    return jnp.dot(left, right, precision=lax.Precision.HIGHEST, preferred_element_type=jnp.float32)


def inverse_first(product, section_table, twist_cos, twist_sin):
    turned = jnp.einsum(
        "ktcj,cjdm->kmtd", product, section_table, preferred_element_type=jnp.float32
    )
    real_part = turned[..., 0]
    imag_part = turned[..., 1]
    rotated = jnp.stack(
        [
            real_part * twist_cos[:, :, None] - imag_part * twist_sin[:, :, None],
            real_part * twist_sin[:, :, None] + imag_part * twist_cos[:, :, None],
        ],
        -1,
    ).astype(jnp.bfloat16)
    return rotated.reshape(rotated.shape[0], -1)


def inverse_last(received, templ_count, last_table, total_size):
    side_size = received.shape[0]
    arranged = received.reshape(side_size, -1, templ_count, 2)
    return jnp.einsum(
        "kmtc,kcdn->tdmn", arranged, last_table, preferred_element_type=jnp.float32
    ) * (1.0 / total_size)


def local(strain, inv_asd, spectra, cutoff):
    row_count = strain.shape[0]
    side_size = strain.shape[1]
    total_size = side_size * side_size
    templ_count = spectra.shape[1]
    positions = jnp.arange(side_size, dtype=jnp.int32)
    local_rows = lax.axis_index("freq") * row_count + jnp.arange(row_count, dtype=jnp.int32)
    full_angle = angle_table(positions, positions, side_size)
    cosines = jnp.cos(full_angle)
    sine_part = jnp.sin(full_angle)
    row_angle = angle_table(local_rows, positions, total_size)
    row_cos = jnp.cos(row_angle)
    row_sin = jnp.sin(row_angle)
    columns = lax.all_to_all(strain, "freq", split_axis=1, concat_axis=0, tiled=True)
    first_real = exact_dot(cosines, columns)
    first_imag = -exact_dot(sine_part, columns)
    twist_angle = angle_table(positions, local_rows, total_size)
    twist_cos = jnp.cos(twist_angle)
    twist_sin = jnp.sin(twist_angle)
    turned = jnp.stack(
        [
            first_real * twist_cos + first_imag * twist_sin,
            first_imag * twist_cos - first_real * twist_sin,
        ],
        1,
    )
    returned = lax.all_to_all(turned, "freq", split_axis=0, concat_axis=2, tiled=True)
    mid_real = returned[:, 0]
    mid_imag = returned[:, 1]
    white_real = (exact_dot(mid_real, cosines) + exact_dot(mid_imag, sine_part)) * inv_asd
    white_imag = (exact_dot(mid_imag, cosines) - exact_dot(mid_real, sine_part)) * inv_asd
    band_mask = (positions[None, :] < cutoff[:, None]).astype(jnp.float32)[None]
    spec_real = spectra[:, :, 0].astype(jnp.float32)
    spec_imag = spectra[:, :, 1].astype(jnp.float32)
    prod_real = (white_real[:, None] * spec_real + white_imag[:, None] * spec_imag) * band_mask
    prod_imag = (white_imag[:, None] * spec_real - white_real[:, None] * spec_imag) * band_mask
    product = jnp.stack([prod_real, prod_imag], 2).astype(jnp.bfloat16)
    base_table = jnp.stack(
        [jnp.stack([cosines, sine_part]), jnp.stack([-sine_part, cosines])]
    ).astype(jnp.bfloat16)
    section_table = jnp.transpose(base_table, (0, 2, 1, 3))
    last_table = jnp.transpose(base_table, (2, 0, 1, 3))
    outgoing = inverse_first(product, section_table, row_cos, row_sin)
    received = lax.all_to_all(outgoing, "freq", split_axis=1, concat_axis=0, tiled=True)
    filter_series = inverse_last(received, templ_count, last_table, total_size)
    power_sum = filter_series[:, 0] ** 2 + filter_series[:, 1] ** 2
    peak_power = lax.pmax(jnp.max(power_sum, axis=0), "tmpl")
    return (filter_series, peak_power)


def solution(mesh):
    in_specs = (P("freq", None), P("freq", None), P("freq", "tmpl", None, None), P("tmpl"))
    out_specs = (P("tmpl", None, "freq", None), P("freq", None))
    return jax.shard_map(local, mesh=mesh, in_specs=in_specs, out_specs=out_specs, check_vma=False)
```

profile of v0, /device:TPU:0, one launch (start us, length us, event | category | flops | bytes accessed | tf_op | source)
XLA Modules:
  0.0 81.3 jit_solution(13989062648599011347)
XLA Ops:
  0.6 0.9 %all_to_all.37 = f32[16,32,16]{2,1,0:T(8,128)S(1)} reshape(f32[16,512]{1,0:T(8,128)} %param.4) | data formatting | bytes 65536 | tf_op jit(solution)/shard_map/all_to_all | solution.py:55
  1.7 0.8 reshape.188
  2.5 7.3 %all-to-all-start = ((f32[32,1,256]{2,1,0:T(1,128)}), f32[32,1,256]{2,1,0:T(1,128)S(1)}, u32[]{:S(2)}, u32[]{:S(2)}) async-start(f32[32,1,256]{2,1,0:T(1,128)} %reshape.188), calls=%async_computation | async-start | bytes 65536 | tf_op jit(solution)/shard_map/all_to_all | solution.py:55
  9.8 4.3 %negate_convert_fusion = (bf16[1,512,512]{2,1,0:T(8,128)(2,1)S(1)}, bf16[1,512,512]{2,1,0:T(8,128)(2,1)S(1)}) fusion(), kind=kLoop, calls=%fused_computation.30 | loop fusion | flops 4456448 | bytes 1048576 | tf_op jit(solution)/shard_map/convert.7
  14.6 4.0 %fusion.42 = bf16[1,512,512]{2,1,0:T(8,128)(2,1)S(1)} fusion(), kind=kLoop, calls=%fused_computation.43 | loop fusion | flops 3932160 | bytes 524288 | tf_op jit(solution)/shard_map/convert.11
  19.1 0.7 reduce.1
  20.0 5.0 %convolution_negate_fusion = f32[512,16]{0,1:T(8,128)S(1)} fusion(f32[512,16]{1,0:T(8,128)S(1)} %bitcast.87), kind=kOutput, calls=%fused_computation.19 | convolution fusion | flops 54009856 | bytes 65536 | tf_op jit(solution)/shard_map/dot_general | solution.py:15
  25.0 4.8 %add_bitcast_fusion = (f32[512,1,16]{0,2,1:T(8,128)S(1)}, f32[512,1,16]{0,2,1:T(8,128)S(1)}) fusion(f32[512,16]{0,1:T(8,128)S(1)} %convolution_negate_fusion, s32[16]{0:T(128)S(1)} %iota_add_fusion, f32[512,16]{1,0:T(8,128)S(1)} %bitcast.88), kind=kOutput, calls=%fused_computation.84 | convolution fusion | flops 54165504 | bytes 131136 | tf_op jit(solution)/shard_map/dot_general | solution.py:15
  30.1 1.4 %reshape.190 = f32[32,1,512]{2,1,0:T(1,128)} reshape(f32[512,2,16]{2,1,0:T(2,128)S(1)} %copy.22) | data formatting | bytes 131072
  31.4 6.0 %all-to-all-start.1 = ((f32[32,1,512]{2,1,0:T(1,128)}), f32[32,1,512]{2,1,0:T(1,128)S(1)}, u32[]{:S(2)}, u32[]{:S(2)}) async-start(f32[32,1,512]{2,1,0:T(1,128)} %reshape.190), calls=%async_computation.1 | async-start | bytes 131072 | tf_op jit(solution)/shard_map/all_to_all | solution.py:68
  37.5 1.2 %maximum_bitcast_fusion = (bf16[1,2,512,512]{3,2,0,1:T(8,128)(2,1)S(1)}, bf16[1,2,512,512]{3,2,0,1:T(8,128)(2,1)}) fusion(bf16[1,512,512]{2,1,0:T(8,128)(2,1)S(1)} %fusion.42, bf16[1,512,512]{2,1,0:T(8,128)(2,1)S(1)} %get-tuple-element.21, bf16[1,512,512]{2,1,0:T(8,128)(2,1)S(1)} %get-tuple-element.20), kind=kLoop, calls=%fused_computation.26 | loop fusion | flops 1048576 | bytes 3670016 | tf_op jit(solution)/shard_map/stack | solution.py:79
  38.6 6.1 %all-to-all-done.1 = f32[32,1,512]{2,1,0:T(1,128)S(1)} async-done(((f32[32,1,512]{2,1,0:T(1,128)}), f32[32,1,512]{2,1,0:T(1,128)S(1)}, u32[]{:S(2)}, u32[]{:S(2)}) %all-to-all-start.1) | async-done | bytes 65568 | tf_op jit(solution)/shard_map/all_to_all | solution.py:68
  44.7 0.8 reduce.2
  45.5 0.7 reshape.191
  46.8 4.6 %fusion.32 = f32[16,512]{1,0:T(8,128)S(1)} fusion(f32[16,2,512]{2,0,1:T(8,128)S(1)} %all_to_all.44), kind=kOutput, calls=%fused_computation.39 | convolution fusion | flops 54001664 | bytes 65536 | tf_op jit(solution)/shard_map/dot_general | solution.py:15
  51.4 4.6 %fusion.34 = f32[16,512]{1,0:T(8,128)S(1)} fusion(f32[16,2,512]{2,0,1:T(8,128)S(1)} %all_to_all.44), kind=kOutput, calls=%fused_computation.40 | convolution fusion | flops 54001664 | bytes 65536 | tf_op jit(solution)/shard_map/dot_general | solution.py:15
  55.9 4.6 %fusion.16 = f32[16,512]{1,0:T(8,128)S(1)} fusion(f32[16,512]{1,0:T(8,128)S(1)} %copy-done.3, f32[16,512]{1,0:T(8,128)S(1)} %fusion.32, f32[16,2,512]{2,0,1:T(8,128)S(1)} %all_to_all.44), kind=kOutput, calls=%fused_computation.16 | convolution fusion | flops 54018048 | bytes 131072 | tf_op jit(solution)/shard_map/dot_general | solution.py:15
  60.6 4.6 %fusion.17 = f32[16,512]{1,0:T(8,128)S(1)} fusion(f32[16,512]{1,0:T(8,128)S(1)} %copy-done.3, f32[16,512]{1,0:T(8,128)S(1)} %fusion.34, f32[16,2,512]{2,0,1:T(8,128)S(1)} %all_to_all.44), kind=kOutput, calls=%fused_computation.18 | convolution fusion | flops 54018048 | bytes 131072 | tf_op jit(solution)/shard_map/dot_general | solution.py:15
  65.8 0.8 copy.27
  66.9 9.9 %all_to_all.50 = bf16[16,32,128]{2,0,1:T(8,128)(2,1)S(1)} all-to-all(bf16[16,32,128]{2,0,1:T(8,128)(2,1)S(1)} %copy.28), channel_id=1, replica_groups=mesh['tmpl'=1,'freq'=32] {'freq'}, dimensions={1} | all-to-all | bytes 262144 | tf_op jit(solution)/shard_map/all_to_all | solution.py:85
  76.9 1.4 %copy.29 = bf16[32,16,128]{1,0,2:T(8,128)(2,1)S(1)} copy(bf16[32,16,128]{2,1,0:T(8,128)(2,1)S(1)} %bitcast.86) | data formatting | bytes 262144 | tf_op jit(solution)/shard_map/all_to_all | solution.py:85
  78.3 1.1 %reshape.181 = bf16[512,16,4,2]{0,3,2,1:T(2,128)(2,1)S(1)} reshape(bf16[32,16,128]{1,0,2:T(8,128)(2,1)S(1)} %copy.29) | data formatting | bytes 262144 | tf_op jit(solution)/shard_map/reshape | solution.py:36
  79.9 0.7 copy.31
  80.6 0.6 fusion.50
  (26 shorter events, 3.5 us)
Async XLA Ops:
  0.6 13.5 %copy-start.2 = (s32[4]{0:T(128)S(1)}, s32[4]{0:T(128)}, u32[]{:S(2)}) copy-start(s32[4]{0:T(128)} %param.7) | copy-start | bytes 52
  1.5 12.7 %copy-start.1 = (bf16[16,4,2,512]{3,2,1,0:T(2,128)(2,1)S(1)}, bf16[16,4,2,512]{3,2,1,0:T(2,128)(2,1)}, u32[]{:S(2)}) copy-start(bf16[16,4,2,512]{3,2,1,0:T(2,128)(2,1)} %param.6) | copy-start | bytes 393220
  2.5 16.1 %all-to-all-start = ((f32[32,1,256]{2,1,0:T(1,128)}), f32[32,1,256]{2,1,0:T(1,128)S(1)}, u32[]{:S(2)}, u32[]{:S(2)}) async-start(f32[32,1,256]{2,1,0:T(1,128)} %reshape.188), calls=%async_computation | async-start | bytes 65536 | tf_op jit(solution)/shard_map/all_to_all | solution.py:55
  31.4 13.2 %all-to-all-start.1 = ((f32[32,1,512]{2,1,0:T(1,128)}), f32[32,1,512]{2,1,0:T(1,128)S(1)}, u32[]{:S(2)}, u32[]{:S(2)}) async-start(f32[32,1,512]{2,1,0:T(1,128)} %reshape.190), calls=%async_computation.1 | async-start | bytes 131072 | tf_op jit(solution)/shard_map/all_to_all | solution.py:68
  51.3 4.6 %copy-start.3 = (f32[16,512]{1,0:T(8,128)S(1)}, f32[16,512]{1,0:T(8,128)}, u32[]{:S(2)}) copy-start(f32[16,512]{1,0:T(8,128)} %param.5) | copy-start | bytes 98308
  60.5 4.7 %copy-start = (bf16[1,2,512,512]{3,2,0,1:T(8,128)(2,1)S(1)}, bf16[1,2,512,512]{3,2,0,1:T(8,128)(2,1)}, u32[]{:S(2)}) copy-start(bf16[1,2,512,512]{3,2,0,1:T(8,128)(2,1)} %get-tuple-element.9) | copy-start | bytes 3145732
where the time goes:
time: 81.6 us; the launch traced here: 81.3 us
  matrix products  29.1 us (36%)
  starting transfers between devices  13.3 us (16%)
  other arithmetic  12.1 us (15%)
  local copies, waits for them, and re-layouts  9.94 us (12%)
  blocking collectives  9.93 us (12%)
  waiting for transfers between devices  6.08 us (7%)
  between operations  0.9 us (1%)
    dot_general x6, matrix products, exact_dot(): jnp.dot(left, right, precision=lax.Precision.HIGHEST, preferred_element_t...  28.1 us
    all_to_all x1, blocking collectives, local(): lax.all_to_all(outgoing, 'freq', split_axis=1, concat_axis=0, tiled=True)  9.93 us
    another operation x4, other arithmetic  8.44 us
    all_to_all x1, starting transfers between devices, local(): lax.all_to_all(strain, 'freq', split_axis=1, concat_axis=0, tiled=True)  7.3 us
    all_to_all x1, waiting for transfers between devices, local(): lax.all_to_all(turned, 'freq', split_axis=0, concat_axis=2, tiled=True)  6.07 us
    all_to_all x1, starting transfers between devices, local(): lax.all_to_all(turned, 'freq', split_axis=0, concat_axis=2, tiled=True)  6.01 us
    unnamed x13, local copies, waits for them, and re-layouts  3.71 us
  transfers between devices with their start and end apart: 2, of which 1 were waited for; matrix products, arithmetic and copies ran while one was open for 12% of the time, Pallas kernels for 0%

commit v1 on v0

v1 whole, which is shorter than its diff:
```python
import functools

import jax
import jax.numpy as jnp
import ml_dtypes
import numpy as np
from jax import lax
from jax.experimental import pallas as pl
from jax.experimental.pallas import tpu as pltpu
from jax.sharding import PartitionSpec as P

BAND = 256


def angles(left, right, modulus):
    return 2.0 * np.pi / modulus * (left[:, None] * right[None, :] % modulus)


def split(table):
    high = table.astype(ml_dtypes.bfloat16)
    low = (table - high.astype(np.float64)).astype(ml_dtypes.bfloat16)
    return high, low


def forward_table(side, rows):
    count = side // rows
    positions = np.arange(side)
    angle = angles(positions, positions, side)
    core = positions // rows % 2
    result = []
    for device in range(count):
        order = np.concatenate([positions[core == device % 2], positions[core != device % 2]])
        part = angle[device * rows : (device + 1) * rows][:, order]
        high, low = split(np.concatenate([np.cos(part), -np.sin(part)]))
        result.append(np.concatenate([high, low]))
    return np.stack(result)


def dot(left, right):
    return jnp.dot(left, right, preferred_element_type=jnp.float32)


def spread(slots, rows):
    count = len(slots)
    lane = lax.broadcasted_iota(jnp.int32, slots[0].shape, 1)
    lanes = slots[0].shape[1]
    bit = 1
    while bit < count:
        step = rows * bit
        keep = (lane // step) % 2 == 0
        after = list(slots)
        for low in range(count):
            if low & bit:
                continue
            high = low | bit
            after[low] = jnp.where(keep, slots[low], pltpu.roll(slots[high], step, 1))
            after[high] = jnp.where(keep, pltpu.roll(slots[low], lanes - step, 1), slots[high])
        slots = after
        bit *= 2
    return slots


def middle_kernel(own, other, forward, twist, column_high, column_low, inv_asd, spectra, cutoff, section_table, out):
    rows, side = twist.shape[1:]
    templ_count = spectra.shape[0]
    half = side // 2
    first = dot(forward[0, :, :half], own[...]) + dot(forward[0, :, half:], other[...])
    first = first[: 2 * rows] + first[2 * rows :]
    first_real, first_imag = first[:rows], first[rows:]
    twist_cos, twist_sin = twist[0], twist[1]
    turned = jnp.concatenate(
        [first_real * twist_cos + first_imag * twist_sin, first_imag * twist_cos - first_real * twist_sin], 0
    )
    high = turned.astype(jnp.bfloat16)
    low = (turned - high.astype(jnp.float32)).astype(jnp.bfloat16)
    both = dot(jnp.concatenate([high, low], 0), column_high[...])
    second = both[: 2 * rows] + both[2 * rows :] + dot(high, column_low[...])
    asd = inv_asd[:, :BAND]
    white_real = (second[:rows, :BAND] + second[rows:, BAND:]) * asd
    white_imag = (second[rows:, :BAND] - second[:rows, BAND:]) * asd
    band = lax.broadcasted_iota(jnp.int32, (rows, BAND), 1)
    product = []
    for part in range(2):
        for templ in range(templ_count):
            spec_real = spectra[templ, 0, :, :BAND].astype(jnp.float32)
            spec_imag = spectra[templ, 1, :, :BAND].astype(jnp.float32)
            if part == 0:
                value = white_real * spec_real + white_imag * spec_imag
            else:
                value = white_imag * spec_real - white_real * spec_imag
            product.append(jnp.where(band < cutoff[templ], value, 0.0).astype(jnp.bfloat16))
    turned = dot(jnp.concatenate(product, 0), section_table[...])
    group = templ_count * rows
    real_part = turned[:group, :side] - turned[group:, side:]
    imag_part = turned[:group, side:] + turned[group:, :side]
    slots = []
    for templ in range(templ_count):
        here = slice(templ * rows, (templ + 1) * rows)
        slots.append(real_part[here] * twist_cos - imag_part[here] * twist_sin)
    for templ in range(templ_count):
        here = slice(templ * rows, (templ + 1) * rows)
        slots.append(real_part[here] * twist_sin + imag_part[here] * twist_cos)
    for start in range(0, side, 128):
        pieces = spread([slot[:, start : start + 128] for slot in slots], rows)
        for place, piece in enumerate(pieces):
            out[start // rows + place] = piece.astype(jnp.bfloat16)


def last_kernel(received, table, series, peak):
    templ_count, _, rows, side = series.shape
    scale = 1.0 / (side * side)
    turned = lax.dot_general(
        received[...], table[...], (((0,), (0,)), ((), ())), preferred_element_type=jnp.float32
    )
    group = templ_count * rows
    real_part = (turned[:group, :side] - turned[group:, side:]) * scale
    imag_part = (turned[:group, side:] + turned[group:, :side]) * scale
    power = real_part * real_part + imag_part * imag_part
    best = power[:rows]
    for templ in range(templ_count):
        here = slice(templ * rows, (templ + 1) * rows)
        series[templ, 0] = real_part[here]
        series[templ, 1] = imag_part[here]
        best = jnp.maximum(best, power[here])
    peak[...] = best


def middle_plain(own, other, forward, twist, column_high, column_low, inv_asd, spectra, cutoff, section_table):
    rows, side = twist.shape[1:]
    templ_count = spectra.shape[0]
    first = dot(forward[0], jnp.concatenate([own, other], 0))
    first = first[: 2 * rows] + first[2 * rows :]
    first_real, first_imag = first[:rows], first[rows:]
    twist_cos, twist_sin = twist[0], twist[1]
    turned = jnp.concatenate(
        [first_real * twist_cos + first_imag * twist_sin, first_imag * twist_cos - first_real * twist_sin], 0
    )
    high = turned.astype(jnp.bfloat16)
    low = (turned - high.astype(jnp.float32)).astype(jnp.bfloat16)
    second = dot(high, column_high) + dot(low, column_high) + dot(high, column_low)
    asd = inv_asd[:, :BAND]
    white_real = (second[:rows, :BAND] + second[rows:, BAND:]) * asd
    white_imag = (second[rows:, :BAND] - second[:rows, BAND:]) * asd
    keep = jnp.arange(BAND, dtype=jnp.int32)[None, :] < cutoff[:, None]
    spec_real = spectra[:, 0, :, :BAND].astype(jnp.float32)
    spec_imag = spectra[:, 1, :, :BAND].astype(jnp.float32)
    product = jnp.stack([white_real * spec_real + white_imag * spec_imag, white_imag * spec_real - white_real * spec_imag])
    product = jnp.where(keep[None, :, None], product, 0.0).astype(jnp.bfloat16)
    turned = jnp.einsum("ctkj,jn->ctkn", product, section_table, preferred_element_type=jnp.float32)
    real_part = turned[0, ..., :side] - turned[1, ..., side:]
    imag_part = turned[0, ..., side:] + turned[1, ..., :side]
    rotated = jnp.stack(
        [real_part * twist_cos - imag_part * twist_sin, real_part * twist_sin + imag_part * twist_cos]
    ).astype(jnp.bfloat16)
    pieces = rotated.reshape(2, templ_count, rows, side // rows, rows)
    return jnp.transpose(pieces, (3, 2, 0, 1, 4)).reshape(side // rows, rows, -1)


def last_plain(received, table, templ_count, rows):
    side = received.shape[0]
    scale = 1.0 / (side * side)
    turned = lax.dot_general(received, table, (((0,), (0,)), ((), ())), preferred_element_type=jnp.float32)
    turned = turned.reshape(2, templ_count, rows, 2 * side)
    real_part = (turned[0, ..., :side] - turned[1, ..., side:]) * scale
    imag_part = (turned[0, ..., side:] + turned[1, ..., :side]) * scale
    series = jnp.stack([real_part, imag_part], 1)
    return series, jnp.max(real_part * real_part + imag_part * imag_part, axis=0)


def local(device_count, strain, inv_asd, spectra, cutoff):
    rows, side = strain.shape
    templ_count = spectra.shape[1]
    positions = np.arange(side)
    device = lax.axis_index("freq")
    angle = angles(positions, positions, side)
    cosines, sines = np.cos(angle), np.sin(angle)
    column_high, column_low = split(np.concatenate([cosines[:, :BAND], sines[:, :BAND]], 1))
    full_table = np.concatenate([cosines, sines], 1).astype(ml_dtypes.bfloat16)
    section_table, last_table = full_table[:BAND], full_table
    twist_angle = angles(positions, positions, side * side)
    twist_all = np.stack([np.cos(twist_angle), np.sin(twist_angle)]).astype(np.float32)
    forward = lax.dynamic_slice_in_dim(jnp.asarray(forward_table(side, rows)), device, 1, 0)
    twist = lax.dynamic_slice_in_dim(jnp.asarray(twist_all), device * rows, rows, 1)
    chips = device_count // 2
    groups = [[2 * chip + core for chip in range(chips)] for core in range(2)]
    copies = jnp.broadcast_to(strain.astype(jnp.bfloat16)[None], (chips, rows, side))
    own = lax.all_to_all(copies, "freq", 0, 0, tiled=True, axis_index_groups=groups).reshape(-1, side)
    other = lax.ppermute(own, "freq", [(i, i ^ 1) for i in range(device_count)])
    by_templ = jnp.transpose(spectra, (1, 2, 0, 3))
    args = (
        own,
        other,
        forward,
        twist,
        jnp.asarray(column_high),
        jnp.asarray(column_low),
        inv_asd,
        by_templ,
        cutoff,
        jnp.asarray(section_table),
    )
    tiles_fit = rows % 16 == 0 and 2 * templ_count * rows == 128 and side % 128 == 0
    if tiles_fit:
        vmem = pl.BlockSpec(memory_space=pltpu.VMEM)
        smem = pl.BlockSpec(memory_space=pltpu.SMEM)
        outgoing = pl.pallas_call(
            middle_kernel,
            out_shape=jax.ShapeDtypeStruct((device_count, rows, 128), jnp.bfloat16),
            in_specs=[vmem] * 8 + [smem, vmem],
            out_specs=vmem,
        )(*args)
    else:
        outgoing = middle_plain(*args)
    received = lax.all_to_all(outgoing, "freq", 0, 0, tiled=True).reshape(side, -1)
    if tiles_fit:
        series, peak = pl.pallas_call(
            last_kernel,
            out_shape=(
                jax.ShapeDtypeStruct((templ_count, 2, rows, side), jnp.float32),
                jax.ShapeDtypeStruct((rows, side), jnp.float32),
            ),
            in_specs=[vmem] * 2,
            out_specs=(vmem, vmem),
        )(received, jnp.asarray(last_table))
    else:
        series, peak = last_plain(received, jnp.asarray(last_table), templ_count, rows)
    return series, lax.pmax(peak, "tmpl")


def solution(mesh):
    in_specs = (P("freq", None), P("freq", None), P("freq", "tmpl", None, None), P("tmpl"))
    out_specs = (P("tmpl", None, "freq", None), P("freq", None))
    return jax.shard_map(
        functools.partial(local, mesh.shape["freq"]),
        mesh=mesh,
        in_specs=in_specs,
        out_specs=out_specs,
        check_vma=False,
    )
```

time: 81.6 us -> 42.4 us (0.52)
  matrix products: 29.1 us -> 0 us
  blocking collectives: 9.93 us -> 29.5 us
  starting transfers between devices: 13.3 us -> 0.01 us
  other arithmetic: 12.1 us -> 0.76 us
  waiting for transfers between devices: 6.08 us -> 0.01 us
  Pallas kernels: 0 us -> 5.76 us
  local copies, waits for them, and re-layouts: 9.94 us -> 5.33 us
    dot_general x8 -> x0, matrix products: 29.1 us -> none  [the longest x6 28.1 us: exact_dot(): jnp.dot(left, right, precision=lax.Precision.HIGHEST, preferred_element_t...]
    all_to_all x1 -> x2, blocking collectives: 9.93 us -> 29.5 us  [the longest x1 18 us: local(): lax.all_to_all(copies, 'freq', 0, 0, tiled=True, axis_index_groups=groups)]
    all_to_all x2 -> x0, starting transfers between devices: 13.3 us -> none  [the longest x1 7.3 us: local(): lax.all_to_all(strain, 'freq', split_axis=1, concat_axis=0, tiled=True)]
    another operation x7 -> x0, other arithmetic: 9.61 us -> none
    all_to_all x2 -> x0, waiting for transfers between devices: 6.08 us -> none  [the longest x1 6.07 us: local(): lax.all_to_all(turned, 'freq', split_axis=0, concat_axis=2, tiled=True)]
    pallas_call x0 -> x2, Pallas kernels: none -> 5.76 us  [the longest x1 3.41 us: local(): pl.pallas_call(middle_kernel, out_shape=jax.ShapeDtypeStruct((device_coun...]
    all_to_all x6 -> x0, local copies, waits for them, and re-layouts: 3.56 us -> none  [the longest x3 1.55 us: local(): lax.all_to_all(strain, 'freq', split_axis=1, concat_axis=0, tiled=True)]
    dynamic_slice x0 -> x2, local copies, waits for them, and re-layouts: none -> 2.94 us  [the longest x1 1.47 us: local(): lax.dynamic_slice_in_dim(jnp.asarray(twist_all), device * rows, rows, 1)]
  transfers between devices with their start and end apart: 2 -> 1, of which waited for: 1 -> 0; matrix products, arithmetic and copies ran while one was open for 12% -> 11% of each run, Pallas kernels for 0% -> 0%
where the time goes in v1:
time: 42.4 us; the launch traced here: 42 us
  blocking collectives  29.5 us (70%)
  Pallas kernels  5.76 us (14%)
  local copies, waits for them, and re-layouts  5.33 us (13%)
  other arithmetic  0.76 us (2%)
  between operations  0.65 us (2%)
    all_to_all x1, blocking collectives, local(): lax.all_to_all(copies, 'freq', 0, 0, tiled=True, axis_index_groups=groups)  18 us
    all_to_all x1, blocking collectives, local(): lax.all_to_all(outgoing, 'freq', 0, 0, tiled=True).reshape(side, -1)  11.5 us
    pallas_call x1, Pallas kernels, local(): pl.pallas_call(middle_kernel, out_shape=jax.ShapeDtypeStruct((device_coun...  3.41 us
    unnamed x5, local copies, waits for them, and re-layouts  2.38 us
    pallas_call x1, Pallas kernels, local(): pl.pallas_call(last_kernel, out_shape=(jax.ShapeDtypeStruct((templ_count,...  2.35 us
    dynamic_slice x1, local copies, waits for them, and re-layouts, local(): lax.dynamic_slice_in_dim(jnp.asarray(twist_all), device * rows, rows, 1)  1.47 us
    dynamic_slice x1, local copies, waits for them, and re-layouts, local(): lax.dynamic_slice_in_dim(jnp.asarray(forward_table(side, rows)), device,...  1.47 us
  transfers between devices with their start and end apart: 1, of which 0 were waited for; matrix products, arithmetic and copies ran while one was open for 11% of the time, Pallas kernels for 0%

profile of v1, /device:TPU:0, one launch (start us, length us, event | category | flops | bytes accessed | tf_op | source)
XLA Modules:
  0.0 42.0 jit_solution(14464917408725583353)
XLA Ops:
  0.6 0.8 %convert_element_type.3 = bf16[16,512]{1,0:T(8,128)(2,1)S(1)} convert(f32[16,512]{1,0:T(8,128)} %param.10) | non-fusion elementwise | flops 8192 | bytes 49152 | tf_op jit(solution)/shard_map/convert_element_type | solution.py:186
  1.4 18.0 %all_to_all.10 = bf16[16,16,512]{2,1,0:T(8,128)(2,1)S(1)} all-to-all(bf16[16,16,512]{2,1,0:T(8,128)(2,1)S(1)} %broadcast_in_dim.2), channel_id=1, replica_groups={{0,2,4,6,8,10,12,14,16,18,20,22,24,26,28,30},{1,3,5,7,9,11,13,15,17,19,..., dimensions={0} | all-to-all | bytes 524288 | tf_op jit(solution)/shard_map/all_to_all | solution.py:187
  19.4 0.0 copy-start
  19.4 0.0 collective-permute-start
  19.4 1.7 %copy.14 = bf16[16,4,2,512]{3,0,2,1:T(8,128)(2,1)} copy(bf16[16,4,2,512]{3,2,1,0:T(2,128)(2,1)} %param.12) | data formatting | bytes 262144 | tf_op args[2]
  21.1 1.5 %constant_dynamic-slice_fusion.1.forward = bf16[1,64,512]{2,1,0:T(8,128)(2,1)} fusion(bf16[32,64,512]{2,1,0:T(8,128)(2,1)} %constant.24.clone, s32[]{:T(128)S(6)} %select_n.6), kind=kLoop, calls=%fused_computation.2 | loop fusion | bytes 131076 | tf_op jit(solution)/shard_map/dynamic_slice | solution.py:182
  22.6 1.5 %constant_dynamic-slice_fusion.twist = f32[2,16,512]{2,1,0:T(8,128)} fusion(f32[2,512,512]{2,1,0:T(8,128)} %constant.25.clone, s32[]{:T(128)S(6)} %select_n.7), kind=kLoop, calls=%fused_computation.1 | loop fusion | bytes 131076 | tf_op jit(solution)/shard_map/dynamic_slice | solution.py:183
  24.0 0.0 collective-permute-done.other
  24.0 0.0 copy-start.1
  24.0 0.0 copy-done
  24.0 0.7 %copy-done.1 = bf16[256,512]{1,0:T(8,128)(2,1)} copy-done((bf16[256,512]{1,0:T(8,128)(2,1)}, bf16[256,512]{1,0:T(8,128)(2,1)S(1)}, u32[]{:S(2)}) %copy-start.1) | copy-done | bytes 262168
  24.7 3.4 %shard_map.113 = bf16[32,16,128]{2,1,0:T(8,128)(2,1)} custom-call(bf16[256,512]{1,0:T(8,128)(2,1)} %bitcast.6, bf16[256,512]{1,0:T(8,128)(2,1)} %copy-done.1, bf16[1,64,512]{2,1,0:T(8,128)(2,1)} %constant_dynamic-slice_fusion.1.forward, f32[2,16,512]{2,1,0:T(8,128)} %constant_dynamic-slice_fusion.twist, bf16[512,512]{1,0:T(8,128)(2,1)} %constant.26.clone.column_high, ...), custom_call_target="tpu_custom_call" | custom-call | tf_op jit(solution)/shard_map/pallas_call | solution.py:206
  28.1 11.5 %all_to_all.11 = bf16[32,16,128]{2,1,0:T(8,128)(2,1)} all-to-all(bf16[32,16,128]{2,1,0:T(8,128)(2,1)} %shard_map.113), channel_id=1, replica_groups=mesh['tmpl'=1,'freq'=32] {'freq'}, dimensions={0} | all-to-all | bytes 262144 | tf_op jit(solution)/shard_map/all_to_all | solution.py:214
  39.6 2.3 %shard_map.114 = (f32[4,2,16,512]{3,2,1,0:T(8,128)}, f32[16,512]{1,0:T(8,128)}) custom-call(bf16[512,128]{1,0:T(8,128)(2,1)} %bitcast.8, bf16[512,1024]{1,0:T(8,128)(2,1)} %constant.29.clone.table), custom_call_target="tpu_custom_call" | custom-call | tf_op jit(solution)/shard_map/pallas_call | solution.py:216
  (1 shorter events, 0.0 us)
Async XLA Ops:
  19.4 4.6 %copy-start = (bf16[16,16,512]{2,1,0:T(8,128)(2,1)}, bf16[16,16,512]{2,1,0:T(8,128)(2,1)S(1)}, u32[]{:S(2)}) copy-start(bf16[16,16,512]{2,1,0:T(8,128)(2,1)S(1)} %all_to_all.10) | copy-start | bytes 786436
  19.4 4.6 %collective-permute-start = (bf16[256,512]{1,0:T(8,128)(2,1)S(1)}, bf16[256,512]{1,0:T(8,128)(2,1)S(1)}, u32[]{:S(2)}, u32[]{:S(2)}) collective-permute-start(bf16[256,512]{1,0:T(8,128)(2,1)S(1)} %bitcast.5), channel_id=1, source_target_pairs={{0,1},{1,0},{2,3},{3,2},{4,5},{5,4},{6,7},{7,6},{8,9},{9,8},{10,11... | collective-permute-start | bytes 786440 | tf_op jit(solution)/shard_map/ppermute | solution.py:188
  24.0 0.7 %copy-start.1 = (bf16[256,512]{1,0:T(8,128)(2,1)}, bf16[256,512]{1,0:T(8,128)(2,1)S(1)}, u32[]{:S(2)}) copy-start(bf16[256,512]{1,0:T(8,128)(2,1)S(1)} %collective-permute-done.other) | copy-start | bytes 786436

commit v2 on v1

v2 whole, which is shorter than its diff:
```python
import functools

import jax
import jax.numpy as jnp
import ml_dtypes
import numpy as np
from jax import lax
from jax.experimental import pallas as pl
from jax.experimental.pallas import tpu as pltpu
from jax.sharding import PartitionSpec as P

BAND = 256
VMEM_LIMIT = 16 << 20


def angles(left, right, modulus):
    return 2.0 * np.pi / modulus * (left[:, None] * right[None, :] % modulus)


def split(table):
    high = table.astype(ml_dtypes.bfloat16)
    low = (table - high.astype(np.float64)).astype(ml_dtypes.bfloat16)
    return high, low


def device_tables(side, rows):
    count = side // rows
    positions = np.arange(side)
    core = positions // rows % 2
    orders = [np.concatenate([positions[core == own], positions[core != own]]) for own in range(2)]
    devices = np.arange(count)
    twist = angles(devices * rows, positions, side * side)
    forward = angles(devices * rows, positions, side)
    forward = np.stack([forward[device, orders[device % 2]] for device in range(count)])
    result = [np.cos(twist), np.sin(twist), np.cos(forward), np.sin(forward)]
    for own in range(2):
        twist = angles(np.arange(rows), positions, side * side)
        forward = angles(np.arange(rows), positions, side)[:, orders[own]]
        result += [np.cos(twist), np.sin(twist), np.cos(forward), np.sin(forward)]
    return np.concatenate(result).astype(np.float32)


def transform_table(side):
    angle = angles(np.arange(side), np.arange(side), side)
    cos_high, cos_low = split(np.cos(angle))
    sin_high, sin_low = split(np.sin(angle))
    return np.concatenate([cos_high, sin_high, cos_low[:, :BAND], sin_low[:, :BAND]], 1)


def device_rows(take, count, rows):
    device = lax.axis_index("freq")

    def turn(which):
        base = 4 * count + (device % 2 * 4 + which) * rows
        row_cos, row_sin = take(which * count + device, 1), take((which + 1) * count + device, 1)
        part_cos, part_sin = take(base, rows), take(base + rows, rows)
        return row_cos * part_cos - row_sin * part_sin, row_cos * part_sin + row_sin * part_cos

    twist_cos, twist_sin = turn(0)
    forward_cos, forward_sin = turn(2)
    exact = jnp.concatenate([forward_cos, -forward_sin], 0)
    high = exact.astype(jnp.bfloat16)
    low = (exact - high.astype(jnp.float32)).astype(jnp.bfloat16)
    return twist_cos, twist_sin, jnp.concatenate([high, low], 0)


def dot(left, right):
    return jnp.dot(left, right, preferred_element_type=jnp.float32)


def spread(slots, rows):
    count = len(slots)
    lane = lax.broadcasted_iota(jnp.int32, slots[0].shape, 1)
    lanes = slots[0].shape[1]
    bit = 1
    while bit < count:
        step = rows * bit
        keep = (lane // step) % 2 == 0
        after = list(slots)
        for low in range(count):
            if low & bit:
                continue
            high = low | bit
            after[low] = jnp.where(keep, slots[low], pltpu.roll(slots[high], step, 1))
            after[high] = jnp.where(keep, pltpu.roll(slots[low], lanes - step, 1), slots[high])
        slots = after
        bit *= 2
    return slots


def prepare_kernel(turns, table, twist, forward, table_out, copied):
    copy = pltpu.make_async_copy(table, table_out, copied)
    copy.start()
    _, rows, side = twist.shape
    twist[0], twist[1], forward[...] = device_rows(lambda start, size: turns[pl.ds(start, size), :], side // rows, rows)
    copy.wait()


def middle_kernel(own, other, twist, forward, table, inv_asd, spectra, out):
    templ_count, _, rows, _ = spectra.shape
    side = own.shape[1]
    half = side // 2
    twist_cos, twist_sin = twist[0], twist[1]
    first = dot(forward[:, :half], own[...]) + dot(forward[:, half:], other[...])
    first = first[: 2 * rows] + first[2 * rows :]
    first_real, first_imag = first[:rows], first[rows:]
    turned = jnp.concatenate(
        [first_real * twist_cos + first_imag * twist_sin, first_imag * twist_cos - first_real * twist_sin], 0
    )
    high = turned.astype(jnp.bfloat16)
    low = (turned - high.astype(jnp.float32)).astype(jnp.bfloat16)
    both = jnp.concatenate([high, low], 0)
    both = [dot(both, table[:, start : start + BAND]) for start in (0, side)]
    rest = [dot(high, table[:, 2 * side + start : 2 * side + start + BAND]) for start in (0, BAND)]
    by_cos, by_sin = [x[: 2 * rows] + x[2 * rows :] + y for x, y in zip(both, rest)]
    asd = inv_asd[...]
    white_real = (by_cos[:rows] + by_sin[rows:]) * asd
    white_imag = (by_cos[rows:] - by_sin[:rows]) * asd
    product = []
    for part in range(2):
        for templ in range(templ_count):
            spec_real = spectra[templ, 0].astype(jnp.float32)
            spec_imag = spectra[templ, 1].astype(jnp.float32)
            if part == 0:
                value = white_real * spec_real + white_imag * spec_imag
            else:
                value = white_imag * spec_real - white_real * spec_imag
            product.append(value.astype(jnp.bfloat16))
    turned = dot(jnp.concatenate(product, 0), table[:BAND, : 2 * side])
    group = templ_count * rows
    real_part = turned[:group, :side] - turned[group:, side:]
    imag_part = turned[:group, side:] + turned[group:, :side]
    slots = []
    for templ in range(templ_count):
        here = slice(templ * rows, (templ + 1) * rows)
        slots.append(real_part[here] * twist_cos - imag_part[here] * twist_sin)
    for templ in range(templ_count):
        here = slice(templ * rows, (templ + 1) * rows)
        slots.append(real_part[here] * twist_sin + imag_part[here] * twist_cos)
    for start in range(0, side, 128):
        pieces = spread([slot[:, start : start + 128] for slot in slots], rows)
        for place, piece in enumerate(pieces):
            out[start // rows + place] = piece.astype(jnp.bfloat16)


def last_kernel(received, table, series, peak):
    templ_count, _, rows, side = series.shape
    scale = 1.0 / (side * side)
    turned = lax.dot_general(
        received[...], table[:, : 2 * side], (((0,), (0,)), ((), ())), preferred_element_type=jnp.float32
    )
    group = templ_count * rows
    real_part = (turned[:group, :side] - turned[group:, side:]) * scale
    imag_part = (turned[:group, side:] + turned[group:, :side]) * scale
    power = real_part * real_part + imag_part * imag_part
    best = power[:rows]
    for templ in range(templ_count):
        here = slice(templ * rows, (templ + 1) * rows)
        series[templ, 0] = real_part[here]
        series[templ, 1] = imag_part[here]
        best = jnp.maximum(best, power[here])
    peak[...] = best


def prepare_plain(turns, table, rows):
    twist_cos, twist_sin, forward = device_rows(
        lambda start, size: lax.dynamic_slice_in_dim(turns, start, size, 0), table.shape[0] // rows, rows
    )
    return jnp.stack([twist_cos, twist_sin]), forward, table


def middle_plain(own, other, twist, forward, table, inv_asd, spectra):
    templ_count, _, rows, _ = spectra.shape
    side = own.shape[1]
    twist_cos, twist_sin = twist[0], twist[1]
    first = dot(forward, jnp.concatenate([own, other], 0))
    first = first[: 2 * rows] + first[2 * rows :]
    first_real, first_imag = first[:rows], first[rows:]
    turned = jnp.concatenate(
        [first_real * twist_cos + first_imag * twist_sin, first_imag * twist_cos - first_real * twist_sin], 0
    )
    high = turned.astype(jnp.bfloat16)
    low = (turned - high.astype(jnp.float32)).astype(jnp.bfloat16)
    column_high = jnp.concatenate([table[:, :BAND], table[:, side : side + BAND]], 1)
    second = dot(high, column_high) + dot(low, column_high) + dot(high, table[:, 2 * side :])
    asd = inv_asd[...]
    white_real = (second[:rows, :BAND] + second[rows:, BAND:]) * asd
    white_imag = (second[rows:, :BAND] - second[:rows, BAND:]) * asd
    spec_real = spectra[:, 0].astype(jnp.float32)
    spec_imag = spectra[:, 1].astype(jnp.float32)
    product = jnp.stack([white_real * spec_real + white_imag * spec_imag, white_imag * spec_real - white_real * spec_imag])
    product = product.astype(jnp.bfloat16)
    turned = jnp.einsum("ctkj,jn->ctkn", product, table[:BAND, : 2 * side], preferred_element_type=jnp.float32)
    real_part = turned[0, ..., :side] - turned[1, ..., side:]
    imag_part = turned[0, ..., side:] + turned[1, ..., :side]
    rotated = jnp.stack(
        [real_part * twist_cos - imag_part * twist_sin, real_part * twist_sin + imag_part * twist_cos]
    ).astype(jnp.bfloat16)
    pieces = rotated.reshape(2, templ_count, rows, side // rows, rows)
    return jnp.transpose(pieces, (3, 2, 0, 1, 4)).reshape(side // rows, rows, -1)


def last_plain(received, table, templ_count, rows):
    side = received.shape[0]
    scale = 1.0 / (side * side)
    turned = lax.dot_general(received, table, (((0,), (0,)), ((), ())), preferred_element_type=jnp.float32)
    turned = turned[:, : 2 * side].reshape(2, templ_count, rows, 2 * side)
    real_part = (turned[0, ..., :side] - turned[1, ..., side:]) * scale
    imag_part = (turned[0, ..., side:] + turned[1, ..., :side]) * scale
    series = jnp.stack([real_part, imag_part], 1)
    return series, jnp.max(real_part * real_part + imag_part * imag_part, axis=0)


def local(device_count, strain, inv_asd, spectra, cutoff):
    rows, side = strain.shape
    templ_count = spectra.shape[1]
    tiles_fit = rows % 16 == 0 and 2 * templ_count * rows == 128 and side % 128 == 0
    vmem = pl.BlockSpec(memory_space=pltpu.VMEM)
    chips = device_count // 2
    groups = [[2 * chip + core for chip in range(chips)] for core in range(2)]
    copies = jnp.broadcast_to(strain.astype(jnp.bfloat16)[None], (chips, rows, side))
    own = lax.all_to_all(copies, "freq", 0, 0, tiled=True, axis_index_groups=groups).reshape(-1, side)
    turns, table = jnp.asarray(device_tables(side, rows)), jnp.asarray(transform_table(side))
    if tiles_fit:
        twist, forward, table = pl.pallas_call(
            prepare_kernel,
            out_shape=(
                jax.ShapeDtypeStruct((2, rows, side), jnp.float32),
                jax.ShapeDtypeStruct((4 * rows, side), jnp.bfloat16),
                jax.ShapeDtypeStruct(table.shape, jnp.bfloat16),
            ),
            in_specs=[vmem, pl.BlockSpec(memory_space=pl.ANY)],
            out_specs=(vmem, vmem, vmem),
            scratch_shapes=[pltpu.SemaphoreType.DMA(())],
            compiler_params=pltpu.CompilerParams(vmem_limit_bytes=VMEM_LIMIT),
            cost_estimate=pl.CostEstimate(flops=0, bytes_accessed=16 * table.size, transcendentals=0),
        )(turns, table)
    else:
        twist, forward, table = prepare_plain(turns, table, rows)
    keep = jnp.arange(BAND, dtype=jnp.int32)[None, :] < cutoff[:, None]
    kept = jnp.where(keep[:, None, None], jnp.transpose(spectra[..., :BAND], (1, 2, 0, 3)), 0)
    ready = (twist, forward, table, inv_asd[:, :BAND], kept)
    own, ready = lax.optimization_barrier((own, ready))
    table = ready[2]
    other = lax.ppermute(own, "freq", [(i, i ^ 1) for i in range(device_count)])
    args = (own, other) + ready
    if tiles_fit:
        outgoing = pl.pallas_call(
            middle_kernel,
            out_shape=jax.ShapeDtypeStruct((device_count, rows, 128), jnp.bfloat16),
            in_specs=[vmem] * len(args),
            out_specs=vmem,
            compiler_params=pltpu.CompilerParams(vmem_limit_bytes=VMEM_LIMIT),
        )(*args)
    else:
        outgoing = middle_plain(*args)
    received = lax.all_to_all(outgoing, "freq", 0, 0, tiled=True).reshape(side, -1)
    if tiles_fit:
        series, peak = pl.pallas_call(
            last_kernel,
            out_shape=(
                jax.ShapeDtypeStruct((templ_count, 2, rows, side), jnp.float32),
                jax.ShapeDtypeStruct((rows, side), jnp.float32),
            ),
            in_specs=[vmem] * 2,
            out_specs=(vmem, vmem),
            compiler_params=pltpu.CompilerParams(vmem_limit_bytes=VMEM_LIMIT),
        )(received, table)
    else:
        series, peak = last_plain(received, table, templ_count, rows)
    return series, lax.pmax(peak, "tmpl")


def solution(mesh):
    in_specs = (P("freq", None), P("freq", None), P("freq", "tmpl", None, None), P("tmpl"))
    out_specs = (P("tmpl", None, "freq", None), P("freq", None))
    return jax.shard_map(
        functools.partial(local, mesh.shape["freq"]),
        mesh=mesh,
        in_specs=in_specs,
        out_specs=out_specs,
        check_vma=False,
    )
```

time: 42.4 us -> 35 us (0.83)
  blocking collectives: 29.5 us -> 10.6 us
  starting transfers between devices: 0.01 us -> 8.32 us
  waiting for transfers between devices: 0.01 us -> 7.96 us
  Pallas kernels: 5.76 us -> 2.28 us
  local copies, waits for them, and re-layouts: 5.33 us -> 3.91 us
    all_to_all x1 -> x0, blocking collectives: 18 us -> none  [local(): lax.all_to_all(copies, 'freq', 0, 0, tiled=True, axis_index_groups=groups)]
    all_to_all x0 -> x1, starting transfers between devices: none -> 8.31 us  [local(): lax.all_to_all(copies, 'freq', 0, 0, tiled=True, axis_index_groups=groups)]
    all_to_all x0 -> x1, waiting for transfers between devices: none -> 6.43 us  [local(): lax.all_to_all(copies, 'freq', 0, 0, tiled=True, axis_index_groups=groups)]
    dynamic_slice x2 -> x0, local copies, waits for them, and re-layouts: 2.94 us -> none  [the longest x1 1.47 us: local(): lax.dynamic_slice_in_dim(jnp.asarray(twist_all), device * rows, rows, 1)]
    pallas_call x1, Pallas kernels: 3.41 us -> 1.09 us  [local(): pl.pallas_call(middle_kernel, out_shape=jax.ShapeDtypeStruct((device_coun...]
    ppermute x1, waiting for transfers between devices: 0.01 us -> 1.53 us  [local(): other = lax.ppermute(own, 'freq', [(i, i ^ 1) for i in range(device_count)])]
    pallas_call x1, Pallas kernels: 2.35 us -> 1.04 us  [local(): pl.pallas_call(last_kernel, out_shape=(jax.ShapeDtypeStruct((templ_count,...]
    all_to_all x1, blocking collectives: 11.5 us -> 10.6 us  [local(): lax.all_to_all(outgoing, 'freq', 0, 0, tiled=True).reshape(side, -1)]
  transfers between devices with their start and end apart: 1 -> 2, of which waited for: 0 -> 2; matrix products, arithmetic and copies ran while one was open for 11% -> 2% of each run, Pallas kernels for 0% -> 0%
where the time goes in v2:
time: 35 us; the launch traced here: 34.6 us
  blocking collectives  10.6 us (30%)
  starting transfers between devices  8.32 us (24%)
  waiting for transfers between devices  7.96 us (23%)
  local copies, waits for them, and re-layouts  3.91 us (11%)
  Pallas kernels  2.28 us (7%)
  other arithmetic  0.89 us (3%)
  between operations  0.69 us (2%)
    all_to_all x1, blocking collectives, local(): lax.all_to_all(outgoing, 'freq', 0, 0, tiled=True).reshape(side, -1)  10.6 us
    all_to_all x1, starting transfers between devices, local(): lax.all_to_all(copies, 'freq', 0, 0, tiled=True, axis_index_groups=groups)  8.31 us
    all_to_all x1, waiting for transfers between devices, local(): lax.all_to_all(copies, 'freq', 0, 0, tiled=True, axis_index_groups=groups)  6.43 us
    unnamed x6, local copies, waits for them, and re-layouts  2.45 us
    ppermute x1, waiting for transfers between devices, local(): other = lax.ppermute(own, 'freq', [(i, i ^ 1) for i in range(device_count)])  1.53 us
    pallas_call x1, Pallas kernels, local(): pl.pallas_call(middle_kernel, out_shape=jax.ShapeDtypeStruct((device_coun...  1.09 us
    pallas_call x1, Pallas kernels, local(): pl.pallas_call(last_kernel, out_shape=(jax.ShapeDtypeStruct((templ_count,...  1.04 us
    convert_element_type x1, other arithmetic, local(): strain.astype(jnp.bfloat16)[None]  0.8 us
  transfers between devices with their start and end apart: 2, of which 2 were waited for; matrix products, arithmetic and copies ran while one was open for 2% of the time, Pallas kernels for 0%

profile of v2, /device:TPU:0, one launch (start us, length us, event | category | flops | bytes accessed | tf_op | source)
XLA Modules:
  0.0 34.6 jit_solution(1159841226304946425)
XLA Ops:
  0.6 0.0 slice-start
  0.6 0.0 copy-start.2
  0.7 0.8 %convert_element_type.5 = bf16[16,512]{1,0:T(8,128)(2,1)S(1)} convert(f32[16,512]{1,0:T(8,128)} %param.6) | non-fusion elementwise | flops 8192 | bytes 49152 | tf_op jit(solution)/shard_map/convert_element_type | solution.py:221
  1.4 0.7 %broadcast_in_dim.10 = bf16[16,16,512]{2,1,0:T(8,128)(2,1)} broadcast(bf16[16,512]{1,0:T(8,128)(2,1)S(1)} %convert_element_type.5), dimensions={1,2} | broadcast | bytes 278528 | tf_op jit(solution)/shard_map/broadcast_in_dim | solution.py:221
  2.2 8.3 %all-to-all-start = ((bf16[16,16,512]{2,1,0:T(8,128)(2,1)}), bf16[16,16,512]{2,1,0:T(8,128)(2,1)S(1)}, u32[]{:S(2)}, u32[]{:S(2)}) async-start(bf16[16,16,512]{2,1,0:T(8,128)(2,1)} %broadcast_in_dim.10), calls=%async_computation | async-start | bytes 524288 | tf_op jit(solution)/shard_map/all_to_all | solution.py:222
  10.5 0.7 %slice.6.inv_asd = f32[16,256]{1,0:T(8,128)S(1)} slice(f32[16,512]{1,0:T(8,128)} %param.7), slice={[0:16], [0:256]} | slice | bytes 32768 | tf_op jit(solution)/shard_map/slice | solution.py:242
  11.2 0.0 copy-start
  11.2 1.4 %copy-done = bf16[512,1536]{1,0:T(8,128)(2,1)S(1)} copy-done((bf16[512,1536]{1,0:T(8,128)(2,1)S(1)}, bf16[512,1536]{1,0:T(8,128)(2,1)}, u32[]{:S(2)}) %copy-start) | copy-done | bytes 1572888
  12.6 0.0 copy-start.1
  12.6 1.0 %copy-done.1 = f32[256,512]{1,0:T(8,128)S(1)} copy-done((f32[256,512]{1,0:T(8,128)S(1)}, f32[256,512]{1,0:T(8,128)}, u32[]{:S(2)}) %copy-start.1) | copy-done | bytes 524312
  13.7 0.1 shard_map.77
  13.8 0.0 copy-done.2
  13.8 0.1 iota_compare_fusion
  13.9 0.0 slice-done
  13.9 6.4 %all-to-all-done = bf16[16,16,512]{2,1,0:T(8,128)(2,1)S(1)} async-done(((bf16[16,16,512]{2,1,0:T(8,128)(2,1)}), bf16[16,16,512]{2,1,0:T(8,128)(2,1)S(1)}, u32[]{:S(2)}, u32[]{:S(2)}) %all-to-all-start) | async-done | bytes 262176 | tf_op jit(solution)/shard_map/all_to_all | solution.py:222
  20.4 0.0 collective-permute-start
  20.4 1.5 %collective-permute-done.other = bf16[256,512]{1,0:T(8,128)(2,1)S(1)} collective-permute-done((bf16[256,512]{1,0:T(8,128)(2,1)S(1)}, bf16[256,512]{1,0:T(8,128)(2,1)S(1)}, u32[]{:S(2)}, u32[]{:S(2)}) %collective-permute-start) | collective-permute-done | bytes 262176 | tf_op jit(solution)/shard_map/ppermute | solution.py:245
  21.9 1.1 %shard_map.78 = bf16[32,16,128]{2,1,0:T(8,128)(2,1)S(1)} custom-call(bf16[256,512]{1,0:T(8,128)(2,1)S(1)} %bitcast.5, bf16[256,512]{1,0:T(8,128)(2,1)S(1)} %collective-permute-done.other, f32[2,16,512]{2,1,0:T(8,128)S(1)} %get-tuple-element.15.twist, bf16[64,512]{1,0:T(8,128)(2,1)S(1)} %get-tuple-element.16.forward, ...), custom_call_target="tpu_custom_call" | custom-call | tf_op jit(solution)/shard_map/pallas_call | solution.py:248
  23.0 10.6 %all_to_all.10 = bf16[32,16,128]{2,1,0:T(8,128)(2,1)S(1)} all-to-all(bf16[32,16,128]{2,1,0:T(8,128)(2,1)S(1)} %shard_map.78), channel_id=1, replica_groups=mesh['tmpl'=1,'freq'=32] {'freq'}, dimensions={0} | all-to-all | bytes 262144 | tf_op jit(solution)/shard_map/all_to_all | solution.py:257
  33.6 1.0 %shard_map.79 = (f32[4,2,16,512]{3,2,1,0:T(8,128)}, f32[16,512]{1,0:T(8,128)}) custom-call(bf16[512,128]{1,0:T(8,128)(2,1)S(1)} %bitcast.6, bf16[512,1536]{1,0:T(8,128)(2,1)S(1)} %get-tuple-element.17.table), custom_call_target="tpu_custom_call" | custom-call | tf_op jit(solution)/shard_map/pallas_call | solution.py:259
  (1 shorter events, 0.0 us)
Async XLA Ops:
  0.6 13.3 %slice-start = ((bf16[16,4,2,512]{3,2,1,0:T(2,128)(2,1)}), bf16[16,4,2,256]{3,2,1,0:T(2,128)(2,1)S(1)}, s32[]{:S(2)}) async-start(bf16[16,4,2,512]{3,2,1,0:T(2,128)(2,1)} %param.8), calls=%async_computation.2 | async-start | bytes 131072 | tf_op jit(solution)/shard_map/slice | solution.py:241
  0.6 13.2 %copy-start.2 = (s32[4]{0:T(128)S(1)}, s32[4]{0:T(128)}, u32[]{:S(2)}) copy-start(s32[4]{0:T(128)} %param.9) | copy-start | bytes 52
  2.2 18.2 %all-to-all-start = ((bf16[16,16,512]{2,1,0:T(8,128)(2,1)}), bf16[16,16,512]{2,1,0:T(8,128)(2,1)S(1)}, u32[]{:S(2)}, u32[]{:S(2)}) async-start(bf16[16,16,512]{2,1,0:T(8,128)(2,1)} %broadcast_in_dim.10), calls=%async_computation | async-start | bytes 524288 | tf_op jit(solution)/shard_map/all_to_all | solution.py:222
  11.2 1.4 %copy-start = (bf16[512,1536]{1,0:T(8,128)(2,1)S(1)}, bf16[512,1536]{1,0:T(8,128)(2,1)}, u32[]{:S(2)}) copy-start(bf16[512,1536]{1,0:T(8,128)(2,1)} %constant.8.clone.table) | copy-start | bytes 4718596
  12.6 1.0 %copy-start.1 = (f32[256,512]{1,0:T(8,128)S(1)}, f32[256,512]{1,0:T(8,128)}, u32[]{:S(2)}) copy-start(f32[256,512]{1,0:T(8,128)} %constant.7.clone.turns) | copy-start | bytes 1572868
  20.4 1.5 %collective-permute-start = (bf16[256,512]{1,0:T(8,128)(2,1)S(1)}, bf16[256,512]{1,0:T(8,128)(2,1)S(1)}, u32[]{:S(2)}, u32[]{:S(2)}) collective-permute-start(bf16[256,512]{1,0:T(8,128)(2,1)S(1)} %bitcast.4), channel_id=1, source_target_pairs={{0,1},{1,0},{2,3},{3,2},{4,5},{5,4},{6,7},{7,6},{8,9},{9,8},{10,11... | collective-permute-start | bytes 786440 | tf_op jit(solution)/shard_map/ppermute | solution.py:245

commit v3 on v1

v3 whole, which is shorter than its diff:
```python
import functools

import jax
import jax.numpy as jnp
import ml_dtypes
import numpy as np
from jax import lax
from jax.experimental import pallas as pl
from jax.experimental.pallas import tpu as pltpu
from jax.sharding import PartitionSpec as P

BAND = 256
CORES = 2
INNER = 4
VMEM_LIMIT = 16 << 20


def angles(left, right, modulus):
    return 2.0 * np.pi / modulus * (left[:, None] * right[None, :] % modulus)


def split(table):
    high = table.astype(ml_dtypes.bfloat16)
    low = (table - high.astype(np.float64)).astype(ml_dtypes.bfloat16)
    return high, low


def rows_of(devices, rows):
    return (np.asarray(devices)[:, None] * rows + np.arange(rows)).reshape(-1)


def device_tables(count, rows, side):
    outer = count // (INNER * CORES)
    positions = np.arange(side)
    forward, twist = [], []
    for device in range(count):
        wanted = rows_of([device ^ (INNER * CORES * j) for j in range(outer)], rows)
        held = rows_of([device ^ core ^ (CORES * m) for core in range(CORES) for m in range(INNER)], rows)
        angle = angles(wanted, held, side)
        forward.append(np.concatenate(split(np.concatenate([np.cos(angle), -np.sin(angle)]))))
        angle = angles(wanted, positions, side * side)
        twist.append(np.stack([np.cos(angle), np.sin(angle)]))
    return np.stack(forward), np.stack(twist).astype(np.float32)


def transform_table(side):
    angle = angles(np.arange(side), np.arange(side), side)
    cos_high, cos_low = split(np.cos(angle))
    sin_high, sin_low = split(np.sin(angle))
    return np.concatenate([cos_high, sin_high, cos_low[:, :BAND], sin_low[:, :BAND]], 1)


def dot(left, right):
    return jnp.dot(left, right, preferred_element_type=jnp.float32)


def halves(value):
    high = value.astype(jnp.bfloat16)
    return high, (value - high.astype(jnp.float32)).astype(jnp.bfloat16)


def partial_spectrum(blocks, forward, twist, table):
    _, wanted, side = twist.shape
    high, low = halves(jnp.concatenate(blocks, 0))
    both = dot(forward, high)
    first = both[: 2 * wanted] + both[2 * wanted :] + dot(forward[: 2 * wanted], low)
    real, imag = first[:wanted], first[wanted:]
    turned = jnp.concatenate([real * twist[0] + imag * twist[1], imag * twist[0] - real * twist[1]], 0)
    high, low = halves(turned)
    by_part = []
    for part in range(2):
        both = dot(jnp.concatenate([high, low], 0), table[:, part * side : part * side + BAND])
        rest = dot(high, table[:, 2 * side + part * BAND : 2 * side + (part + 1) * BAND])
        by_part.append(both[: 2 * wanted] + both[2 * wanted :] + rest)
    by_cos, by_sin = by_part
    return by_cos[:wanted] + by_sin[wanted:], by_cos[wanted:] - by_sin[:wanted]


def sections(parts, asd, keep, spectra, twist_cos, twist_sin, table):
    templ_count, _, rows, _ = spectra.shape
    side = twist_cos.shape[1]
    white = functools.reduce(jnp.add, parts)
    white_real, white_imag = white[:rows] * asd, white[rows:] * asd
    product = []
    for part in range(2):
        for templ in range(templ_count):
            spec_real = spectra[templ, 0].astype(jnp.float32)
            spec_imag = spectra[templ, 1].astype(jnp.float32)
            if part == 0:
                value = white_real * spec_real + white_imag * spec_imag
            else:
                value = white_imag * spec_real - white_real * spec_imag
            product.append(jnp.where(keep[templ : templ + 1] > 0, value, 0.0).astype(jnp.bfloat16))
    turned = dot(jnp.concatenate(product, 0), table[:BAND, : 2 * side])
    group = templ_count * rows
    real_part = turned[:group, :side] - turned[group:, side:]
    imag_part = turned[:group, side:] + turned[group:, :side]
    result = []
    for part in range(2):
        for templ in range(templ_count):
            here = slice(templ * rows, (templ + 1) * rows)
            if part == 0:
                result.append(real_part[here] * twist_cos - imag_part[here] * twist_sin)
            else:
                result.append(real_part[here] * twist_sin + imag_part[here] * twist_cos)
    return result


def last_stage(received, table, templ_count):
    side = received.shape[0]
    scale = 1.0 / (side * side)
    turned = lax.dot_general(received, table, (((0,), (0,)), ((), ())), preferred_element_type=jnp.float32)
    group = turned.shape[0] // 2
    real_part = (turned[:group, :side] - turned[group:, side:]) * scale
    imag_part = (turned[:group, side:] + turned[group:, :side]) * scale
    return real_part, imag_part


def spread(slots, rows):
    count = len(slots)
    lane = lax.broadcasted_iota(jnp.int32, slots[0].shape, 1)
    lanes = slots[0].shape[1]
    bit = 1
    while bit < count:
        step = rows * bit
        keep = (lane // step) % 2 == 0
        after = list(slots)
        for low in range(count):
            if low & bit:
                continue
            high = low | bit
            after[low] = jnp.where(keep, slots[low], pltpu.roll(slots[high], step, 1))
            after[high] = jnp.where(keep, pltpu.roll(slots[low], lanes - step, 1), slots[high])
        slots = after
        bit *= 2
    return slots


def prepare_kernel(
    forwards, twists, table, strain, inv_asd, cutoff, forward, twist, table_out, strain_out, asd, keep, limits, arrived
):
    device = lax.axis_index("freq")
    moves = (
        (cutoff, limits),
        (strain, strain_out),
        (forwards.at[device], forward),
        (twists.at[device], twist),
        (inv_asd.at[:, :BAND], asd),
        (table, table_out),
    )
    copies = [pltpu.make_async_copy(source, target, arrived.at[i]) for i, (source, target) in enumerate(moves)]
    for copy in copies:
        copy.start()
    copies[0].wait()
    band = lax.broadcasted_iota(jnp.int32, (1, BAND), 1)
    for templ in range(keep.shape[0]):
        keep[templ : templ + 1, :] = jnp.where(band < limits[templ], 1.0, 0.0)
    for copy in copies[1:]:
        copy.wait()


def spectrum_kernel(*refs):
    inputs = INNER * CORES + 3
    (*blocks, forward, twist, table), outs = refs[:inputs], refs[inputs:]
    real, imag = partial_spectrum([block[...] for block in blocks], forward[...], twist, table)
    rows = outs[0].shape[0] // 2
    for m, out in enumerate(outs):
        out[:rows] = real[m * rows : (m + 1) * rows]
        out[rows:] = imag[m * rows : (m + 1) * rows]


def section_kernel(*refs):
    *parts, asd, keep, spectra, twist, table, out = refs
    rows = asd.shape[0]
    slots = sections(
        [part[...] for part in parts], asd[...], keep[...], spectra, twist[0, :rows], twist[1, :rows], table
    )
    for start in range(0, twist.shape[2], 128):
        pieces = spread([slot[:, start : start + 128] for slot in slots], rows)
        for place, piece in enumerate(pieces):
            out[start // rows + place] = piece.astype(jnp.bfloat16)


def last_kernel(received, table, series, peak):
    templ_count, _, rows, side = series.shape
    real_part, imag_part = last_stage(received[...], table[:, : 2 * side], templ_count)
    power = real_part * real_part + imag_part * imag_part
    best = power[:rows]
    for templ in range(templ_count):
        here = slice(templ * rows, (templ + 1) * rows)
        series[templ, 0] = real_part[here]
        series[templ, 1] = imag_part[here]
        best = jnp.maximum(best, power[here])
    peak[...] = best


def local(device_count, strain, inv_asd, spectra, cutoff):
    rows, side = strain.shape
    templ_count = spectra.shape[1]
    outer = device_count // (INNER * CORES)
    forwards, twists = (jnp.asarray(x) for x in device_tables(device_count, rows, side))
    table = jnp.asarray(transform_table(side))
    tiles_fit = rows % 16 == 0 and 2 * templ_count * rows == 128 and side % 128 == 0
    params = pltpu.CompilerParams(vmem_limit_bytes=VMEM_LIMIT)
    vmem = pl.BlockSpec(memory_space=pltpu.VMEM)
    hbm = pl.BlockSpec(memory_space=pltpu.HBM)

    def swap(value, distance):
        return lax.ppermute(value, "freq", [(i, i ^ distance) for i in range(device_count)])

    held = [None] * INNER
    for m in (3, 2, 1):
        held[m] = swap(strain, CORES * m)
    if tiles_fit:
        results = [
            pltpu.VMEM(forwards.shape[1:], jnp.bfloat16),
            pltpu.VMEM(twists.shape[1:], jnp.float32),
            pltpu.VMEM(table.shape, jnp.bfloat16),
            pltpu.VMEM(strain.shape, jnp.float32),
            pltpu.VMEM((rows, BAND), jnp.float32),
            pltpu.VMEM((templ_count, BAND), jnp.float32),
        ]
        sources = (forwards, twists, table, strain, inv_asd, cutoff)
        forward, twist, table, mine, asd, keep = pl.pallas_call(
            prepare_kernel,
            out_shape=results,
            in_specs=[hbm] * 6,
            out_specs=[vmem] * 6,
            scratch_shapes=[pltpu.SMEM(cutoff.shape, jnp.int32), pltpu.SemaphoreType.DMA((6,))],
            compiler_params=params,
            cost_estimate=pl.CostEstimate(flops=0, bytes_accessed=4 * table.size, transcendentals=0),
        )(*[pltpu.with_memory_space_constraint(source, pltpu.HBM) for source in sources])
    else:
        device = lax.axis_index("freq")
        forward, twist, mine, asd = forwards[device], twists[device], strain, inv_asd[:, :BAND]
        keep = (jnp.arange(BAND, dtype=jnp.int32)[None, :] < cutoff[:, None]).astype(jnp.float32)
    by_templ = jnp.transpose(spectra[..., :BAND], (1, 2, 0, 3))
    held[0] = mine
    held[1], forward, twist, table, asd, keep = lax.optimization_barrier((held[1], forward, twist, table, asd, keep))
    blocks = held + [swap(strain if j == 0 else block, 1) for j, block in enumerate(held)]
    if tiles_fit:
        parts = pl.pallas_call(
            spectrum_kernel,
            out_shape=[jax.ShapeDtypeStruct((2 * rows, BAND), jnp.float32)] * outer,
            in_specs=[vmem] * (len(blocks) + 3),
            out_specs=[vmem] * outer,
            compiler_params=params,
        )(*blocks, forward, twist, table)
    else:
        real, imag = partial_spectrum(blocks, forward, twist, table)
        parts = [jnp.concatenate([x[m * rows : (m + 1) * rows] for x in (real, imag)], 0) for m in range(outer)]
    parts, by_templ = lax.optimization_barrier((list(parts), by_templ))
    parts = [parts[0]] + [swap(parts[j], INNER * CORES * j) for j in (3, 1, 2)]
    if tiles_fit:
        outgoing = pl.pallas_call(
            section_kernel,
            out_shape=jax.ShapeDtypeStruct((device_count, rows, 128), jnp.bfloat16),
            in_specs=[vmem] * (outer + 5),
            out_specs=vmem,
            compiler_params=params,
        )(*parts, asd, keep, by_templ, twist, table)
    else:
        slots = sections(parts, asd, keep, by_templ, twist[0, :rows], twist[1, :rows], table)
        slots = jnp.stack(slots).astype(jnp.bfloat16).reshape(2 * templ_count, rows, device_count, rows)
        outgoing = jnp.transpose(slots, (2, 1, 0, 3)).reshape(device_count, rows, -1)
    received = lax.all_to_all(outgoing, "freq", 0, 0, tiled=True).reshape(side, -1)
    if tiles_fit:
        series, peak = pl.pallas_call(
            last_kernel,
            out_shape=(
                jax.ShapeDtypeStruct((templ_count, 2, rows, side), jnp.float32),
                jax.ShapeDtypeStruct((rows, side), jnp.float32),
            ),
            in_specs=[vmem] * 2,
            out_specs=(vmem, vmem),
            compiler_params=params,
        )(received, table)
    else:
        both = jnp.stack(last_stage(received, table[:, : 2 * side], templ_count))
        series = jnp.transpose(both.reshape(2, templ_count, rows, side), (1, 0, 2, 3))
        peak = jnp.max(series[:, 0] ** 2 + series[:, 1] ** 2, axis=0)
    return series, lax.pmax(peak, "tmpl")


def solution(mesh):
    in_specs = (P("freq", None), P("freq", None), P("freq", "tmpl", None, None), P("tmpl"))
    out_specs = (P("tmpl", None, "freq", None), P("freq", None))
    return jax.shard_map(
        functools.partial(local, mesh.shape["freq"]),
        mesh=mesh,
        in_specs=in_specs,
        out_specs=out_specs,
        check_vma=False,
    )
```

time: 42.4 us -> 32.7 us (0.77)
  blocking collectives: 29.5 us -> 10.1 us
  starting transfers between devices: 0.01 us -> 9.58 us
  waiting for transfers between devices: 0.01 us -> 8.33 us
  local copies, waits for them, and re-layouts: 5.33 us -> 0.02 us
  Pallas kernels: 5.76 us -> 3.83 us
  other arithmetic: 0.76 us -> 0 us
    all_to_all x1 -> x0, blocking collectives: 18 us -> none  [local(): lax.all_to_all(copies, 'freq', 0, 0, tiled=True, axis_index_groups=groups)]
    ppermute x1 -> x10, starting transfers between devices: 0.01 us -> 9.58 us  [swap(): lax.ppermute(value, 'freq', [(i, i ^ distance) for i in range(device_coun...]
    ppermute x1 -> x10, waiting for transfers between devices: 0.01 us -> 8.33 us  [swap(): lax.ppermute(value, 'freq', [(i, i ^ distance) for i in range(device_coun...]
    dynamic_slice x2 -> x0, local copies, waits for them, and re-layouts: 2.94 us -> none  [the longest x1 1.47 us: local(): lax.dynamic_slice_in_dim(jnp.asarray(twist_all), device * rows, rows, 1)]
    unnamed x5 -> x1, local copies, waits for them, and re-layouts: 2.38 us -> 0.01 us
    all_to_all x1, blocking collectives: 11.5 us -> 10.1 us  [local(): lax.all_to_all(outgoing, 'freq', 0, 0, tiled=True).reshape(side, -1)]
    pallas_call x1, Pallas kernels: 2.35 us -> 1.04 us  [local(): pl.pallas_call(last_kernel, out_shape=(jax.ShapeDtypeStruct((templ_count,...]
    convert_element_type x1 -> x0, other arithmetic: 0.76 us -> none  [local(): strain.astype(jnp.bfloat16)[None]]
  transfers between devices with their start and end apart: 1 -> 10, of which waited for: 0 -> 6; matrix products, arithmetic and copies ran while one was open for 11% -> 0% of each run, Pallas kernels for 0% -> 5%
where the time goes in v3:
time: 32.7 us; the launch traced here: 32.5 us
  blocking collectives  10.1 us (31%)
  starting transfers between devices  9.58 us (29%)
  waiting for transfers between devices  8.33 us (25%)
  Pallas kernels  3.83 us (12%)
  between operations  0.71 us (2%)
    all_to_all x1, blocking collectives, local(): lax.all_to_all(outgoing, 'freq', 0, 0, tiled=True).reshape(side, -1)  10.1 us
    ppermute x10, starting transfers between devices, swap(): lax.ppermute(value, 'freq', [(i, i ^ distance) for i in range(device_coun...  9.58 us
    ppermute x10, waiting for transfers between devices, swap(): lax.ppermute(value, 'freq', [(i, i ^ distance) for i in range(device_coun...  8.33 us
    pallas_call x1, Pallas kernels, local(): pl.pallas_call(prepare_kernel, out_shape=results, in_specs=[hbm] * 6, out...  1.62 us
    pallas_call x1, Pallas kernels, local(): pl.pallas_call(last_kernel, out_shape=(jax.ShapeDtypeStruct((templ_count,...  1.04 us
    pallas_call x1, Pallas kernels, local(): pl.pallas_call(spectrum_kernel, out_shape=[jax.ShapeDtypeStruct((2 * rows...  0.68 us
  transfers between devices with their start and end apart: 10, of which 6 were waited for; matrix products, arithmetic and copies ran while one was open for 0% of the time, Pallas kernels for 5%

profile of v3, /device:TPU:0, one launch (start us, length us, event | category | flops | bytes accessed | tf_op | source)
XLA Modules:
  0.0 32.5 jit_solution(11320227860846885726)
XLA Ops:
  0.6 0.0 slice-start
  0.6 3.0 %collective-permute-start = (f32[16,512]{1,0:T(8,128)}, f32[16,512]{1,0:T(8,128)S(1)}, u32[]{:S(2)}, u32[]{:S(2)}) collective-permute-start(f32[16,512]{1,0:T(8,128)} %strain.1), channel_id=1, source_target_pairs={{0,2},{1,3},{2,0},{3,1},{4,6},{5,7},{6,4},{7,5},{8,10},{9,11},{10,... | collective-permute-start | bytes 98312 | tf_op jit(solution)/shard_map/ppermute | solution.py:209
  3.6 1.5 %collective-permute-start.1 = (f32[16,512]{1,0:T(8,128)}, f32[16,512]{1,0:T(8,128)S(1)}, u32[]{:S(2)}, u32[]{:S(2)}) collective-permute-start(f32[16,512]{1,0:T(8,128)} %strain.1), channel_id=1, source_target_pairs={{0,4},{1,5},{2,6},{3,7},{4,0},{5,1},{6,2},{7,3},{8,12},{9,13},{10,... | collective-permute-start | bytes 98312 | tf_op jit(solution)/shard_map/ppermute | solution.py:209
  5.2 0.0 collective-permute-start.2
  5.2 0.0 collective-permute-start.3
  5.2 1.6 %shard_map.86 = (bf16[256,128]{1,0:T(8,128)(2,1)S(1)}, f32[2,64,512]{2,1,0:T(8,128)S(1)}, bf16[512,1536]{1,0:T(8,128)(2,1)S(1)}, f32[16,512]{1,0:T(8,128)S(1)}, ...) custom-call(bf16[32,256,128]{2,1,0:T(8,128)(2,1)} %constant.6.clone.forwards, f32[32,2,64,512]{3,2,1,0:T(8,128)} %constant.7.clone.twists, ...), custom_call_target="tpu_custom_call" | custom-call | bytes 3145728 | tf_op jit(solution)/shard_map/pallas_call | solution.py:224
  6.8 0.0 collective-permute-done.refs_1_
  6.8 0.6 %collective-permute-start.4 = (f32[16,512]{1,0:T(8,128)S(1)}, f32[16,512]{1,0:T(8,128)S(1)}, u32[]{:S(2)}, u32[]{:S(2)}) collective-permute-start(f32[16,512]{1,0:T(8,128)S(1)} %collective-permute-done.refs_1_), channel_id=1, source_target_pairs={{0,1},{1,0},{2,3},{3,2},{4,5},{5,4},{6,7},{7,6},{8,9},{9,8},{10,11... | collective-permute-start | bytes 98312 | tf_op jit(solution)/shard_map/ppermute | solution.py:209
  7.4 0.4 %collective-permute-done.1.refs_2_ = f32[16,512]{1,0:T(8,128)S(1)} collective-permute-done((f32[16,512]{1,0:T(8,128)}, f32[16,512]{1,0:T(8,128)S(1)}, u32[]{:S(2)}, u32[]{:S(2)}) %collective-permute-start.1) | collective-permute-done | bytes 32800 | tf_op jit(solution)/shard_map/ppermute | solution.py:209
  7.8 0.0 collective-permute-start.5
  7.8 2.4 %collective-permute-done.2.refs_3_ = f32[16,512]{1,0:T(8,128)S(1)} collective-permute-done((f32[16,512]{1,0:T(8,128)}, f32[16,512]{1,0:T(8,128)S(1)}, u32[]{:S(2)}, u32[]{:S(2)}) %collective-permute-start.2) | collective-permute-done | bytes 32800 | tf_op jit(solution)/shard_map/ppermute | solution.py:209
  10.2 0.0 collective-permute-done.4.refs_5_
  10.2 0.0 collective-permute-done.5.refs_6_
  10.2 1.2 %collective-permute-done.6.refs_7_ = f32[16,512]{1,0:T(8,128)S(1)} collective-permute-done((f32[16,512]{1,0:T(8,128)S(1)}, f32[16,512]{1,0:T(8,128)S(1)}, u32[]{:S(2)}, u32[]{:S(2)}) %collective-permute-start.6) | collective-permute-done | bytes 32800 | tf_op jit(solution)/shard_map/ppermute | solution.py:209
  11.4 0.7 %shard_map.87 = (f32[32,256]{1,0:T(8,128)S(1)}, f32[32,256]{1,0:T(8,128)S(1)}, f32[32,256]{1,0:T(8,128)S(1)}, f32[32,256]{1,0:T(8,128)S(1)}) custom-call(f32[16,512]{1,0:T(8,128)S(1)} %get-tuple-element.23.refs_0_, f32[16,512]{1,0:T(8,128)S(1)} %collective-permute-done.refs_1_, f32[16,512]{1,0:T(8,128)S(1)} %collective-permute-done.1.refs_2_, ...), custom_call_target="tpu_custom_call" | custom-call | tf_op jit(solution)/shard_map/pallas_call | solution.py:242
  12.1 3.7 %collective-permute-start.7 = (f32[32,256]{1,0:T(8,128)S(1)}, f32[32,256]{1,0:T(8,128)S(1)}, u32[]{:S(2)}, u32[]{:S(2)}) collective-permute-start(f32[32,256]{1,0:T(8,128)S(1)} %get-tuple-element.38), channel_id=1, source_target_pairs={{0,24},{1,25},{2,26},{3,27},{4,28},{5,29},{6,30},{7,31},{8,16},{9,... | collective-permute-start | bytes 98312 | tf_op jit(solution)/shard_map/ppermute | solution.py:209
  15.8 0.0 collective-permute-start.8
  15.8 0.8 %collective-permute-start.9 = (f32[32,256]{1,0:T(8,128)S(1)}, f32[32,256]{1,0:T(8,128)S(1)}, u32[]{:S(2)}, u32[]{:S(2)}) collective-permute-start(f32[32,256]{1,0:T(8,128)S(1)} %get-tuple-element.40), channel_id=1, source_target_pairs={{0,16},{1,17},{2,18},{3,19},{4,20},{5,21},{6,22},{7,23},{8,24},{9,... | collective-permute-start | bytes 98312 | tf_op jit(solution)/shard_map/ppermute | solution.py:209
  16.5 1.3 %collective-permute-done.7.refs_1_ = f32[32,256]{1,0:T(8,128)S(1)} collective-permute-done((f32[32,256]{1,0:T(8,128)S(1)}, f32[32,256]{1,0:T(8,128)S(1)}, u32[]{:S(2)}, u32[]{:S(2)}) %collective-permute-start.7) | collective-permute-done | bytes 32800 | tf_op jit(solution)/shard_map/ppermute | solution.py:209
  17.9 2.0 %collective-permute-done.8.refs_2_ = f32[32,256]{1,0:T(8,128)S(1)} collective-permute-done((f32[32,256]{1,0:T(8,128)S(1)}, f32[32,256]{1,0:T(8,128)S(1)}, u32[]{:S(2)}, u32[]{:S(2)}) %collective-permute-start.8) | collective-permute-done | bytes 32800 | tf_op jit(solution)/shard_map/ppermute | solution.py:209
  19.8 1.1 %collective-permute-done.9.refs_3_ = f32[32,256]{1,0:T(8,128)S(1)} collective-permute-done((f32[32,256]{1,0:T(8,128)S(1)}, f32[32,256]{1,0:T(8,128)S(1)}, u32[]{:S(2)}, u32[]{:S(2)}) %collective-permute-start.9) | collective-permute-done | bytes 32800 | tf_op jit(solution)/shard_map/ppermute | solution.py:209
  20.9 0.5 %shard_map.88 = bf16[32,16,128]{2,1,0:T(8,128)(2,1)S(1)} custom-call(f32[32,256]{1,0:T(8,128)S(1)} %get-tuple-element.37.refs_0_, f32[32,256]{1,0:T(8,128)S(1)} %collective-permute-done.7.refs_1_, f32[32,256]{1,0:T(8,128)S(1)} %collective-permute-done.8.refs_2_, f32[32,256]{1,0:T(8,128)S(1)} %collective-permute-done.9.refs_3_, ...), custom_call_target="tpu_custom_call" | custom-call | tf_op jit(solution)/shard_map/pallas_call | solution.py:255
  21.4 10.1 %all_to_all.5 = bf16[32,16,128]{2,1,0:T(8,128)(2,1)S(1)} all-to-all(bf16[32,16,128]{2,1,0:T(8,128)(2,1)S(1)} %shard_map.88), channel_id=1, replica_groups=mesh['tmpl'=1,'freq'=32] {'freq'}, dimensions={0} | all-to-all | bytes 262144 | tf_op jit(solution)/shard_map/all_to_all | solution.py:266
  31.5 1.0 %shard_map.89 = (f32[4,2,16,512]{3,2,1,0:T(8,128)}, f32[16,512]{1,0:T(8,128)}) custom-call(bf16[512,128]{1,0:T(8,128)(2,1)S(1)} %bitcast.4, bf16[512,1536]{1,0:T(8,128)(2,1)S(1)} %get-tuple-element.32.refs_10_.refs_8_.table), custom_call_target="tpu_custom_call" | custom-call | tf_op jit(solution)/shard_map/pallas_call | solution.py:268
  (4 shorter events, 0.0 us)
Async XLA Ops:
  0.6 9.6 %slice-start = ((bf16[16,4,2,512]{3,2,1,0:T(2,128)(2,1)}), bf16[16,4,2,256]{3,2,1,0:T(2,128)(2,1)S(1)}, s32[]{:S(2)}) async-start(bf16[16,4,2,512]{3,2,1,0:T(2,128)(2,1)} %param.9), calls=%async_computation.1 | async-start | bytes 131072 | tf_op jit(solution)/shard_map/slice | solution.py:237
  0.6 6.2 %collective-permute-start = (f32[16,512]{1,0:T(8,128)}, f32[16,512]{1,0:T(8,128)S(1)}, u32[]{:S(2)}, u32[]{:S(2)}) collective-permute-start(f32[16,512]{1,0:T(8,128)} %strain.1), channel_id=1, source_target_pairs={{0,2},{1,3},{2,0},{3,1},{4,6},{5,7},{6,4},{7,5},{8,10},{9,11},{10,... | collective-permute-start | bytes 98312 | tf_op jit(solution)/shard_map/ppermute | solution.py:209
  3.6 4.1 %collective-permute-start.1 = (f32[16,512]{1,0:T(8,128)}, f32[16,512]{1,0:T(8,128)S(1)}, u32[]{:S(2)}, u32[]{:S(2)}) collective-permute-start(f32[16,512]{1,0:T(8,128)} %strain.1), channel_id=1, source_target_pairs={{0,4},{1,5},{2,6},{3,7},{4,0},{5,1},{6,2},{7,3},{8,12},{9,13},{10,... | collective-permute-start | bytes 98312 | tf_op jit(solution)/shard_map/ppermute | solution.py:209
  5.2 5.0 %collective-permute-start.2 = (f32[16,512]{1,0:T(8,128)}, f32[16,512]{1,0:T(8,128)S(1)}, u32[]{:S(2)}, u32[]{:S(2)}) collective-permute-start(f32[16,512]{1,0:T(8,128)} %strain.1), channel_id=1, source_target_pairs={{0,6},{1,7},{2,4},{3,5},{4,2},{5,3},{6,0},{7,1},{8,14},{9,15},{10,... | collective-permute-start | bytes 98312 | tf_op jit(solution)/shard_map/ppermute | solution.py:209
  5.2 5.0 %collective-permute-start.3 = (f32[16,512]{1,0:T(8,128)}, f32[16,512]{1,0:T(8,128)S(1)}, u32[]{:S(2)}, u32[]{:S(2)}) collective-permute-start(f32[16,512]{1,0:T(8,128)} %strain.1), channel_id=1, source_target_pairs={{0,1},{1,0},{2,3},{3,2},{4,5},{5,4},{6,7},{7,6},{8,9},{9,8},{10,11... | collective-permute-start | bytes 98312 | tf_op jit(solution)/shard_map/ppermute | solution.py:209
  6.8 3.4 %collective-permute-start.4 = (f32[16,512]{1,0:T(8,128)S(1)}, f32[16,512]{1,0:T(8,128)S(1)}, u32[]{:S(2)}, u32[]{:S(2)}) collective-permute-start(f32[16,512]{1,0:T(8,128)S(1)} %collective-permute-done.refs_1_), channel_id=1, source_target_pairs={{0,1},{1,0},{2,3},{3,2},{4,5},{5,4},{6,7},{7,6},{8,9},{9,8},{10,11... | collective-permute-start | bytes 98312 | tf_op jit(solution)/shard_map/ppermute | solution.py:209
  7.8 2.5 %collective-permute-start.5 = (f32[16,512]{1,0:T(8,128)S(1)}, f32[16,512]{1,0:T(8,128)S(1)}, u32[]{:S(2)}, u32[]{:S(2)}) collective-permute-start(f32[16,512]{1,0:T(8,128)S(1)} %collective-permute-done.1.refs_2_), channel_id=1, source_target_pairs={{0,1},{1,0},{2,3},{3,2},{4,5},{5,4},{6,7},{7,6},{8,9},{9,8},{10,11... | collective-permute-start | bytes 98312 | tf_op jit(solution)/shard_map/ppermute | solution.py:209
  10.2 1.2 %collective-permute-start.6 = (f32[16,512]{1,0:T(8,128)S(1)}, f32[16,512]{1,0:T(8,128)S(1)}, u32[]{:S(2)}, u32[]{:S(2)}) collective-permute-start(f32[16,512]{1,0:T(8,128)S(1)} %collective-permute-done.2.refs_3_), channel_id=1, source_target_pairs={{0,1},{1,0},{2,3},{3,2},{4,5},{5,4},{6,7},{7,6},{8,9},{9,8},{10,11... | collective-permute-start | bytes 98312 | tf_op jit(solution)/shard_map/ppermute | solution.py:209
  12.1 5.8 %collective-permute-start.7 = (f32[32,256]{1,0:T(8,128)S(1)}, f32[32,256]{1,0:T(8,128)S(1)}, u32[]{:S(2)}, u32[]{:S(2)}) collective-permute-start(f32[32,256]{1,0:T(8,128)S(1)} %get-tuple-element.38), channel_id=1, source_target_pairs={{0,24},{1,25},{2,26},{3,27},{4,28},{5,29},{6,30},{7,31},{8,16},{9,... | collective-permute-start | bytes 98312 | tf_op jit(solution)/shard_map/ppermute | solution.py:209
  15.8 4.1 %collective-permute-start.8 = (f32[32,256]{1,0:T(8,128)S(1)}, f32[32,256]{1,0:T(8,128)S(1)}, u32[]{:S(2)}, u32[]{:S(2)}) collective-permute-start(f32[32,256]{1,0:T(8,128)S(1)} %get-tuple-element.39), channel_id=1, source_target_pairs={{0,8},{1,9},{2,10},{3,11},{4,12},{5,13},{6,14},{7,15},{8,0},{9,1},... | collective-permute-start | bytes 98312 | tf_op jit(solution)/shard_map/ppermute | solution.py:209
  15.8 5.2 %collective-permute-start.9 = (f32[32,256]{1,0:T(8,128)S(1)}, f32[32,256]{1,0:T(8,128)S(1)}, u32[]{:S(2)}, u32[]{:S(2)}) collective-permute-start(f32[32,256]{1,0:T(8,128)S(1)} %get-tuple-element.40), channel_id=1, source_target_pairs={{0,16},{1,17},{2,18},{3,19},{4,20},{5,21},{6,22},{7,23},{8,24},{9,... | collective-permute-start | bytes 98312 | tf_op jit(solution)/shard_map/ppermute | solution.py:209

commit v4 on v3

--- a/solution.py
+++ b/solution.py
@@ -12,6 +12,7 @@
 BAND = 256
 CORES = 2
 INNER = 4
+LANES = 128
 VMEM_LIMIT = 16 << 20
 
 
@@ -27,6 +28,14 @@
 
 def rows_of(devices, rows):
     return (np.asarray(devices)[:, None] * rows + np.arange(rows)).reshape(-1)
+
+
+def plane(device, step):
+    return device ^ (CORES * step ^ 1 if step else 0)
+
+
+def line(device, step):
+    return device ^ (INNER * CORES * step ^ 1 if step else 0)
 
 
 def device_tables(count, rows, side):
@@ -34,8 +43,8 @@
     positions = np.arange(side)
     forward, twist = [], []
     for device in range(count):
-        wanted = rows_of([device ^ (INNER * CORES * j) for j in range(outer)], rows)
-        held = rows_of([device ^ core ^ (CORES * m) for core in range(CORES) for m in range(INNER)], rows)
+        wanted = rows_of([line(device, step) for step in range(outer)], rows)
+        held = rows_of([plane(device ^ core, step) for core in range(CORES) for step in range(INNER)], rows)
         angle = angles(wanted, held, side)
         forward.append(np.concatenate(split(np.concatenate([np.cos(angle), -np.sin(angle)]))))
         angle = angles(wanted, positions, side * side)
@@ -47,7 +56,11 @@
     angle = angles(np.arange(side), np.arange(side), side)
     cos_high, cos_low = split(np.cos(angle))
     sin_high, sin_low = split(np.sin(angle))
-    return np.concatenate([cos_high, sin_high, cos_low[:, :BAND], sin_low[:, :BAND]], 1)
+    columns = []
+    for cos_part, sin_part, width in ((cos_high, sin_high, side), (cos_low, sin_low, BAND)):
+        for start in range(0, width, LANES):
+            columns += [x[:, start : start + LANES] for x in (cos_part, sin_part)]
+    return np.concatenate(columns, 1)
 
 
 def dot(left, right):
@@ -57,6 +70,13 @@
 def halves(value):
     high = value.astype(jnp.bfloat16)
     return high, (value - high.astype(jnp.float32)).astype(jnp.bfloat16)
+
+
+def turns(value):
+    starts = range(0, value.shape[1], 2 * LANES)
+    return tuple(
+        jnp.concatenate([value[:, start + part : start + part + LANES] for start in starts], 1) for part in (0, LANES)
+    )
 
 
 def partial_spectrum(blocks, forward, twist, table):
@@ -67,21 +87,17 @@
     real, imag = first[:wanted], first[wanted:]
     turned = jnp.concatenate([real * twist[0] + imag * twist[1], imag * twist[0] - real * twist[1]], 0)
     high, low = halves(turned)
-    by_part = []
-    for part in range(2):
-        both = dot(jnp.concatenate([high, low], 0), table[:, part * side : part * side + BAND])
-        rest = dot(high, table[:, 2 * side + part * BAND : 2 * side + (part + 1) * BAND])
-        by_part.append(both[: 2 * wanted] + both[2 * wanted :] + rest)
-    by_cos, by_sin = by_part
+    both = dot(jnp.concatenate([high, low], 0), table[:, : 2 * BAND])
+    second = both[: 2 * wanted] + both[2 * wanted :] + dot(high, table[:, 2 * side :])
+    by_cos, by_sin = turns(second)
     return by_cos[:wanted] + by_sin[wanted:], by_cos[wanted:] - by_sin[:wanted]
 
 
-def sections(parts, asd, keep, spectra, twist_cos, twist_sin, table):
+def products(parts, asd, keep, spectra):
     templ_count, _, rows, _ = spectra.shape
-    side = twist_cos.shape[1]
     white = functools.reduce(jnp.add, parts)
     white_real, white_imag = white[:rows] * asd, white[rows:] * asd
-    product = []
+    result = []
     for part in range(2):
         for templ in range(templ_count):
             spec_real = spectra[templ, 0].astype(jnp.float32)
@@ -90,15 +106,20 @@
                 value = white_real * spec_real + white_imag * spec_imag
             else:
                 value = white_imag * spec_real - white_real * spec_imag
-            product.append(jnp.where(keep[templ : templ + 1] > 0, value, 0.0).astype(jnp.bfloat16))
-    turned = dot(jnp.concatenate(product, 0), table[:BAND, : 2 * side])
-    group = templ_count * rows
-    real_part = turned[:group, :side] - turned[group:, side:]
-    imag_part = turned[:group, side:] + turned[group:, :side]
+            result.append(jnp.where(keep[templ : templ + 1] > 0, value, 0.0).astype(jnp.bfloat16))
+    return jnp.concatenate(result, 0)
+
+
+def section(product, table, twist_cos, twist_sin):
+    rows = twist_cos.shape[0]
+    group = product.shape[0] // 2
+    by_cos, by_sin = turns(dot(product, table))
+    real_part = by_cos[:group] - by_sin[group:]
+    imag_part = by_sin[:group] + by_cos[group:]
     result = []
     for part in range(2):
-        for templ in range(templ_count):
-            here = slice(templ * rows, (templ + 1) * rows)
+        for start in range(0, group, rows):
+            here = slice(start, start + rows)
             if part == 0:
                 result.append(real_part[here] * twist_cos - imag_part[here] * twist_sin)
             else:
@@ -106,14 +127,11 @@
     return result
 
 
-def last_stage(received, table, templ_count):
-    side = received.shape[0]
-    scale = 1.0 / (side * side)
+def last_stage(received, table, total):
     turned = lax.dot_general(received, table, (((0,), (0,)), ((), ())), preferred_element_type=jnp.float32)
+    by_cos, by_sin = turns(turned)
     group = turned.shape[0] // 2
-    real_part = (turned[:group, :side] - turned[group:, side:]) * scale
-    imag_part = (turned[:group, side:] + turned[group:, :side]) * scale
-    return real_part, imag_part
+    return (by_cos[:group] - by_sin[group:]) * (1.0 / total), (by_sin[:group] + by_cos[group:]) * (1.0 / total)
 
 
 def spread(slots, rows):
@@ -172,27 +190,30 @@
 def section_kernel(*refs):
     *parts, asd, keep, spectra, twist, table, out = refs
     rows = asd.shape[0]
-    slots = sections(
-        [part[...] for part in parts], asd[...], keep[...], spectra, twist[0, :rows], twist[1, :rows], table
-    )
-    for start in range(0, twist.shape[2], 128):
-        pieces = spread([slot[:, start : start + 128] for slot in slots], rows)
-        for place, piece in enumerate(pieces):
+    product = products([part[...] for part in parts], asd[...], keep[...], spectra)
+    for start in range(0, twist.shape[2], LANES):
+        columns = slice(start, start + LANES)
+        slots = section(
+            product, table[:BAND, 2 * start : 2 * (start + LANES)], twist[0, :rows, columns], twist[1, :rows, columns]
+        )
+        for place, piece in enumerate(spread(slots, rows)):
             out[start // rows + place] = piece.astype(jnp.bfloat16)
 
 
 def last_kernel(received, table, series, peak):
     templ_count, _, rows, side = series.shape
-    real_part, imag_part = last_stage(received[...], table[:, : 2 * side], templ_count)
-    power = real_part * real_part + imag_part * imag_part
-    best = power[:rows]
-    for templ in range(templ_count):
-        here = slice(templ * rows, (templ + 1) * rows)
-        series[templ, 0] = real_part[here]
-        series[templ, 1] = imag_part[here]
-        best = jnp.maximum(best, power[here])
-    peak[...] = best
-
+    values = received[...]
+    for start in range(0, side, LANES):
+        columns = slice(start, start + LANES)
+        real_part, imag_part = last_stage(values, table[:, 2 * start : 2 * (start + LANES)], side * side)
+        power = real_part * real_part + imag_part * imag_part
+        best = power[:rows]
+        for templ in range(templ_count):
+            here = slice(templ * rows, (templ + 1) * rows)
+            series[templ, 0, :, columns] = real_part[here]
+            series[templ, 1, :, columns] = imag_part[here]
+            best = jnp.maximum(best, power[here])
+        peak[:, columns] = best
 
 def local(device_count, strain, inv_asd, spectra, cutoff):
     rows, side = strain.shape
@@ -205,12 +226,10 @@
     vmem = pl.BlockSpec(memory_space=pltpu.VMEM)
     hbm = pl.BlockSpec(memory_space=pltpu.HBM)
 
-    def swap(value, distance):
-        return lax.ppermute(value, "freq", [(i, i ^ distance) for i in range(device_count)])
-
-    held = [None] * INNER
-    for m in (3, 2, 1):
-        held[m] = swap(strain, CORES * m)
+    def exchange(value, partner):
+        return lax.ppermute(value, "freq", [(i, partner(i)) for i in range(device_count)])
+
+    held = [strain] + [exchange(strain, functools.partial(plane, step=step)) for step in range(1, INNER)]
     if tiles_fit:
         results = [
             pltpu.VMEM(forwards.shape[1:], jnp.bfloat16),
@@ -237,7 +256,7 @@
     by_templ = jnp.transpose(spectra[..., :BAND], (1, 2, 0, 3))
     held[0] = mine
     held[1], forward, twist, table, asd, keep = lax.optimization_barrier((held[1], forward, twist, table, asd, keep))
-    blocks = held + [swap(strain if j == 0 else block, 1) for j, block in enumerate(held)]
+    blocks = held + [exchange(block, lambda i: i ^ 1) for block in [strain] + held[1:]]
     if tiles_fit:
         parts = pl.pallas_call(
             spectrum_kernel,
@@ -250,7 +269,8 @@
         real, imag = partial_spectrum(blocks, forward, twist, table)
         parts = [jnp.concatenate([x[m * rows : (m + 1) * rows] for x in (real, imag)], 0) for m in range(outer)]
     parts, by_templ = lax.optimization_barrier((list(parts), by_templ))
-    parts = [parts[0]] + [swap(parts[j], INNER * CORES * j) for j in (3, 1, 2)]
+    received = [exchange(parts[step], functools.partial(line, step=step)) for step in reversed(range(1, outer))]
+    parts = parts[:1] + received
     if tiles_fit:
         outgoing = pl.pallas_call(
             section_kernel,
@@ -260,7 +280,8 @@
             compiler_params=params,
         )(*parts, asd, keep, by_templ, twist, table)
     else:
-        slots = sections(parts, asd, keep, by_templ, twist[0, :rows], twist[1, :rows], table)
+        product = products(parts, asd, keep, by_templ)
+        slots = section(product, table[:BAND, : 2 * side], twist[0, :rows], twist[1, :rows])
         slots = jnp.stack(slots).astype(jnp.bfloat16).reshape(2 * templ_count, rows, device_count, rows)
         outgoing = jnp.transpose(slots, (2, 1, 0, 3)).reshape(device_count, rows, -1)
     received = lax.all_to_all(outgoing, "freq", 0, 0, tiled=True).reshape(side, -1)
@@ -276,7 +297,7 @@
             compiler_params=params,
         )(received, table)
     else:
-        both = jnp.stack(last_stage(received, table[:, : 2 * side], templ_count))
+        both = jnp.stack(last_stage(received, table[:, : 2 * side], side * side))
         series = jnp.transpose(both.reshape(2, templ_count, rows, side), (1, 0, 2, 3))
         peak = jnp.max(series[:, 0] ** 2 + series[:, 1] ** 2, axis=0)
     return series, lax.pmax(peak, "tmpl")

time: 32.7 us -> 31.2 us (0.954)
  waiting for transfers between devices: 8.33 us -> 7.06 us
  starting transfers between devices: 9.58 us -> 9.18 us
    ppermute x10, waiting for transfers between devices: 8.33 us -> 7.06 us  [exchange(): lax.ppermute(value, 'freq', [(i, partner(i)) for i in range(device_count)])]
    ppermute x10, starting transfers between devices: 9.58 us -> 9.18 us  [exchange(): lax.ppermute(value, 'freq', [(i, partner(i)) for i in range(device_count)])]
  transfers between devices with their start and end apart: 10 -> 10, of which waited for: 6 -> 4; matrix products, arithmetic and copies ran while one was open for 0% -> 0% of each run, Pallas kernels for 5% -> 5%
where the time goes in v4:
time: 31.2 us; the launch traced here: 31.1 us
  blocking collectives  10.4 us (33%)
  starting transfers between devices  9.18 us (29%)
  waiting for transfers between devices  7.06 us (23%)
  Pallas kernels  3.73 us (12%)
  between operations  0.71 us (2%)
    all_to_all x1, blocking collectives, local(): lax.all_to_all(outgoing, 'freq', 0, 0, tiled=True).reshape(side, -1)  10.4 us
    ppermute x10, starting transfers between devices, exchange(): lax.ppermute(value, 'freq', [(i, partner(i)) for i in range(device_count)])  9.18 us
    ppermute x10, waiting for transfers between devices, exchange(): lax.ppermute(value, 'freq', [(i, partner(i)) for i in range(device_count)])  7.06 us
    pallas_call x1, Pallas kernels, local(): pl.pallas_call(prepare_kernel, out_shape=results, in_specs=[hbm] * 6, out...  1.62 us
    pallas_call x1, Pallas kernels, local(): pl.pallas_call(last_kernel, out_shape=(jax.ShapeDtypeStruct((templ_count,...  1.04 us
  transfers between devices with their start and end apart: 10, of which 4 were waited for; matrix products, arithmetic and copies ran while one was open for 0% of the time, Pallas kernels for 5%

profile of v4, /device:TPU:0, one launch (start us, length us, event | category | flops | bytes accessed | tf_op | source)
XLA Modules:
  0.0 31.1 jit_solution(17501645898995661840)
XLA Ops:
  0.6 0.0 slice-start
  0.6 2.4 %collective-permute-start = (f32[16,512]{1,0:T(8,128)}, f32[16,512]{1,0:T(8,128)S(1)}, u32[]{:S(2)}, u32[]{:S(2)}) collective-permute-start(f32[16,512]{1,0:T(8,128)} %strain.1), channel_id=1, source_target_pairs={{0,3},{1,2},{2,1},{3,0},{4,7},{5,6},{6,5},{7,4},{8,11},{9,10},{10,... | collective-permute-start | bytes 98312 | tf_op jit(solution)/shard_map/ppermute | solution.py:230
  3.1 1.8 %collective-permute-start.1 = (f32[16,512]{1,0:T(8,128)}, f32[16,512]{1,0:T(8,128)S(1)}, u32[]{:S(2)}, u32[]{:S(2)}) collective-permute-start(f32[16,512]{1,0:T(8,128)} %strain.1), channel_id=1, source_target_pairs={{0,5},{1,4},{2,7},{3,6},{4,1},{5,0},{6,3},{7,2},{8,13},{9,12},{10,... | collective-permute-start | bytes 98312 | tf_op jit(solution)/shard_map/ppermute | solution.py:230
  4.9 0.0 collective-permute-start.2
  4.9 0.0 collective-permute-start.3
  4.9 1.6 %shard_map.86 = (bf16[256,128]{1,0:T(8,128)(2,1)S(1)}, f32[2,64,512]{2,1,0:T(8,128)S(1)}, bf16[512,1536]{1,0:T(8,128)(2,1)S(1)}, f32[16,512]{1,0:T(8,128)S(1)}, ...) custom-call(bf16[32,256,128]{2,1,0:T(8,128)(2,1)} %constant.6.clone.forwards, f32[32,2,64,512]{3,2,1,0:T(8,128)} %constant.7.clone.twists, ...), custom_call_target="tpu_custom_call" | custom-call | bytes 3145728 | tf_op jit(solution)/shard_map/pallas_call | solution.py:243
  6.5 0.0 collective-permute-done.refs_1_
  6.5 0.6 %collective-permute-start.4 = (f32[16,512]{1,0:T(8,128)S(1)}, f32[16,512]{1,0:T(8,128)S(1)}, u32[]{:S(2)}, u32[]{:S(2)}) collective-permute-start(f32[16,512]{1,0:T(8,128)S(1)} %collective-permute-done.refs_1_), channel_id=1, source_target_pairs={{0,1},{1,0},{2,3},{3,2},{4,5},{5,4},{6,7},{7,6},{8,9},{9,8},{10,11... | collective-permute-start | bytes 98312 | tf_op jit(solution)/shard_map/ppermute | solution.py:230
  7.1 0.2 collective-permute-start.5
  7.3 2.4 %collective-permute-done.2.refs_3_ = f32[16,512]{1,0:T(8,128)S(1)} collective-permute-done((f32[16,512]{1,0:T(8,128)}, f32[16,512]{1,0:T(8,128)S(1)}, u32[]{:S(2)}, u32[]{:S(2)}) %collective-permute-start.2) | collective-permute-done | bytes 32800 | tf_op jit(solution)/shard_map/ppermute | solution.py:230
  9.7 0.1 collective-permute-start.6
  9.8 0.0 collective-permute-done.3.refs_4_
  9.8 0.0 collective-permute-done.5.refs_6_
  9.8 1.0 %collective-permute-done.6.refs_7_ = f32[16,512]{1,0:T(8,128)S(1)} collective-permute-done((f32[16,512]{1,0:T(8,128)S(1)}, f32[16,512]{1,0:T(8,128)S(1)}, u32[]{:S(2)}, u32[]{:S(2)}) %collective-permute-start.6) | collective-permute-done | bytes 32800 | tf_op jit(solution)/shard_map/ppermute | solution.py:230
  10.9 0.6 %shard_map.87 = (f32[32,256]{1,0:T(8,128)S(1)}, f32[32,256]{1,0:T(8,128)S(1)}, f32[32,256]{1,0:T(8,128)S(1)}, f32[32,256]{1,0:T(8,128)S(1)}) custom-call(f32[16,512]{1,0:T(8,128)S(1)} %get-tuple-element.23.refs_0_, f32[16,512]{1,0:T(8,128)S(1)} %collective-permute-done.refs_1_, f32[16,512]{1,0:T(8,128)S(1)} %collective-permute-done.1.refs_2_, ...), custom_call_target="tpu_custom_call" | custom-call | tf_op jit(solution)/shard_map/pallas_call | solution.py:261
  11.5 3.4 %collective-permute-start.7 = (f32[32,256]{1,0:T(8,128)S(1)}, f32[32,256]{1,0:T(8,128)S(1)}, u32[]{:S(2)}, u32[]{:S(2)}) collective-permute-start(f32[32,256]{1,0:T(8,128)S(1)} %get-tuple-element.38), channel_id=1, source_target_pairs={{0,25},{1,24},{2,27},{3,26},{4,29},{5,28},{6,31},{7,30},{8,17},{9,... | collective-permute-start | bytes 98312 | tf_op jit(solution)/shard_map/ppermute | solution.py:230
  14.9 0.0 collective-permute-start.8
  14.9 0.6 %collective-permute-start.9 = (f32[32,256]{1,0:T(8,128)S(1)}, f32[32,256]{1,0:T(8,128)S(1)}, u32[]{:S(2)}, u32[]{:S(2)}) collective-permute-start(f32[32,256]{1,0:T(8,128)S(1)} %get-tuple-element.40), channel_id=1, source_target_pairs={{0,9},{1,8},{2,11},{3,10},{4,13},{5,12},{6,15},{7,14},{8,1},{9,0},... | collective-permute-start | bytes 98312 | tf_op jit(solution)/shard_map/ppermute | solution.py:230
  15.5 1.2 %collective-permute-done.7.refs_1_ = f32[32,256]{1,0:T(8,128)S(1)} collective-permute-done((f32[32,256]{1,0:T(8,128)S(1)}, f32[32,256]{1,0:T(8,128)S(1)}, u32[]{:S(2)}, u32[]{:S(2)}) %collective-permute-start.7) | collective-permute-done | bytes 32800 | tf_op jit(solution)/shard_map/ppermute | solution.py:230
  16.7 2.5 %collective-permute-done.8.refs_2_ = f32[32,256]{1,0:T(8,128)S(1)} collective-permute-done((f32[32,256]{1,0:T(8,128)S(1)}, f32[32,256]{1,0:T(8,128)S(1)}, u32[]{:S(2)}, u32[]{:S(2)}) %collective-permute-start.8) | collective-permute-done | bytes 32800 | tf_op jit(solution)/shard_map/ppermute | solution.py:230
  19.2 0.0 collective-permute-done.9.refs_3_
  19.2 0.5 %shard_map.88 = bf16[32,16,128]{2,1,0:T(8,128)(2,1)S(1)} custom-call(f32[32,256]{1,0:T(8,128)S(1)} %get-tuple-element.37.refs_0_, f32[32,256]{1,0:T(8,128)S(1)} %collective-permute-done.7.refs_1_, f32[32,256]{1,0:T(8,128)S(1)} %collective-permute-done.8.refs_2_, f32[32,256]{1,0:T(8,128)S(1)} %collective-permute-done.9.refs_3_, ...), custom_call_target="tpu_custom_call" | custom-call | tf_op jit(solution)/shard_map/pallas_call | solution.py:275
  19.6 10.4 %all_to_all.5 = bf16[32,16,128]{2,1,0:T(8,128)(2,1)S(1)} all-to-all(bf16[32,16,128]{2,1,0:T(8,128)(2,1)S(1)} %shard_map.88), channel_id=1, replica_groups=mesh['tmpl'=1,'freq'=32] {'freq'}, dimensions={0} | all-to-all | bytes 262144 | tf_op jit(solution)/shard_map/all_to_all | solution.py:287
  30.0 1.0 %shard_map.89 = (f32[4,2,16,512]{3,2,1,0:T(8,128)}, f32[16,512]{1,0:T(8,128)}) custom-call(bf16[512,128]{1,0:T(8,128)(2,1)S(1)} %bitcast.4, bf16[512,1536]{1,0:T(8,128)(2,1)S(1)} %get-tuple-element.32.refs_10_.refs_8_.table), custom_call_target="tpu_custom_call" | custom-call | tf_op jit(solution)/shard_map/pallas_call | solution.py:289
  (4 shorter events, 0.0 us)
Async XLA Ops:
  0.6 9.2 %slice-start = ((bf16[16,4,2,512]{3,2,1,0:T(2,128)(2,1)}), bf16[16,4,2,256]{3,2,1,0:T(2,128)(2,1)S(1)}, s32[]{:S(2)}) async-start(bf16[16,4,2,512]{3,2,1,0:T(2,128)(2,1)} %param.9), calls=%async_computation.1 | async-start | bytes 131072 | tf_op jit(solution)/shard_map/slice | solution.py:256
  0.6 5.9 %collective-permute-start = (f32[16,512]{1,0:T(8,128)}, f32[16,512]{1,0:T(8,128)S(1)}, u32[]{:S(2)}, u32[]{:S(2)}) collective-permute-start(f32[16,512]{1,0:T(8,128)} %strain.1), channel_id=1, source_target_pairs={{0,3},{1,2},{2,1},{3,0},{4,7},{5,6},{6,5},{7,4},{8,11},{9,10},{10,... | collective-permute-start | bytes 98312 | tf_op jit(solution)/shard_map/ppermute | solution.py:230
  3.1 4.0 %collective-permute-start.1 = (f32[16,512]{1,0:T(8,128)}, f32[16,512]{1,0:T(8,128)S(1)}, u32[]{:S(2)}, u32[]{:S(2)}) collective-permute-start(f32[16,512]{1,0:T(8,128)} %strain.1), channel_id=1, source_target_pairs={{0,5},{1,4},{2,7},{3,6},{4,1},{5,0},{6,3},{7,2},{8,13},{9,12},{10,... | collective-permute-start | bytes 98312 | tf_op jit(solution)/shard_map/ppermute | solution.py:230
  4.9 4.8 %collective-permute-start.2 = (f32[16,512]{1,0:T(8,128)}, f32[16,512]{1,0:T(8,128)S(1)}, u32[]{:S(2)}, u32[]{:S(2)}) collective-permute-start(f32[16,512]{1,0:T(8,128)} %strain.1), channel_id=1, source_target_pairs={{0,7},{1,6},{2,5},{3,4},{4,3},{5,2},{6,1},{7,0},{8,15},{9,14},{10,... | collective-permute-start | bytes 98312 | tf_op jit(solution)/shard_map/ppermute | solution.py:230
  4.9 4.9 %collective-permute-start.3 = (f32[16,512]{1,0:T(8,128)}, f32[16,512]{1,0:T(8,128)S(1)}, u32[]{:S(2)}, u32[]{:S(2)}) collective-permute-start(f32[16,512]{1,0:T(8,128)} %strain.1), channel_id=1, source_target_pairs={{0,1},{1,0},{2,3},{3,2},{4,5},{5,4},{6,7},{7,6},{8,9},{9,8},{10,11... | collective-permute-start | bytes 98312 | tf_op jit(solution)/shard_map/ppermute | solution.py:230
  6.5 3.3 %collective-permute-start.4 = (f32[16,512]{1,0:T(8,128)S(1)}, f32[16,512]{1,0:T(8,128)S(1)}, u32[]{:S(2)}, u32[]{:S(2)}) collective-permute-start(f32[16,512]{1,0:T(8,128)S(1)} %collective-permute-done.refs_1_), channel_id=1, source_target_pairs={{0,1},{1,0},{2,3},{3,2},{4,5},{5,4},{6,7},{7,6},{8,9},{9,8},{10,11... | collective-permute-start | bytes 98312 | tf_op jit(solution)/shard_map/ppermute | solution.py:230
  7.1 2.7 %collective-permute-start.5 = (f32[16,512]{1,0:T(8,128)S(1)}, f32[16,512]{1,0:T(8,128)S(1)}, u32[]{:S(2)}, u32[]{:S(2)}) collective-permute-start(f32[16,512]{1,0:T(8,128)S(1)} %collective-permute-done.1.refs_2_), channel_id=1, source_target_pairs={{0,1},{1,0},{2,3},{3,2},{4,5},{5,4},{6,7},{7,6},{8,9},{9,8},{10,11... | collective-permute-start | bytes 98312 | tf_op jit(solution)/shard_map/ppermute | solution.py:230
  9.7 1.2 %collective-permute-start.6 = (f32[16,512]{1,0:T(8,128)S(1)}, f32[16,512]{1,0:T(8,128)S(1)}, u32[]{:S(2)}, u32[]{:S(2)}) collective-permute-start(f32[16,512]{1,0:T(8,128)S(1)} %collective-permute-done.2.refs_3_), channel_id=1, source_target_pairs={{0,1},{1,0},{2,3},{3,2},{4,5},{5,4},{6,7},{7,6},{8,9},{9,8},{10,11... | collective-permute-start | bytes 98312 | tf_op jit(solution)/shard_map/ppermute | solution.py:230
  11.5 5.2 %collective-permute-start.7 = (f32[32,256]{1,0:T(8,128)S(1)}, f32[32,256]{1,0:T(8,128)S(1)}, u32[]{:S(2)}, u32[]{:S(2)}) collective-permute-start(f32[32,256]{1,0:T(8,128)S(1)} %get-tuple-element.38), channel_id=1, source_target_pairs={{0,25},{1,24},{2,27},{3,26},{4,29},{5,28},{6,31},{7,30},{8,17},{9,... | collective-permute-start | bytes 98312 | tf_op jit(solution)/shard_map/ppermute | solution.py:230
  14.9 4.3 %collective-permute-start.8 = (f32[32,256]{1,0:T(8,128)S(1)}, f32[32,256]{1,0:T(8,128)S(1)}, u32[]{:S(2)}, u32[]{:S(2)}) collective-permute-start(f32[32,256]{1,0:T(8,128)S(1)} %get-tuple-element.39), channel_id=1, source_target_pairs={{0,17},{1,16},{2,19},{3,18},{4,21},{5,20},{6,23},{7,22},{8,25},{9,... | collective-permute-start | bytes 98312 | tf_op jit(solution)/shard_map/ppermute | solution.py:230
  14.9 4.3 %collective-permute-start.9 = (f32[32,256]{1,0:T(8,128)S(1)}, f32[32,256]{1,0:T(8,128)S(1)}, u32[]{:S(2)}, u32[]{:S(2)}) collective-permute-start(f32[32,256]{1,0:T(8,128)S(1)} %get-tuple-element.40), channel_id=1, source_target_pairs={{0,9},{1,8},{2,11},{3,10},{4,13},{5,12},{6,15},{7,14},{8,1},{9,0},... | collective-permute-start | bytes 98312 | tf_op jit(solution)/shard_map/ppermute | solution.py:230

commit v5 on v4

--- a/solution.py
+++ b/solution.py
@@ -30,8 +30,20 @@
     return (np.asarray(devices)[:, None] * rows + np.arange(rows)).reshape(-1)
 
 
-def plane(device, step):
-    return device ^ (CORES * step ^ 1 if step else 0)
+def across(device):
+    return device ^ (INNER - 1) * CORES ^ 1
+
+
+def beside(device):
+    chip = device // CORES
+    return device ^ CORES * (1 + (chip + chip // 2 + device) % 2) ^ 1
+
+
+def held_by(device):
+    result = [device, device ^ 1]
+    for here in (device, device ^ 1):
+        result += [beside(here), beside(here) ^ 1, across(here)]
+    return result
 
 
 def line(device, step):
@@ -44,7 +56,7 @@
     forward, twist = [], []
     for device in range(count):
         wanted = rows_of([line(device, step) for step in range(outer)], rows)
-        held = rows_of([plane(device ^ core, step) for core in range(CORES) for step in range(INNER)], rows)
+        held = rows_of(held_by(device), rows)
         angle = angles(wanted, held, side)
         forward.append(np.concatenate(split(np.concatenate([np.cos(angle), -np.sin(angle)]))))
         angle = angles(wanted, positions, side * side)
@@ -215,6 +227,7 @@
             best = jnp.maximum(best, power[here])
         peak[:, columns] = best
 
+
 def local(device_count, strain, inv_asd, spectra, cutoff):
     rows, side = strain.shape
     templ_count = spectra.shape[1]
@@ -229,7 +242,10 @@
     def exchange(value, partner):
         return lax.ppermute(value, "freq", [(i, partner(i)) for i in range(device_count)])
 
-    held = [strain] + [exchange(strain, functools.partial(plane, step=step)) for step in range(1, INNER)]
+    other = exchange(strain, lambda i: i ^ 1)
+    first = exchange(strain, beside)
+    second = exchange(other, beside)
+    single = exchange(strain, across)
     if tiles_fit:
         results = [
             pltpu.VMEM(forwards.shape[1:], jnp.bfloat16),
@@ -254,9 +270,8 @@
         forward, twist, mine, asd = forwards[device], twists[device], strain, inv_asd[:, :BAND]
         keep = (jnp.arange(BAND, dtype=jnp.int32)[None, :] < cutoff[:, None]).astype(jnp.float32)
     by_templ = jnp.transpose(spectra[..., :BAND], (1, 2, 0, 3))
-    held[0] = mine
-    held[1], forward, twist, table, asd, keep = lax.optimization_barrier((held[1], forward, twist, table, asd, keep))
-    blocks = held + [exchange(block, lambda i: i ^ 1) for block in [strain] + held[1:]]
+    single, forward, twist, table, asd, keep = lax.optimization_barrier((single, forward, twist, table, asd, keep))
+    blocks = [mine, other, first, second, single] + [exchange(block, lambda i: i ^ 1) for block in (first, second, single)]
     if tiles_fit:
         parts = pl.pallas_call(
             spectrum_kernel,

time: 31.2 us -> 31.1 us (level)
  waiting for transfers between devices: 7.06 us -> 4.77 us
  starting transfers between devices: 9.18 us -> 10.5 us
  blocking collectives: 10.4 us -> 11.2 us
    ppermute x10, waiting for transfers between devices: 7.06 us -> 4.77 us  [exchange(): lax.ppermute(value, 'freq', [(i, partner(i)) for i in range(device_count)])]
    ppermute x10, starting transfers between devices: 9.18 us -> 10.5 us  [exchange(): lax.ppermute(value, 'freq', [(i, partner(i)) for i in range(device_count)])]
    all_to_all x1, blocking collectives: 10.4 us -> 11.2 us  [local(): lax.all_to_all(outgoing, 'freq', 0, 0, tiled=True).reshape(side, -1)]
  transfers between devices with their start and end apart: 10 -> 10, of which waited for: 4 -> 5; matrix products, arithmetic and copies ran while one was open for 0% -> 0% of each run, Pallas kernels for 5% -> 5%
where the time goes in v5:
time: 31.1 us; the launch traced here: 30.9 us
  blocking collectives  11.2 us (36%)
  starting transfers between devices  10.5 us (34%)
  waiting for transfers between devices  4.77 us (15%)
  Pallas kernels  3.73 us (12%)
  between operations  0.68 us (2%)
    all_to_all x1, blocking collectives, local(): lax.all_to_all(outgoing, 'freq', 0, 0, tiled=True).reshape(side, -1)  11.2 us
    ppermute x10, starting transfers between devices, exchange(): lax.ppermute(value, 'freq', [(i, partner(i)) for i in range(device_count)])  10.5 us
    ppermute x10, waiting for transfers between devices, exchange(): lax.ppermute(value, 'freq', [(i, partner(i)) for i in range(device_count)])  4.77 us
    pallas_call x1, Pallas kernels, local(): pl.pallas_call(prepare_kernel, out_shape=results, in_specs=[hbm] * 6, out...  1.62 us
    pallas_call x1, Pallas kernels, local(): pl.pallas_call(last_kernel, out_shape=(jax.ShapeDtypeStruct((templ_count,...  1.04 us
  transfers between devices with their start and end apart: 10, of which 5 were waited for; matrix products, arithmetic and copies ran while one was open for 0% of the time, Pallas kernels for 5%

profile of v5, /device:TPU:0, one launch (start us, length us, event | category | flops | bytes accessed | tf_op | source)
XLA Modules:
  0.0 30.9 jit_solution(4345577504845963587)
XLA Ops:
  0.6 0.0 slice-start
  0.6 0.5 %collective-permute-start = (f32[16,512]{1,0:T(8,128)}, f32[16,512]{1,0:T(8,128)S(1)}, u32[]{:S(2)}, u32[]{:S(2)}) collective-permute-start(f32[16,512]{1,0:T(8,128)} %strain.1), channel_id=1, source_target_pairs={{0,1},{1,0},{2,3},{3,2},{4,5},{5,4},{6,7},{7,6},{8,9},{9,8},{10,11... | collective-permute-start | bytes 98312 | tf_op jit(solution)/shard_map/ppermute | solution.py:243
  1.2 3.6 %collective-permute-start.3 = (f32[16,512]{1,0:T(8,128)}, f32[16,512]{1,0:T(8,128)S(1)}, u32[]{:S(2)}, u32[]{:S(2)}) collective-permute-start(f32[16,512]{1,0:T(8,128)} %strain.1), channel_id=1, source_target_pairs={{0,7},{1,6},{2,5},{3,4},{4,3},{5,2},{6,1},{7,0},{8,15},{9,14},{10,... | collective-permute-start | bytes 98312 | tf_op jit(solution)/shard_map/ppermute | solution.py:243
  4.7 0.2 collective-permute-start.1
  4.9 0.0 collective-permute-done.refs_1_
  4.9 1.5 %collective-permute-start.2 = (f32[16,512]{1,0:T(8,128)S(1)}, f32[16,512]{1,0:T(8,128)S(1)}, u32[]{:S(2)}, u32[]{:S(2)}) collective-permute-start(f32[16,512]{1,0:T(8,128)S(1)} %collective-permute-done.refs_1_), channel_id=1, source_target_pairs={{0,3},{1,4},{2,7},{3,0},{4,1},{5,6},{6,5},{7,2},{8,11},{9,12},{10,... | collective-permute-start | bytes 98312 | tf_op jit(solution)/shard_map/ppermute | solution.py:243
  6.5 1.6 %shard_map.86 = (bf16[256,128]{1,0:T(8,128)(2,1)S(1)}, f32[2,64,512]{2,1,0:T(8,128)S(1)}, bf16[512,1536]{1,0:T(8,128)(2,1)S(1)}, f32[16,512]{1,0:T(8,128)S(1)}, ...) custom-call(bf16[32,256,128]{2,1,0:T(8,128)(2,1)} %constant.6.clone.forwards, f32[32,2,64,512]{3,2,1,0:T(8,128)} %constant.7.clone.twists, ...), custom_call_target="tpu_custom_call" | custom-call | bytes 3145728 | tf_op jit(solution)/shard_map/pallas_call | solution.py:259
  8.1 0.0 collective-permute-done.3.refs_4_
  8.1 0.1 collective-permute-start.6
  8.2 0.0 collective-permute-done.1.refs_2_
  8.3 0.4 %collective-permute-start.4 = (f32[16,512]{1,0:T(8,128)S(1)}, f32[16,512]{1,0:T(8,128)S(1)}, u32[]{:S(2)}, u32[]{:S(2)}) collective-permute-start(f32[16,512]{1,0:T(8,128)S(1)} %collective-permute-done.1.refs_2_), channel_id=1, source_target_pairs={{0,1},{1,0},{2,3},{3,2},{4,5},{5,4},{6,7},{7,6},{8,9},{9,8},{10,11... | collective-permute-start | bytes 98312 | tf_op jit(solution)/shard_map/ppermute | solution.py:243
  8.7 0.1 collective-permute-start.5
  8.8 0.6 %collective-permute-done.6.refs_7_ = f32[16,512]{1,0:T(8,128)S(1)} collective-permute-done((f32[16,512]{1,0:T(8,128)S(1)}, f32[16,512]{1,0:T(8,128)S(1)}, u32[]{:S(2)}, u32[]{:S(2)}) %collective-permute-start.6) | collective-permute-done | bytes 32800 | tf_op jit(solution)/shard_map/ppermute | solution.py:243
  9.4 0.2 collective-permute-done.4.refs_5_
  9.6 0.4 %collective-permute-done.5.refs_6_ = f32[16,512]{1,0:T(8,128)S(1)} collective-permute-done((f32[16,512]{1,0:T(8,128)S(1)}, f32[16,512]{1,0:T(8,128)S(1)}, u32[]{:S(2)}, u32[]{:S(2)}) %collective-permute-start.5) | collective-permute-done | bytes 32800 | tf_op jit(solution)/shard_map/ppermute | solution.py:243
  9.9 0.6 %shard_map.87 = (f32[32,256]{1,0:T(8,128)S(1)}, f32[32,256]{1,0:T(8,128)S(1)}, f32[32,256]{1,0:T(8,128)S(1)}, f32[32,256]{1,0:T(8,128)S(1)}) custom-call(f32[16,512]{1,0:T(8,128)S(1)} %get-tuple-element.23.refs_0_, f32[16,512]{1,0:T(8,128)S(1)} %collective-permute-done.refs_1_, f32[16,512]{1,0:T(8,128)S(1)} %collective-permute-done.1.refs_2_, ...), custom_call_target="tpu_custom_call" | custom-call | tf_op jit(solution)/shard_map/pallas_call | solution.py:276
  10.5 3.4 %collective-permute-start.7 = (f32[32,256]{1,0:T(8,128)S(1)}, f32[32,256]{1,0:T(8,128)S(1)}, u32[]{:S(2)}, u32[]{:S(2)}) collective-permute-start(f32[32,256]{1,0:T(8,128)S(1)} %get-tuple-element.38), channel_id=1, source_target_pairs={{0,25},{1,24},{2,27},{3,26},{4,29},{5,28},{6,31},{7,30},{8,17},{9,... | collective-permute-start | bytes 98312 | tf_op jit(solution)/shard_map/ppermute | solution.py:243
  13.9 0.0 collective-permute-start.8
  13.9 0.6 %collective-permute-start.9 = (f32[32,256]{1,0:T(8,128)S(1)}, f32[32,256]{1,0:T(8,128)S(1)}, u32[]{:S(2)}, u32[]{:S(2)}) collective-permute-start(f32[32,256]{1,0:T(8,128)S(1)} %get-tuple-element.40), channel_id=1, source_target_pairs={{0,9},{1,8},{2,11},{3,10},{4,13},{5,12},{6,15},{7,14},{8,1},{9,0},... | collective-permute-start | bytes 98312 | tf_op jit(solution)/shard_map/ppermute | solution.py:243
  14.5 1.2 %collective-permute-done.7.refs_1_ = f32[32,256]{1,0:T(8,128)S(1)} collective-permute-done((f32[32,256]{1,0:T(8,128)S(1)}, f32[32,256]{1,0:T(8,128)S(1)}, u32[]{:S(2)}, u32[]{:S(2)}) %collective-permute-start.7) | collective-permute-done | bytes 32800 | tf_op jit(solution)/shard_map/ppermute | solution.py:243
  15.7 2.5 %collective-permute-done.8.refs_2_ = f32[32,256]{1,0:T(8,128)S(1)} collective-permute-done((f32[32,256]{1,0:T(8,128)S(1)}, f32[32,256]{1,0:T(8,128)S(1)}, u32[]{:S(2)}, u32[]{:S(2)}) %collective-permute-start.8) | collective-permute-done | bytes 32800 | tf_op jit(solution)/shard_map/ppermute | solution.py:243
  18.2 0.5 %shard_map.88 = bf16[32,16,128]{2,1,0:T(8,128)(2,1)S(1)} custom-call(f32[32,256]{1,0:T(8,128)S(1)} %get-tuple-element.37.refs_0_, f32[32,256]{1,0:T(8,128)S(1)} %collective-permute-done.7.refs_1_, f32[32,256]{1,0:T(8,128)S(1)} %collective-permute-done.8.refs_2_, f32[32,256]{1,0:T(8,128)S(1)} %collective-permute-done.9.refs_3_, ...), custom_call_target="tpu_custom_call" | custom-call | tf_op jit(solution)/shard_map/pallas_call | solution.py:290
  18.7 11.2 %all_to_all.5 = bf16[32,16,128]{2,1,0:T(8,128)(2,1)S(1)} all-to-all(bf16[32,16,128]{2,1,0:T(8,128)(2,1)S(1)} %shard_map.88), channel_id=1, replica_groups=mesh['tmpl'=1,'freq'=32] {'freq'}, dimensions={0} | all-to-all | bytes 262144 | tf_op jit(solution)/shard_map/all_to_all | solution.py:302
  29.9 1.0 %shard_map.89 = (f32[4,2,16,512]{3,2,1,0:T(8,128)}, f32[16,512]{1,0:T(8,128)}) custom-call(bf16[512,128]{1,0:T(8,128)(2,1)S(1)} %bitcast.4, bf16[512,1536]{1,0:T(8,128)(2,1)S(1)} %get-tuple-element.32.refs_10_.refs_8_.table), custom_call_target="tpu_custom_call" | custom-call | tf_op jit(solution)/shard_map/pallas_call | solution.py:304
  (4 shorter events, 0.0 us)
Async XLA Ops:
  0.6 8.2 %slice-start = ((bf16[16,4,2,512]{3,2,1,0:T(2,128)(2,1)}), bf16[16,4,2,256]{3,2,1,0:T(2,128)(2,1)S(1)}, s32[]{:S(2)}) async-start(bf16[16,4,2,512]{3,2,1,0:T(2,128)(2,1)} %param.9), calls=%async_computation.1 | async-start | bytes 131072 | tf_op jit(solution)/shard_map/slice | solution.py:272
  0.6 4.3 %collective-permute-start = (f32[16,512]{1,0:T(8,128)}, f32[16,512]{1,0:T(8,128)S(1)}, u32[]{:S(2)}, u32[]{:S(2)}) collective-permute-start(f32[16,512]{1,0:T(8,128)} %strain.1), channel_id=1, source_target_pairs={{0,1},{1,0},{2,3},{3,2},{4,5},{5,4},{6,7},{7,6},{8,9},{9,8},{10,11... | collective-permute-start | bytes 98312 | tf_op jit(solution)/shard_map/ppermute | solution.py:243
  1.2 6.9 %collective-permute-start.3 = (f32[16,512]{1,0:T(8,128)}, f32[16,512]{1,0:T(8,128)S(1)}, u32[]{:S(2)}, u32[]{:S(2)}) collective-permute-start(f32[16,512]{1,0:T(8,128)} %strain.1), channel_id=1, source_target_pairs={{0,7},{1,6},{2,5},{3,4},{4,3},{5,2},{6,1},{7,0},{8,15},{9,14},{10,... | collective-permute-start | bytes 98312 | tf_op jit(solution)/shard_map/ppermute | solution.py:243
  4.7 3.6 %collective-permute-start.1 = (f32[16,512]{1,0:T(8,128)}, f32[16,512]{1,0:T(8,128)S(1)}, u32[]{:S(2)}, u32[]{:S(2)}) collective-permute-start(f32[16,512]{1,0:T(8,128)} %strain.1), channel_id=1, source_target_pairs={{0,3},{1,4},{2,7},{3,0},{4,1},{5,6},{6,5},{7,2},{8,11},{9,12},{10,... | collective-permute-start | bytes 98312 | tf_op jit(solution)/shard_map/ppermute | solution.py:243
  4.9 3.8 %collective-permute-start.2 = (f32[16,512]{1,0:T(8,128)S(1)}, f32[16,512]{1,0:T(8,128)S(1)}, u32[]{:S(2)}, u32[]{:S(2)}) collective-permute-start(f32[16,512]{1,0:T(8,128)S(1)} %collective-permute-done.refs_1_), channel_id=1, source_target_pairs={{0,3},{1,4},{2,7},{3,0},{4,1},{5,6},{6,5},{7,2},{8,11},{9,12},{10,... | collective-permute-start | bytes 98312 | tf_op jit(solution)/shard_map/ppermute | solution.py:243
  8.1 1.3 %collective-permute-start.6 = (f32[16,512]{1,0:T(8,128)S(1)}, f32[16,512]{1,0:T(8,128)S(1)}, u32[]{:S(2)}, u32[]{:S(2)}) collective-permute-start(f32[16,512]{1,0:T(8,128)S(1)} %collective-permute-done.3.refs_4_), channel_id=1, source_target_pairs={{0,1},{1,0},{2,3},{3,2},{4,5},{5,4},{6,7},{7,6},{8,9},{9,8},{10,11... | collective-permute-start | bytes 98312 | tf_op jit(solution)/shard_map/ppermute | solution.py:243
  8.3 1.3 %collective-permute-start.4 = (f32[16,512]{1,0:T(8,128)S(1)}, f32[16,512]{1,0:T(8,128)S(1)}, u32[]{:S(2)}, u32[]{:S(2)}) collective-permute-start(f32[16,512]{1,0:T(8,128)S(1)} %collective-permute-done.1.refs_2_), channel_id=1, source_target_pairs={{0,1},{1,0},{2,3},{3,2},{4,5},{5,4},{6,7},{7,6},{8,9},{9,8},{10,11... | collective-permute-start | bytes 98312 | tf_op jit(solution)/shard_map/ppermute | solution.py:243
  8.7 1.2 %collective-permute-start.5 = (f32[16,512]{1,0:T(8,128)S(1)}, f32[16,512]{1,0:T(8,128)S(1)}, u32[]{:S(2)}, u32[]{:S(2)}) collective-permute-start(f32[16,512]{1,0:T(8,128)S(1)} %collective-permute-done.2.refs_3_), channel_id=1, source_target_pairs={{0,1},{1,0},{2,3},{3,2},{4,5},{5,4},{6,7},{7,6},{8,9},{9,8},{10,11... | collective-permute-start | bytes 98312 | tf_op jit(solution)/shard_map/ppermute | solution.py:243
  10.5 5.2 %collective-permute-start.7 = (f32[32,256]{1,0:T(8,128)S(1)}, f32[32,256]{1,0:T(8,128)S(1)}, u32[]{:S(2)}, u32[]{:S(2)}) collective-permute-start(f32[32,256]{1,0:T(8,128)S(1)} %get-tuple-element.38), channel_id=1, source_target_pairs={{0,25},{1,24},{2,27},{3,26},{4,29},{5,28},{6,31},{7,30},{8,17},{9,... | collective-permute-start | bytes 98312 | tf_op jit(solution)/shard_map/ppermute | solution.py:243
  13.9 4.2 %collective-permute-start.8 = (f32[32,256]{1,0:T(8,128)S(1)}, f32[32,256]{1,0:T(8,128)S(1)}, u32[]{:S(2)}, u32[]{:S(2)}) collective-permute-start(f32[32,256]{1,0:T(8,128)S(1)} %get-tuple-element.39), channel_id=1, source_target_pairs={{0,17},{1,16},{2,19},{3,18},{4,21},{5,20},{6,23},{7,22},{8,25},{9,... | collective-permute-start | bytes 98312 | tf_op jit(solution)/shard_map/ppermute | solution.py:243
  13.9 4.2 %collective-permute-start.9 = (f32[32,256]{1,0:T(8,128)S(1)}, f32[32,256]{1,0:T(8,128)S(1)}, u32[]{:S(2)}, u32[]{:S(2)}) collective-permute-start(f32[32,256]{1,0:T(8,128)S(1)} %get-tuple-element.40), channel_id=1, source_target_pairs={{0,9},{1,8},{2,11},{3,10},{4,13},{5,12},{6,15},{7,14},{8,1},{9,0},... | collective-permute-start | bytes 98312 | tf_op jit(solution)/shard_map/ppermute | solution.py:243

commit v6 on v5

--- a/solution.py
+++ b/solution.py
@@ -77,6 +77,10 @@
 
 def dot(left, right):
     return jnp.dot(left, right, preferred_element_type=jnp.float32)
+
+
+def inner(left, right):
+    return lax.dot_general(left, right, (((0,), (0,)), ((), ())), preferred_element_type=jnp.float32)
 
 
 def halves(value):
@@ -140,7 +144,7 @@
 
 
 def last_stage(received, table, total):
-    turned = lax.dot_general(received, table, (((0,), (0,)), ((), ())), preferred_element_type=jnp.float32)
+    turned = inner(received, table)
     by_cos, by_sin = turns(turned)
     group = turned.shape[0] // 2
     return (by_cos[:group] - by_sin[group:]) * (1.0 / total), (by_sin[:group] + by_cos[group:]) * (1.0 / total)
@@ -148,22 +152,15 @@
 
 def spread(slots, rows):
     count = len(slots)
-    lane = lax.broadcasted_iota(jnp.int32, slots[0].shape, 1)
-    lanes = slots[0].shape[1]
+    group = lax.broadcasted_iota(jnp.int32, slots[0].shape, 1) // rows
+    turned = [slots[0]] + [pltpu.roll(slots[s], s * rows, 1) for s in range(1, count)]
+    result = [turned[-d % count] for d in range(count)]
     bit = 1
     while bit < count:
-        step = rows * bit
-        keep = (lane // step) % 2 == 0
-        after = list(slots)
-        for low in range(count):
-            if low & bit:
-                continue
-            high = low | bit
-            after[low] = jnp.where(keep, slots[low], pltpu.roll(slots[high], step, 1))
-            after[high] = jnp.where(keep, pltpu.roll(slots[low], lanes - step, 1), slots[high])
-        slots = after
+        moved = (group // bit) % 2 == 1
+        result = [jnp.where(moved, result[d - bit], result[d]) for d in range(count)]
         bit *= 2
-    return slots
+    return result
 
 
 def prepare_kernel(
@@ -212,19 +209,29 @@
             out[start // rows + place] = piece.astype(jnp.bfloat16)
 
 
-def last_kernel(received, table, series, peak):
+def last_kernel(received, table, series, peak, held):
     templ_count, _, rows, side = series.shape
+    device = lax.axis_index("freq")
+    scale = 1.0 / (side * side)
     values = received[...]
+
+    def slot(which):
+        start = pl.multiple_of((which + device) % (2 * templ_count) * rows, rows)
+        return held[pl.ds(start, rows), :LANES], held[pl.ds(start, rows), LANES:]
+
     for start in range(0, side, LANES):
         columns = slice(start, start + LANES)
-        real_part, imag_part = last_stage(values, table[:, 2 * start : 2 * (start + LANES)], side * side)
-        power = real_part * real_part + imag_part * imag_part
-        best = power[:rows]
+        held[...] = inner(values, table[:, 2 * start : 2 * (start + LANES)])
+        best = None
         for templ in range(templ_count):
-            here = slice(templ * rows, (templ + 1) * rows)
-            series[templ, 0, :, columns] = real_part[here]
-            series[templ, 1, :, columns] = imag_part[here]
-            best = jnp.maximum(best, power[here])
+            real_cos, real_sin = slot(templ)
+            imag_cos, imag_sin = slot(templ_count + templ)
+            real_part = (real_cos - imag_sin) * scale
+            imag_part = (real_sin + imag_cos) * scale
+            series[templ, 0, :, columns] = real_part
+            series[templ, 1, :, columns] = imag_part
+            power = real_part * real_part + imag_part * imag_part
+            best = power if best is None else jnp.maximum(best, power)
         peak[:, columns] = best
 
 
@@ -234,7 +241,7 @@
     outer = device_count // (INNER * CORES)
     forwards, twists = (jnp.asarray(x) for x in device_tables(device_count, rows, side))
     table = jnp.asarray(transform_table(side))
-    tiles_fit = rows % 16 == 0 and 2 * templ_count * rows == 128 and side % 128 == 0
+    tiles_fit = rows % 16 == 0 and 2 * templ_count * rows == LANES and side % LANES == 0
     params = pltpu.CompilerParams(vmem_limit_bytes=VMEM_LIMIT)
     vmem = pl.BlockSpec(memory_space=pltpu.VMEM)
     hbm = pl.BlockSpec(memory_space=pltpu.HBM)
@@ -289,7 +296,7 @@
     if tiles_fit:
         outgoing = pl.pallas_call(
             section_kernel,
-            out_shape=jax.ShapeDtypeStruct((device_count, rows, 128), jnp.bfloat16),
+            out_shape=jax.ShapeDtypeStruct((device_count, rows, LANES), jnp.bfloat16),
             in_specs=[vmem] * (outer + 5),
             out_specs=vmem,
             compiler_params=params,
@@ -309,6 +316,7 @@
             ),
             in_specs=[vmem] * 2,
             out_specs=(vmem, vmem),
+            scratch_shapes=[pltpu.VMEM((LANES, 2 * LANES), jnp.float32)],
             compiler_params=params,
         )(received, table)
     else:

time: 31.1 us -> 30.9 us (level)
  no operation moved by 1% of the time
where the time goes in v6:
time: 30.9 us; the launch traced here: 30.8 us
  blocking collectives  11.2 us (36%)
  starting transfers between devices  10.5 us (34%)
  waiting for transfers between devices  4.77 us (15%)
  Pallas kernels  3.61 us (12%)
  between operations  0.69 us (2%)
    all_to_all x1, blocking collectives, local(): lax.all_to_all(outgoing, 'freq', 0, 0, tiled=True).reshape(side, -1)  11.2 us
    ppermute x10, starting transfers between devices, exchange(): lax.ppermute(value, 'freq', [(i, partner(i)) for i in range(device_count)])  10.5 us
    ppermute x10, waiting for transfers between devices, exchange(): lax.ppermute(value, 'freq', [(i, partner(i)) for i in range(device_count)])  4.77 us
    pallas_call x1, Pallas kernels, local(): pl.pallas_call(prepare_kernel, out_shape=results, in_specs=[hbm] * 6, out...  1.62 us
    pallas_call x1, Pallas kernels, local(): pl.pallas_call(last_kernel, out_shape=(jax.ShapeDtypeStruct((templ_count,...  1.07 us
  transfers between devices with their start and end apart: 10, of which 5 were waited for; matrix products, arithmetic and copies ran while one was open for 0% of the time, Pallas kernels for 5%

profile of v6, /device:TPU:0, one launch (start us, length us, event | category | flops | bytes accessed | tf_op | source)
XLA Modules:
  0.0 30.8 jit_solution(14895588424021056073)
XLA Ops:
  0.6 0.0 slice-start
  0.6 0.5 %collective-permute-start = (f32[16,512]{1,0:T(8,128)}, f32[16,512]{1,0:T(8,128)S(1)}, u32[]{:S(2)}, u32[]{:S(2)}) collective-permute-start(f32[16,512]{1,0:T(8,128)} %strain.1), channel_id=1, source_target_pairs={{0,1},{1,0},{2,3},{3,2},{4,5},{5,4},{6,7},{7,6},{8,9},{9,8},{10,11... | collective-permute-start | bytes 98312 | tf_op jit(solution)/shard_map/ppermute | solution.py:250
  1.2 3.6 %collective-permute-start.3 = (f32[16,512]{1,0:T(8,128)}, f32[16,512]{1,0:T(8,128)S(1)}, u32[]{:S(2)}, u32[]{:S(2)}) collective-permute-start(f32[16,512]{1,0:T(8,128)} %strain.1), channel_id=1, source_target_pairs={{0,7},{1,6},{2,5},{3,4},{4,3},{5,2},{6,1},{7,0},{8,15},{9,14},{10,... | collective-permute-start | bytes 98312 | tf_op jit(solution)/shard_map/ppermute | solution.py:250
  4.7 0.2 collective-permute-start.1
  4.9 0.0 collective-permute-done.refs_1_
  4.9 1.5 %collective-permute-start.2 = (f32[16,512]{1,0:T(8,128)S(1)}, f32[16,512]{1,0:T(8,128)S(1)}, u32[]{:S(2)}, u32[]{:S(2)}) collective-permute-start(f32[16,512]{1,0:T(8,128)S(1)} %collective-permute-done.refs_1_), channel_id=1, source_target_pairs={{0,3},{1,4},{2,7},{3,0},{4,1},{5,6},{6,5},{7,2},{8,11},{9,12},{10,... | collective-permute-start | bytes 98312 | tf_op jit(solution)/shard_map/ppermute | solution.py:250
  6.5 1.6 %shard_map.86 = (bf16[256,128]{1,0:T(8,128)(2,1)S(1)}, f32[2,64,512]{2,1,0:T(8,128)S(1)}, bf16[512,1536]{1,0:T(8,128)(2,1)S(1)}, f32[16,512]{1,0:T(8,128)S(1)}, ...) custom-call(bf16[32,256,128]{2,1,0:T(8,128)(2,1)} %constant.6.clone.forwards, f32[32,2,64,512]{3,2,1,0:T(8,128)} %constant.7.clone.twists, ...), custom_call_target="tpu_custom_call" | custom-call | bytes 3145728 | tf_op jit(solution)/shard_map/pallas_call | solution.py:266
  8.1 0.0 collective-permute-done.3.refs_4_
  8.1 0.1 collective-permute-start.6
  8.2 0.0 collective-permute-done.1.refs_2_
  8.3 0.4 %collective-permute-start.4 = (f32[16,512]{1,0:T(8,128)S(1)}, f32[16,512]{1,0:T(8,128)S(1)}, u32[]{:S(2)}, u32[]{:S(2)}) collective-permute-start(f32[16,512]{1,0:T(8,128)S(1)} %collective-permute-done.1.refs_2_), channel_id=1, source_target_pairs={{0,1},{1,0},{2,3},{3,2},{4,5},{5,4},{6,7},{7,6},{8,9},{9,8},{10,11... | collective-permute-start | bytes 98312 | tf_op jit(solution)/shard_map/ppermute | solution.py:250
  8.7 0.1 collective-permute-start.5
  8.8 0.6 %collective-permute-done.6.refs_7_ = f32[16,512]{1,0:T(8,128)S(1)} collective-permute-done((f32[16,512]{1,0:T(8,128)S(1)}, f32[16,512]{1,0:T(8,128)S(1)}, u32[]{:S(2)}, u32[]{:S(2)}) %collective-permute-start.6) | collective-permute-done | bytes 32800 | tf_op jit(solution)/shard_map/ppermute | solution.py:250
  9.4 0.2 collective-permute-done.4.refs_5_
  9.6 0.4 %collective-permute-done.5.refs_6_ = f32[16,512]{1,0:T(8,128)S(1)} collective-permute-done((f32[16,512]{1,0:T(8,128)S(1)}, f32[16,512]{1,0:T(8,128)S(1)}, u32[]{:S(2)}, u32[]{:S(2)}) %collective-permute-start.5) | collective-permute-done | bytes 32800 | tf_op jit(solution)/shard_map/ppermute | solution.py:250
  9.9 0.6 %shard_map.87 = (f32[32,256]{1,0:T(8,128)S(1)}, f32[32,256]{1,0:T(8,128)S(1)}, f32[32,256]{1,0:T(8,128)S(1)}, f32[32,256]{1,0:T(8,128)S(1)}) custom-call(f32[16,512]{1,0:T(8,128)S(1)} %get-tuple-element.23.refs_0_, f32[16,512]{1,0:T(8,128)S(1)} %collective-permute-done.refs_1_, f32[16,512]{1,0:T(8,128)S(1)} %collective-permute-done.1.refs_2_, ...), custom_call_target="tpu_custom_call" | custom-call | tf_op jit(solution)/shard_map/pallas_call | solution.py:283
  10.5 3.4 %collective-permute-start.7 = (f32[32,256]{1,0:T(8,128)S(1)}, f32[32,256]{1,0:T(8,128)S(1)}, u32[]{:S(2)}, u32[]{:S(2)}) collective-permute-start(f32[32,256]{1,0:T(8,128)S(1)} %get-tuple-element.38), channel_id=1, source_target_pairs={{0,25},{1,24},{2,27},{3,26},{4,29},{5,28},{6,31},{7,30},{8,17},{9,... | collective-permute-start | bytes 98312 | tf_op jit(solution)/shard_map/ppermute | solution.py:250
  13.9 0.0 collective-permute-start.8
  13.9 0.6 %collective-permute-start.9 = (f32[32,256]{1,0:T(8,128)S(1)}, f32[32,256]{1,0:T(8,128)S(1)}, u32[]{:S(2)}, u32[]{:S(2)}) collective-permute-start(f32[32,256]{1,0:T(8,128)S(1)} %get-tuple-element.40), channel_id=1, source_target_pairs={{0,9},{1,8},{2,11},{3,10},{4,13},{5,12},{6,15},{7,14},{8,1},{9,0},... | collective-permute-start | bytes 98312 | tf_op jit(solution)/shard_map/ppermute | solution.py:250
  14.5 1.2 %collective-permute-done.7.refs_1_ = f32[32,256]{1,0:T(8,128)S(1)} collective-permute-done((f32[32,256]{1,0:T(8,128)S(1)}, f32[32,256]{1,0:T(8,128)S(1)}, u32[]{:S(2)}, u32[]{:S(2)}) %collective-permute-start.7) | collective-permute-done | bytes 32800 | tf_op jit(solution)/shard_map/ppermute | solution.py:250
  15.7 2.5 %collective-permute-done.8.refs_2_ = f32[32,256]{1,0:T(8,128)S(1)} collective-permute-done((f32[32,256]{1,0:T(8,128)S(1)}, f32[32,256]{1,0:T(8,128)S(1)}, u32[]{:S(2)}, u32[]{:S(2)}) %collective-permute-start.8) | collective-permute-done | bytes 32800 | tf_op jit(solution)/shard_map/ppermute | solution.py:250
  18.2 0.3 %shard_map.88 = bf16[32,16,128]{2,1,0:T(8,128)(2,1)S(1)} custom-call(f32[32,256]{1,0:T(8,128)S(1)} %get-tuple-element.37.refs_0_, f32[32,256]{1,0:T(8,128)S(1)} %collective-permute-done.7.refs_1_, f32[32,256]{1,0:T(8,128)S(1)} %collective-permute-done.8.refs_2_, f32[32,256]{1,0:T(8,128)S(1)} %collective-permute-done.9.refs_3_, ...), custom_call_target="tpu_custom_call" | custom-call | tf_op jit(solution)/shard_map/pallas_call | solution.py:297
  18.5 11.2 %all_to_all.5 = bf16[32,16,128]{2,1,0:T(8,128)(2,1)S(1)} all-to-all(bf16[32,16,128]{2,1,0:T(8,128)(2,1)S(1)} %shard_map.88), channel_id=1, replica_groups=mesh['tmpl'=1,'freq'=32] {'freq'}, dimensions={0} | all-to-all | bytes 262144 | tf_op jit(solution)/shard_map/all_to_all | solution.py:309
  29.7 1.1 %shard_map.89 = (f32[4,2,16,512]{3,2,1,0:T(8,128)}, f32[16,512]{1,0:T(8,128)}) custom-call(bf16[512,128]{1,0:T(8,128)(2,1)S(1)} %bitcast.4, bf16[512,1536]{1,0:T(8,128)(2,1)S(1)} %get-tuple-element.32.refs_10_.refs_8_.table), custom_call_target="tpu_custom_call" | custom-call | tf_op jit(solution)/shard_map/pallas_call | solution.py:311
  (4 shorter events, 0.0 us)
Async XLA Ops:
  0.6 8.2 %slice-start = ((bf16[16,4,2,512]{3,2,1,0:T(2,128)(2,1)}), bf16[16,4,2,256]{3,2,1,0:T(2,128)(2,1)S(1)}, s32[]{:S(2)}) async-start(bf16[16,4,2,512]{3,2,1,0:T(2,128)(2,1)} %param.9), calls=%async_computation.1 | async-start | bytes 131072 | tf_op jit(solution)/shard_map/slice | solution.py:279
  0.6 4.3 %collective-permute-start = (f32[16,512]{1,0:T(8,128)}, f32[16,512]{1,0:T(8,128)S(1)}, u32[]{:S(2)}, u32[]{:S(2)}) collective-permute-start(f32[16,512]{1,0:T(8,128)} %strain.1), channel_id=1, source_target_pairs={{0,1},{1,0},{2,3},{3,2},{4,5},{5,4},{6,7},{7,6},{8,9},{9,8},{10,11... | collective-permute-start | bytes 98312 | tf_op jit(solution)/shard_map/ppermute | solution.py:250
  1.2 6.9 %collective-permute-start.3 = (f32[16,512]{1,0:T(8,128)}, f32[16,512]{1,0:T(8,128)S(1)}, u32[]{:S(2)}, u32[]{:S(2)}) collective-permute-start(f32[16,512]{1,0:T(8,128)} %strain.1), channel_id=1, source_target_pairs={{0,7},{1,6},{2,5},{3,4},{4,3},{5,2},{6,1},{7,0},{8,15},{9,14},{10,... | collective-permute-start | bytes 98312 | tf_op jit(solution)/shard_map/ppermute | solution.py:250
  4.7 3.6 %collective-permute-start.1 = (f32[16,512]{1,0:T(8,128)}, f32[16,512]{1,0:T(8,128)S(1)}, u32[]{:S(2)}, u32[]{:S(2)}) collective-permute-start(f32[16,512]{1,0:T(8,128)} %strain.1), channel_id=1, source_target_pairs={{0,3},{1,4},{2,7},{3,0},{4,1},{5,6},{6,5},{7,2},{8,11},{9,12},{10,... | collective-permute-start | bytes 98312 | tf_op jit(solution)/shard_map/ppermute | solution.py:250
  4.9 3.8 %collective-permute-start.2 = (f32[16,512]{1,0:T(8,128)S(1)}, f32[16,512]{1,0:T(8,128)S(1)}, u32[]{:S(2)}, u32[]{:S(2)}) collective-permute-start(f32[16,512]{1,0:T(8,128)S(1)} %collective-permute-done.refs_1_), channel_id=1, source_target_pairs={{0,3},{1,4},{2,7},{3,0},{4,1},{5,6},{6,5},{7,2},{8,11},{9,12},{10,... | collective-permute-start | bytes 98312 | tf_op jit(solution)/shard_map/ppermute | solution.py:250
  8.1 1.3 %collective-permute-start.6 = (f32[16,512]{1,0:T(8,128)S(1)}, f32[16,512]{1,0:T(8,128)S(1)}, u32[]{:S(2)}, u32[]{:S(2)}) collective-permute-start(f32[16,512]{1,0:T(8,128)S(1)} %collective-permute-done.3.refs_4_), channel_id=1, source_target_pairs={{0,1},{1,0},{2,3},{3,2},{4,5},{5,4},{6,7},{7,6},{8,9},{9,8},{10,11... | collective-permute-start | bytes 98312 | tf_op jit(solution)/shard_map/ppermute | solution.py:250
  8.3 1.3 %collective-permute-start.4 = (f32[16,512]{1,0:T(8,128)S(1)}, f32[16,512]{1,0:T(8,128)S(1)}, u32[]{:S(2)}, u32[]{:S(2)}) collective-permute-start(f32[16,512]{1,0:T(8,128)S(1)} %collective-permute-done.1.refs_2_), channel_id=1, source_target_pairs={{0,1},{1,0},{2,3},{3,2},{4,5},{5,4},{6,7},{7,6},{8,9},{9,8},{10,11... | collective-permute-start | bytes 98312 | tf_op jit(solution)/shard_map/ppermute | solution.py:250
  8.7 1.2 %collective-permute-start.5 = (f32[16,512]{1,0:T(8,128)S(1)}, f32[16,512]{1,0:T(8,128)S(1)}, u32[]{:S(2)}, u32[]{:S(2)}) collective-permute-start(f32[16,512]{1,0:T(8,128)S(1)} %collective-permute-done.2.refs_3_), channel_id=1, source_target_pairs={{0,1},{1,0},{2,3},{3,2},{4,5},{5,4},{6,7},{7,6},{8,9},{9,8},{10,11... | collective-permute-start | bytes 98312 | tf_op jit(solution)/shard_map/ppermute | solution.py:250
  10.5 5.2 %collective-permute-start.7 = (f32[32,256]{1,0:T(8,128)S(1)}, f32[32,256]{1,0:T(8,128)S(1)}, u32[]{:S(2)}, u32[]{:S(2)}) collective-permute-start(f32[32,256]{1,0:T(8,128)S(1)} %get-tuple-element.38), channel_id=1, source_target_pairs={{0,25},{1,24},{2,27},{3,26},{4,29},{5,28},{6,31},{7,30},{8,17},{9,... | collective-permute-start | bytes 98312 | tf_op jit(solution)/shard_map/ppermute | solution.py:250
  13.9 4.2 %collective-permute-start.8 = (f32[32,256]{1,0:T(8,128)S(1)}, f32[32,256]{1,0:T(8,128)S(1)}, u32[]{:S(2)}, u32[]{:S(2)}) collective-permute-start(f32[32,256]{1,0:T(8,128)S(1)} %get-tuple-element.39), channel_id=1, source_target_pairs={{0,17},{1,16},{2,19},{3,18},{4,21},{5,20},{6,23},{7,22},{8,25},{9,... | collective-permute-start | bytes 98312 | tf_op jit(solution)/shard_map/ppermute | solution.py:250
  13.9 4.2 %collective-permute-start.9 = (f32[32,256]{1,0:T(8,128)S(1)}, f32[32,256]{1,0:T(8,128)S(1)}, u32[]{:S(2)}, u32[]{:S(2)}) collective-permute-start(f32[32,256]{1,0:T(8,128)S(1)} %get-tuple-element.40), channel_id=1, source_target_pairs={{0,9},{1,8},{2,11},{3,10},{4,13},{5,12},{6,15},{7,14},{8,1},{9,0},... | collective-permute-start | bytes 98312 | tf_op jit(solution)/shard_map/ppermute | solution.py:250

commit v7 on v6

--- a/solution.py
+++ b/solution.py
@@ -111,7 +111,7 @@
 
 def products(parts, asd, keep, spectra):
     templ_count, _, rows, _ = spectra.shape
-    white = functools.reduce(jnp.add, parts)
+    white = functools.reduce(jnp.add, [part.astype(jnp.float32) for part in parts])
     white_real, white_imag = white[:rows] * asd, white[rows:] * asd
     result = []
     for part in range(2):
@@ -192,8 +192,8 @@
     real, imag = partial_spectrum([block[...] for block in blocks], forward[...], twist, table)
     rows = outs[0].shape[0] // 2
     for m, out in enumerate(outs):
-        out[:rows] = real[m * rows : (m + 1) * rows]
-        out[rows:] = imag[m * rows : (m + 1) * rows]
+        out[:rows] = real[m * rows : (m + 1) * rows].astype(out.dtype)
+        out[rows:] = imag[m * rows : (m + 1) * rows].astype(out.dtype)
 
 
 def section_kernel(*refs):
@@ -242,6 +242,7 @@
     forwards, twists = (jnp.asarray(x) for x in device_tables(device_count, rows, side))
     table = jnp.asarray(transform_table(side))
     tiles_fit = rows % 16 == 0 and 2 * templ_count * rows == LANES and side % LANES == 0
+    sent_as = [jnp.float32 if step < 1 else jnp.bfloat16 for step in range(outer)]
     params = pltpu.CompilerParams(vmem_limit_bytes=VMEM_LIMIT)
     vmem = pl.BlockSpec(memory_space=pltpu.VMEM)
     hbm = pl.BlockSpec(memory_space=pltpu.HBM)
@@ -282,14 +283,16 @@
     if tiles_fit:
         parts = pl.pallas_call(
             spectrum_kernel,
-            out_shape=[jax.ShapeDtypeStruct((2 * rows, BAND), jnp.float32)] * outer,
+            out_shape=[jax.ShapeDtypeStruct((2 * rows, BAND), sent) for sent in sent_as],
             in_specs=[vmem] * (len(blocks) + 3),
             out_specs=[vmem] * outer,
             compiler_params=params,
         )(*blocks, forward, twist, table)
     else:
         real, imag = partial_spectrum(blocks, forward, twist, table)
-        parts = [jnp.concatenate([x[m * rows : (m + 1) * rows] for x in (real, imag)], 0) for m in range(outer)]
+        parts = [
+            jnp.concatenate([x[m * rows : (m + 1) * rows] for x in (real, imag)], 0).astype(sent_as[m]) for m in range(outer)
+        ]
     parts, by_templ = lax.optimization_barrier((list(parts), by_templ))
     received = [exchange(parts[step], functools.partial(line, step=step)) for step in reversed(range(1, outer))]
     parts = parts[:1] + received

time: 30.9 us -> 30.6 us (level)
  no operation moved by 1% of the time
where the time goes in v7:
time: 30.6 us; the launch traced here: 30.4 us
  blocking collectives  11 us (36%)
  starting transfers between devices  10.5 us (34%)
  waiting for transfers between devices  4.6 us (15%)
  Pallas kernels  3.62 us (12%)
  between operations  0.69 us (2%)
    all_to_all x1, blocking collectives, local(): lax.all_to_all(outgoing, 'freq', 0, 0, tiled=True).reshape(side, -1)  11 us
    ppermute x10, starting transfers between devices, exchange(): lax.ppermute(value, 'freq', [(i, partner(i)) for i in range(device_count)])  10.5 us
    ppermute x10, waiting for transfers between devices, exchange(): lax.ppermute(value, 'freq', [(i, partner(i)) for i in range(device_count)])  4.6 us
    pallas_call x1, Pallas kernels, local(): pl.pallas_call(prepare_kernel, out_shape=results, in_specs=[hbm] * 6, out...  1.62 us
    pallas_call x1, Pallas kernels, local(): pl.pallas_call(last_kernel, out_shape=(jax.ShapeDtypeStruct((templ_count,...  1.07 us
  transfers between devices with their start and end apart: 10, of which 5 were waited for; matrix products, arithmetic and copies ran while one was open for 0% of the time, Pallas kernels for 5%

profile of v7, /device:TPU:0, one launch (start us, length us, event | category | flops | bytes accessed | tf_op | source)
XLA Modules:
  0.0 30.4 jit_solution(18348140029902680880)
XLA Ops:
  0.6 0.0 slice-start
  0.6 0.5 %collective-permute-start = (f32[16,512]{1,0:T(8,128)}, f32[16,512]{1,0:T(8,128)S(1)}, u32[]{:S(2)}, u32[]{:S(2)}) collective-permute-start(f32[16,512]{1,0:T(8,128)} %strain.1), channel_id=1, source_target_pairs={{0,1},{1,0},{2,3},{3,2},{4,5},{5,4},{6,7},{7,6},{8,9},{9,8},{10,11... | collective-permute-start | bytes 98312 | tf_op jit(solution)/shard_map/ppermute | solution.py:251
  1.2 3.6 %collective-permute-start.3 = (f32[16,512]{1,0:T(8,128)}, f32[16,512]{1,0:T(8,128)S(1)}, u32[]{:S(2)}, u32[]{:S(2)}) collective-permute-start(f32[16,512]{1,0:T(8,128)} %strain.1), channel_id=1, source_target_pairs={{0,7},{1,6},{2,5},{3,4},{4,3},{5,2},{6,1},{7,0},{8,15},{9,14},{10,... | collective-permute-start | bytes 98312 | tf_op jit(solution)/shard_map/ppermute | solution.py:251
  4.7 0.2 collective-permute-start.1
  4.9 0.0 collective-permute-done.refs_1_
  4.9 1.5 %collective-permute-start.2 = (f32[16,512]{1,0:T(8,128)S(1)}, f32[16,512]{1,0:T(8,128)S(1)}, u32[]{:S(2)}, u32[]{:S(2)}) collective-permute-start(f32[16,512]{1,0:T(8,128)S(1)} %collective-permute-done.refs_1_), channel_id=1, source_target_pairs={{0,3},{1,4},{2,7},{3,0},{4,1},{5,6},{6,5},{7,2},{8,11},{9,12},{10,... | collective-permute-start | bytes 98312 | tf_op jit(solution)/shard_map/ppermute | solution.py:251
  6.5 1.6 %shard_map.86 = (bf16[256,128]{1,0:T(8,128)(2,1)S(1)}, f32[2,64,512]{2,1,0:T(8,128)S(1)}, bf16[512,1536]{1,0:T(8,128)(2,1)S(1)}, f32[16,512]{1,0:T(8,128)S(1)}, ...) custom-call(bf16[32,256,128]{2,1,0:T(8,128)(2,1)} %constant.6.clone.forwards, f32[32,2,64,512]{3,2,1,0:T(8,128)} %constant.7.clone.twists, ...), custom_call_target="tpu_custom_call" | custom-call | bytes 3145728 | tf_op jit(solution)/shard_map/pallas_call | solution.py:267
  8.1 0.0 collective-permute-done.3.refs_4_
  8.1 0.1 collective-permute-start.6
  8.2 0.0 collective-permute-done.1.refs_2_
  8.3 0.4 %collective-permute-start.4 = (f32[16,512]{1,0:T(8,128)S(1)}, f32[16,512]{1,0:T(8,128)S(1)}, u32[]{:S(2)}, u32[]{:S(2)}) collective-permute-start(f32[16,512]{1,0:T(8,128)S(1)} %collective-permute-done.1.refs_2_), channel_id=1, source_target_pairs={{0,1},{1,0},{2,3},{3,2},{4,5},{5,4},{6,7},{7,6},{8,9},{9,8},{10,11... | collective-permute-start | bytes 98312 | tf_op jit(solution)/shard_map/ppermute | solution.py:251
  8.7 0.0 collective-permute-done.2.refs_3_
  8.7 0.1 collective-permute-start.5
  8.8 0.6 %collective-permute-done.6.refs_7_ = f32[16,512]{1,0:T(8,128)S(1)} collective-permute-done((f32[16,512]{1,0:T(8,128)S(1)}, f32[16,512]{1,0:T(8,128)S(1)}, u32[]{:S(2)}, u32[]{:S(2)}) %collective-permute-start.6) | collective-permute-done | bytes 32800 | tf_op jit(solution)/shard_map/ppermute | solution.py:251
  9.4 0.2 collective-permute-done.4.refs_5_
  9.6 0.4 %collective-permute-done.5.refs_6_ = f32[16,512]{1,0:T(8,128)S(1)} collective-permute-done((f32[16,512]{1,0:T(8,128)S(1)}, f32[16,512]{1,0:T(8,128)S(1)}, u32[]{:S(2)}, u32[]{:S(2)}) %collective-permute-start.5) | collective-permute-done | bytes 32800 | tf_op jit(solution)/shard_map/ppermute | solution.py:251
  9.9 0.6 %shard_map.87 = (f32[32,256]{1,0:T(8,128)S(1)}, bf16[32,256]{1,0:T(8,128)(2,1)S(1)}, bf16[32,256]{1,0:T(8,128)(2,1)S(1)}, bf16[32,256]{1,0:T(8,128)(2,1)S(1)}) custom-call(f32[16,512]{1,0:T(8,128)S(1)} %get-tuple-element.23.refs_0_, f32[16,512]{1,0:T(8,128)S(1)} %collective-permute-done.refs_1_, f32[16,512]{1,0:T(8,128)S(1)} %collective-permute-done.1.refs_2_, ...), custom_call_target="tpu_custom_call" | custom-call | tf_op jit(solution)/shard_map/pallas_call | solution.py:284
  10.5 3.4 %collective-permute-start.7 = (bf16[32,256]{1,0:T(8,128)(2,1)S(1)}, bf16[32,256]{1,0:T(8,128)(2,1)S(1)}, u32[]{:S(2)}, u32[]{:S(2)}) collective-permute-start(bf16[32,256]{1,0:T(8,128)(2,1)S(1)} %get-tuple-element.38), channel_id=1, source_target_pairs={{0,25},{1,24},{2,27},{3,26},{4,29},{5,28},{6,31},{7,30},{8,17},{9,... | collective-permute-start | bytes 49160 | tf_op jit(solution)/shard_map/ppermute | solution.py:251
  13.9 0.6 %collective-permute-start.9 = (bf16[32,256]{1,0:T(8,128)(2,1)S(1)}, bf16[32,256]{1,0:T(8,128)(2,1)S(1)}, u32[]{:S(2)}, u32[]{:S(2)}) collective-permute-start(bf16[32,256]{1,0:T(8,128)(2,1)S(1)} %get-tuple-element.40), channel_id=1, source_target_pairs={{0,9},{1,8},{2,11},{3,10},{4,13},{5,12},{6,15},{7,14},{8,1},{9,0},... | collective-permute-start | bytes 49160 | tf_op jit(solution)/shard_map/ppermute | solution.py:251
  14.5 1.0 %collective-permute-done.7.refs_1_ = bf16[32,256]{1,0:T(8,128)(2,1)S(1)} collective-permute-done((bf16[32,256]{1,0:T(8,128)(2,1)S(1)}, bf16[32,256]{1,0:T(8,128)(2,1)S(1)}, u32[]{:S(2)}, u32[]{:S(2)}) %collective-permute-start.7) | collective-permute-done | bytes 16416 | tf_op jit(solution)/shard_map/ppermute | solution.py:251
  15.5 2.5 %collective-permute-done.8.refs_2_ = bf16[32,256]{1,0:T(8,128)(2,1)S(1)} collective-permute-done((bf16[32,256]{1,0:T(8,128)(2,1)S(1)}, bf16[32,256]{1,0:T(8,128)(2,1)S(1)}, u32[]{:S(2)}, u32[]{:S(2)}) %collective-permute-start.8) | collective-permute-done | bytes 16416 | tf_op jit(solution)/shard_map/ppermute | solution.py:251
  18.0 0.3 %shard_map.88 = bf16[32,16,128]{2,1,0:T(8,128)(2,1)S(1)} custom-call(f32[32,256]{1,0:T(8,128)S(1)} %get-tuple-element.37.refs_0_, bf16[32,256]{1,0:T(8,128)(2,1)S(1)} %collective-permute-done.7.refs_1_, bf16[32,256]{1,0:T(8,128)(2,1)S(1)} %collective-permute-done.8.refs_2_, bf16[32,256]{1,0:T(8,128)(2,1)S(1)} %collective-permute-done.9.refs_3_, ...), custom_call_target="tpu_custom_call" | custom-call | tf_op jit(solution)/shard_map/pallas_call | solution.py:300
  18.3 11.0 %all_to_all.5 = bf16[32,16,128]{2,1,0:T(8,128)(2,1)S(1)} all-to-all(bf16[32,16,128]{2,1,0:T(8,128)(2,1)S(1)} %shard_map.88), channel_id=1, replica_groups=mesh['tmpl'=1,'freq'=32] {'freq'}, dimensions={0} | all-to-all | bytes 262144 | tf_op jit(solution)/shard_map/all_to_all | solution.py:312
  29.3 1.1 %shard_map.89 = (f32[4,2,16,512]{3,2,1,0:T(8,128)}, f32[16,512]{1,0:T(8,128)}) custom-call(bf16[512,128]{1,0:T(8,128)(2,1)S(1)} %bitcast.4, bf16[512,1536]{1,0:T(8,128)(2,1)S(1)} %get-tuple-element.32.refs_10_.refs_8_.table), custom_call_target="tpu_custom_call" | custom-call | tf_op jit(solution)/shard_map/pallas_call | solution.py:314
  (4 shorter events, 0.0 us)
Async XLA Ops:
  0.6 8.2 %slice-start = ((bf16[16,4,2,512]{3,2,1,0:T(2,128)(2,1)}), bf16[16,4,2,256]{3,2,1,0:T(2,128)(2,1)S(1)}, s32[]{:S(2)}) async-start(bf16[16,4,2,512]{3,2,1,0:T(2,128)(2,1)} %param.9), calls=%async_computation.1 | async-start | bytes 131072 | tf_op jit(solution)/shard_map/slice | solution.py:280
  0.6 4.3 %collective-permute-start = (f32[16,512]{1,0:T(8,128)}, f32[16,512]{1,0:T(8,128)S(1)}, u32[]{:S(2)}, u32[]{:S(2)}) collective-permute-start(f32[16,512]{1,0:T(8,128)} %strain.1), channel_id=1, source_target_pairs={{0,1},{1,0},{2,3},{3,2},{4,5},{5,4},{6,7},{7,6},{8,9},{9,8},{10,11... | collective-permute-start | bytes 98312 | tf_op jit(solution)/shard_map/ppermute | solution.py:251
  1.2 6.9 %collective-permute-start.3 = (f32[16,512]{1,0:T(8,128)}, f32[16,512]{1,0:T(8,128)S(1)}, u32[]{:S(2)}, u32[]{:S(2)}) collective-permute-start(f32[16,512]{1,0:T(8,128)} %strain.1), channel_id=1, source_target_pairs={{0,7},{1,6},{2,5},{3,4},{4,3},{5,2},{6,1},{7,0},{8,15},{9,14},{10,... | collective-permute-start | bytes 98312 | tf_op jit(solution)/shard_map/ppermute | solution.py:251
  4.7 3.6 %collective-permute-start.1 = (f32[16,512]{1,0:T(8,128)}, f32[16,512]{1,0:T(8,128)S(1)}, u32[]{:S(2)}, u32[]{:S(2)}) collective-permute-start(f32[16,512]{1,0:T(8,128)} %strain.1), channel_id=1, source_target_pairs={{0,3},{1,4},{2,7},{3,0},{4,1},{5,6},{6,5},{7,2},{8,11},{9,12},{10,... | collective-permute-start | bytes 98312 | tf_op jit(solution)/shard_map/ppermute | solution.py:251
  4.9 3.8 %collective-permute-start.2 = (f32[16,512]{1,0:T(8,128)S(1)}, f32[16,512]{1,0:T(8,128)S(1)}, u32[]{:S(2)}, u32[]{:S(2)}) collective-permute-start(f32[16,512]{1,0:T(8,128)S(1)} %collective-permute-done.refs_1_), channel_id=1, source_target_pairs={{0,3},{1,4},{2,7},{3,0},{4,1},{5,6},{6,5},{7,2},{8,11},{9,12},{10,... | collective-permute-start | bytes 98312 | tf_op jit(solution)/shard_map/ppermute | solution.py:251
  8.1 1.3 %collective-permute-start.6 = (f32[16,512]{1,0:T(8,128)S(1)}, f32[16,512]{1,0:T(8,128)S(1)}, u32[]{:S(2)}, u32[]{:S(2)}) collective-permute-start(f32[16,512]{1,0:T(8,128)S(1)} %collective-permute-done.3.refs_4_), channel_id=1, source_target_pairs={{0,1},{1,0},{2,3},{3,2},{4,5},{5,4},{6,7},{7,6},{8,9},{9,8},{10,11... | collective-permute-start | bytes 98312 | tf_op jit(solution)/shard_map/ppermute | solution.py:251
  8.3 1.3 %collective-permute-start.4 = (f32[16,512]{1,0:T(8,128)S(1)}, f32[16,512]{1,0:T(8,128)S(1)}, u32[]{:S(2)}, u32[]{:S(2)}) collective-permute-start(f32[16,512]{1,0:T(8,128)S(1)} %collective-permute-done.1.refs_2_), channel_id=1, source_target_pairs={{0,1},{1,0},{2,3},{3,2},{4,5},{5,4},{6,7},{7,6},{8,9},{9,8},{10,11... | collective-permute-start | bytes 98312 | tf_op jit(solution)/shard_map/ppermute | solution.py:251
  8.7 1.2 %collective-permute-start.5 = (f32[16,512]{1,0:T(8,128)S(1)}, f32[16,512]{1,0:T(8,128)S(1)}, u32[]{:S(2)}, u32[]{:S(2)}) collective-permute-start(f32[16,512]{1,0:T(8,128)S(1)} %collective-permute-done.2.refs_3_), channel_id=1, source_target_pairs={{0,1},{1,0},{2,3},{3,2},{4,5},{5,4},{6,7},{7,6},{8,9},{9,8},{10,11... | collective-permute-start | bytes 98312 | tf_op jit(solution)/shard_map/ppermute | solution.py:251
  10.5 5.0 %collective-permute-start.7 = (bf16[32,256]{1,0:T(8,128)(2,1)S(1)}, bf16[32,256]{1,0:T(8,128)(2,1)S(1)}, u32[]{:S(2)}, u32[]{:S(2)}) collective-permute-start(bf16[32,256]{1,0:T(8,128)(2,1)S(1)} %get-tuple-element.38), channel_id=1, source_target_pairs={{0,25},{1,24},{2,27},{3,26},{4,29},{5,28},{6,31},{7,30},{8,17},{9,... | collective-permute-start | bytes 49160 | tf_op jit(solution)/shard_map/ppermute | solution.py:251
  13.9 4.1 %collective-permute-start.8 = (bf16[32,256]{1,0:T(8,128)(2,1)S(1)}, bf16[32,256]{1,0:T(8,128)(2,1)S(1)}, u32[]{:S(2)}, u32[]{:S(2)}) collective-permute-start(bf16[32,256]{1,0:T(8,128)(2,1)S(1)} %get-tuple-element.39), channel_id=1, source_target_pairs={{0,17},{1,16},{2,19},{3,18},{4,21},{5,20},{6,23},{7,22},{8,25},{9,... | collective-permute-start | bytes 49160 | tf_op jit(solution)/shard_map/ppermute | solution.py:251
  13.9 4.1 %collective-permute-start.9 = (bf16[32,256]{1,0:T(8,128)(2,1)S(1)}, bf16[32,256]{1,0:T(8,128)(2,1)S(1)}, u32[]{:S(2)}, u32[]{:S(2)}) collective-permute-start(bf16[32,256]{1,0:T(8,128)(2,1)S(1)} %get-tuple-element.40), channel_id=1, source_target_pairs={{0,9},{1,8},{2,11},{3,10},{4,13},{5,12},{6,15},{7,14},{8,1},{9,0},... | collective-permute-start | bytes 49160 | tf_op jit(solution)/shard_map/ppermute | solution.py:251

commit v8 on v7

--- a/solution.py
+++ b/solution.py
@@ -164,7 +164,7 @@
 
 
 def prepare_kernel(
-    forwards, twists, table, strain, inv_asd, cutoff, forward, twist, table_out, strain_out, asd, keep, limits, arrived
+    forwards, twists, strain, inv_asd, cutoff, forward, twist, strain_out, asd, keep, limits, arrived
 ):
     device = lax.axis_index("freq")
     moves = (
@@ -173,7 +173,6 @@
         (forwards.at[device], forward),
         (twists.at[device], twist),
         (inv_asd.at[:, :BAND], asd),
-        (table, table_out),
     )
     copies = [pltpu.make_async_copy(source, target, arrived.at[i]) for i, (source, target) in enumerate(moves)]
     for copy in copies:
@@ -258,18 +257,17 @@
         results = [
             pltpu.VMEM(forwards.shape[1:], jnp.bfloat16),
             pltpu.VMEM(twists.shape[1:], jnp.float32),
-            pltpu.VMEM(table.shape, jnp.bfloat16),
             pltpu.VMEM(strain.shape, jnp.float32),
             pltpu.VMEM((rows, BAND), jnp.float32),
             pltpu.VMEM((templ_count, BAND), jnp.float32),
         ]
-        sources = (forwards, twists, table, strain, inv_asd, cutoff)
-        forward, twist, table, mine, asd, keep = pl.pallas_call(
+        sources = (forwards, twists, strain, inv_asd, cutoff)
+        forward, twist, mine, asd, keep = pl.pallas_call(
             prepare_kernel,
             out_shape=results,
-            in_specs=[hbm] * 6,
-            out_specs=[vmem] * 6,
-            scratch_shapes=[pltpu.SMEM(cutoff.shape, jnp.int32), pltpu.SemaphoreType.DMA((6,))],
+            in_specs=[hbm] * 5,
+            out_specs=[vmem] * 5,
+            scratch_shapes=[pltpu.SMEM(cutoff.shape, jnp.int32), pltpu.SemaphoreType.DMA((5,))],
             compiler_params=params,
             cost_estimate=pl.CostEstimate(flops=0, bytes_accessed=4 * table.size, transcendentals=0),
         )(*[pltpu.with_memory_space_constraint(source, pltpu.HBM) for source in sources])

time: 30.6 us -> 30.6 us (level)
  Pallas kernels: 3.62 us -> 3.04 us
  waiting for transfers between devices: 4.6 us -> 5.11 us
    pallas_call x1, Pallas kernels: 1.62 us -> 1.05 us  [local(): pl.pallas_call(prepare_kernel, out_shape=results, in_specs=[hbm] * 5, out...]
    ppermute x10, waiting for transfers between devices: 4.6 us -> 5.11 us  [exchange(): lax.ppermute(value, 'freq', [(i, partner(i)) for i in range(device_count)])]
  transfers between devices with their start and end apart: 10 -> 10, of which waited for: 5 -> 5; matrix products, arithmetic and copies ran while one was open for 0% -> 0% of each run, Pallas kernels for 5% -> 3%
where the time goes in v8:
time: 30.6 us; the launch traced here: 30.4 us
  blocking collectives  11 us (36%)
  starting transfers between devices  10.5 us (34%)
  waiting for transfers between devices  5.11 us (17%)
  Pallas kernels  3.04 us (10%)
  between operations  0.69 us (2%)
    all_to_all x1, blocking collectives, local(): lax.all_to_all(outgoing, 'freq', 0, 0, tiled=True).reshape(side, -1)  11 us
    ppermute x10, starting transfers between devices, exchange(): lax.ppermute(value, 'freq', [(i, partner(i)) for i in range(device_count)])  10.5 us
    ppermute x10, waiting for transfers between devices, exchange(): lax.ppermute(value, 'freq', [(i, partner(i)) for i in range(device_count)])  5.11 us
    pallas_call x1, Pallas kernels, local(): pl.pallas_call(last_kernel, out_shape=(jax.ShapeDtypeStruct((templ_count,...  1.07 us
    pallas_call x1, Pallas kernels, local(): pl.pallas_call(prepare_kernel, out_shape=results, in_specs=[hbm] * 5, out...  1.05 us
  transfers between devices with their start and end apart: 10, of which 5 were waited for; matrix products, arithmetic and copies ran while one was open for 0% of the time, Pallas kernels for 3%

profile of v8, /device:TPU:0, one launch (start us, length us, event | category | flops | bytes accessed | tf_op | source)
XLA Modules:
  0.0 30.4 jit_solution(12145028525894886984)
XLA Ops:
  0.6 0.0 copy-start
  0.6 0.0 slice-start
  0.7 0.5 %collective-permute-start = (f32[16,512]{1,0:T(8,128)}, f32[16,512]{1,0:T(8,128)S(1)}, u32[]{:S(2)}, u32[]{:S(2)}) collective-permute-start(f32[16,512]{1,0:T(8,128)} %strain.1), channel_id=1, source_target_pairs={{0,1},{1,0},{2,3},{3,2},{4,5},{5,4},{6,7},{7,6},{8,9},{9,8},{10,11... | collective-permute-start | bytes 98312 | tf_op jit(solution)/shard_map/ppermute | solution.py:250
  1.2 3.6 %collective-permute-start.3 = (f32[16,512]{1,0:T(8,128)}, f32[16,512]{1,0:T(8,128)S(1)}, u32[]{:S(2)}, u32[]{:S(2)}) collective-permute-start(f32[16,512]{1,0:T(8,128)} %strain.1), channel_id=1, source_target_pairs={{0,7},{1,6},{2,5},{3,4},{4,3},{5,2},{6,1},{7,0},{8,15},{9,14},{10,... | collective-permute-start | bytes 98312 | tf_op jit(solution)/shard_map/ppermute | solution.py:250
  4.7 0.2 collective-permute-start.1
  4.9 0.0 collective-permute-done.refs_1_
  5.0 1.5 %collective-permute-start.2 = (f32[16,512]{1,0:T(8,128)S(1)}, f32[16,512]{1,0:T(8,128)S(1)}, u32[]{:S(2)}, u32[]{:S(2)}) collective-permute-start(f32[16,512]{1,0:T(8,128)S(1)} %collective-permute-done.refs_1_), channel_id=1, source_target_pairs={{0,3},{1,4},{2,7},{3,0},{4,1},{5,6},{6,5},{7,2},{8,11},{9,12},{10,... | collective-permute-start | bytes 98312 | tf_op jit(solution)/shard_map/ppermute | solution.py:250
  6.5 1.1 %shard_map.86 = (bf16[256,128]{1,0:T(8,128)(2,1)S(1)}, f32[2,64,512]{2,1,0:T(8,128)S(1)}, f32[16,512]{1,0:T(8,128)S(1)}, f32[16,256]{1,0:T(8,128)S(1)}, f32[4,256]{1,0:T(4,128)S(1)}) custom-call(bf16[32,256,128]{2,1,0:T(8,128)(2,1)} %constant.6.clone.forwards, f32[32,2,64,512]{3,2,1,0:T(8,128)} %constant.7.clone.twists, f32[16,512]{1,0:T(8,128)} %strain.1, ...), custom_call_target="tpu_custom_call" | custom-call | bytes 3145728 | tf_op jit(solution)/shard_map/pallas_call | solution.py:265
  7.6 0.0 collective-permute-done.3.refs_4_
  7.6 0.1 collective-permute-start.6
  7.7 0.6 %collective-permute-done.1.refs_2_ = f32[16,512]{1,0:T(8,128)S(1)} collective-permute-done((f32[16,512]{1,0:T(8,128)}, f32[16,512]{1,0:T(8,128)S(1)}, u32[]{:S(2)}, u32[]{:S(2)}) %collective-permute-start.1) | collective-permute-done | bytes 32800 | tf_op jit(solution)/shard_map/ppermute | solution.py:250
  8.3 0.4 %collective-permute-start.4 = (f32[16,512]{1,0:T(8,128)S(1)}, f32[16,512]{1,0:T(8,128)S(1)}, u32[]{:S(2)}, u32[]{:S(2)}) collective-permute-start(f32[16,512]{1,0:T(8,128)S(1)} %collective-permute-done.1.refs_2_), channel_id=1, source_target_pairs={{0,1},{1,0},{2,3},{3,2},{4,5},{5,4},{6,7},{7,6},{8,9},{9,8},{10,11... | collective-permute-start | bytes 98312 | tf_op jit(solution)/shard_map/ppermute | solution.py:250
  8.7 0.2 collective-permute-start.5
  8.8 0.0 collective-permute-done.6.refs_7_
  8.8 0.7 %collective-permute-done.4.refs_5_ = f32[16,512]{1,0:T(8,128)S(1)} collective-permute-done((f32[16,512]{1,0:T(8,128)S(1)}, f32[16,512]{1,0:T(8,128)S(1)}, u32[]{:S(2)}, u32[]{:S(2)}) %collective-permute-start.4) | collective-permute-done | bytes 32800 | tf_op jit(solution)/shard_map/ppermute | solution.py:250
  9.5 0.4 %collective-permute-done.5.refs_6_ = f32[16,512]{1,0:T(8,128)S(1)} collective-permute-done((f32[16,512]{1,0:T(8,128)S(1)}, f32[16,512]{1,0:T(8,128)S(1)}, u32[]{:S(2)}, u32[]{:S(2)}) %collective-permute-start.5) | collective-permute-done | bytes 32800 | tf_op jit(solution)/shard_map/ppermute | solution.py:250
  9.9 0.6 %shard_map.87 = (f32[32,256]{1,0:T(8,128)S(1)}, bf16[32,256]{1,0:T(8,128)(2,1)S(1)}, bf16[32,256]{1,0:T(8,128)(2,1)S(1)}, bf16[32,256]{1,0:T(8,128)(2,1)S(1)}) custom-call(f32[16,512]{1,0:T(8,128)S(1)} %get-tuple-element.22.refs_0_, f32[16,512]{1,0:T(8,128)S(1)} %collective-permute-done.refs_1_, f32[16,512]{1,0:T(8,128)S(1)} %collective-permute-done.1.refs_2_, ...), custom_call_target="tpu_custom_call" | custom-call | tf_op jit(solution)/shard_map/pallas_call | solution.py:282
  10.5 3.4 %collective-permute-start.7 = (bf16[32,256]{1,0:T(8,128)(2,1)S(1)}, bf16[32,256]{1,0:T(8,128)(2,1)S(1)}, u32[]{:S(2)}, u32[]{:S(2)}) collective-permute-start(bf16[32,256]{1,0:T(8,128)(2,1)S(1)} %get-tuple-element.36), channel_id=1, source_target_pairs={{0,25},{1,24},{2,27},{3,26},{4,29},{5,28},{6,31},{7,30},{8,17},{9,... | collective-permute-start | bytes 49160 | tf_op jit(solution)/shard_map/ppermute | solution.py:250
  13.9 0.6 %collective-permute-start.9 = (bf16[32,256]{1,0:T(8,128)(2,1)S(1)}, bf16[32,256]{1,0:T(8,128)(2,1)S(1)}, u32[]{:S(2)}, u32[]{:S(2)}) collective-permute-start(bf16[32,256]{1,0:T(8,128)(2,1)S(1)} %get-tuple-element.38), channel_id=1, source_target_pairs={{0,9},{1,8},{2,11},{3,10},{4,13},{5,12},{6,15},{7,14},{8,1},{9,0},... | collective-permute-start | bytes 49160 | tf_op jit(solution)/shard_map/ppermute | solution.py:250
  14.5 1.0 %collective-permute-done.7.refs_1_ = bf16[32,256]{1,0:T(8,128)(2,1)S(1)} collective-permute-done((bf16[32,256]{1,0:T(8,128)(2,1)S(1)}, bf16[32,256]{1,0:T(8,128)(2,1)S(1)}, u32[]{:S(2)}, u32[]{:S(2)}) %collective-permute-start.7) | collective-permute-done | bytes 16416 | tf_op jit(solution)/shard_map/ppermute | solution.py:250
  15.5 2.5 %collective-permute-done.8.refs_2_ = bf16[32,256]{1,0:T(8,128)(2,1)S(1)} collective-permute-done((bf16[32,256]{1,0:T(8,128)(2,1)S(1)}, bf16[32,256]{1,0:T(8,128)(2,1)S(1)}, u32[]{:S(2)}, u32[]{:S(2)}) %collective-permute-start.8) | collective-permute-done | bytes 16416 | tf_op jit(solution)/shard_map/ppermute | solution.py:250
  18.0 0.3 %shard_map.88 = bf16[32,16,128]{2,1,0:T(8,128)(2,1)S(1)} custom-call(f32[32,256]{1,0:T(8,128)S(1)} %get-tuple-element.35.refs_0_, bf16[32,256]{1,0:T(8,128)(2,1)S(1)} %collective-permute-done.7.refs_1_, bf16[32,256]{1,0:T(8,128)(2,1)S(1)} %collective-permute-done.8.refs_2_, bf16[32,256]{1,0:T(8,128)(2,1)S(1)} %collective-permute-done.9.refs_3_, ...), custom_call_target="tpu_custom_call" | custom-call | tf_op jit(solution)/shard_map/pallas_call | solution.py:298
  18.3 11.0 %all_to_all.5 = bf16[32,16,128]{2,1,0:T(8,128)(2,1)S(1)} all-to-all(bf16[32,16,128]{2,1,0:T(8,128)(2,1)S(1)} %shard_map.88), channel_id=1, replica_groups=mesh['tmpl'=1,'freq'=32] {'freq'}, dimensions={0} | all-to-all | bytes 262144 | tf_op jit(solution)/shard_map/all_to_all | solution.py:310
  29.4 1.1 %shard_map.89 = (f32[4,2,16,512]{3,2,1,0:T(8,128)}, f32[16,512]{1,0:T(8,128)}) custom-call(bf16[512,128]{1,0:T(8,128)(2,1)S(1)} %bitcast.4, bf16[512,1536]{1,0:T(8,128)(2,1)S(1)} %copy-done), custom_call_target="tpu_custom_call" | custom-call | tf_op jit(solution)/shard_map/pallas_call | solution.py:312
  (6 shorter events, 0.0 us)
Async XLA Ops:
  0.6 9.2 %copy-start = (bf16[512,1536]{1,0:T(8,128)(2,1)S(1)}, bf16[512,1536]{1,0:T(8,128)(2,1)}, u32[]{:S(2)}) copy-start(bf16[512,1536]{1,0:T(8,128)(2,1)} %constant.8.clone.refs_10_.refs_8_.table) | copy-start | bytes 4718596
  0.6 8.2 %slice-start = ((bf16[16,4,2,512]{3,2,1,0:T(2,128)(2,1)}), bf16[16,4,2,256]{3,2,1,0:T(2,128)(2,1)S(1)}, s32[]{:S(2)}) async-start(bf16[16,4,2,512]{3,2,1,0:T(2,128)(2,1)} %param.9), calls=%async_computation.1 | async-start | bytes 131072 | tf_op jit(solution)/shard_map/slice | solution.py:278
  0.7 4.3 %collective-permute-start = (f32[16,512]{1,0:T(8,128)}, f32[16,512]{1,0:T(8,128)S(1)}, u32[]{:S(2)}, u32[]{:S(2)}) collective-permute-start(f32[16,512]{1,0:T(8,128)} %strain.1), channel_id=1, source_target_pairs={{0,1},{1,0},{2,3},{3,2},{4,5},{5,4},{6,7},{7,6},{8,9},{9,8},{10,11... | collective-permute-start | bytes 98312 | tf_op jit(solution)/shard_map/ppermute | solution.py:250
  1.2 6.4 %collective-permute-start.3 = (f32[16,512]{1,0:T(8,128)}, f32[16,512]{1,0:T(8,128)S(1)}, u32[]{:S(2)}, u32[]{:S(2)}) collective-permute-start(f32[16,512]{1,0:T(8,128)} %strain.1), channel_id=1, source_target_pairs={{0,7},{1,6},{2,5},{3,4},{4,3},{5,2},{6,1},{7,0},{8,15},{9,14},{10,... | collective-permute-start | bytes 98312 | tf_op jit(solution)/shard_map/ppermute | solution.py:250
  4.7 3.6 %collective-permute-start.1 = (f32[16,512]{1,0:T(8,128)}, f32[16,512]{1,0:T(8,128)S(1)}, u32[]{:S(2)}, u32[]{:S(2)}) collective-permute-start(f32[16,512]{1,0:T(8,128)} %strain.1), channel_id=1, source_target_pairs={{0,3},{1,4},{2,7},{3,0},{4,1},{5,6},{6,5},{7,2},{8,11},{9,12},{10,... | collective-permute-start | bytes 98312 | tf_op jit(solution)/shard_map/ppermute | solution.py:250
  5.0 3.7 %collective-permute-start.2 = (f32[16,512]{1,0:T(8,128)S(1)}, f32[16,512]{1,0:T(8,128)S(1)}, u32[]{:S(2)}, u32[]{:S(2)}) collective-permute-start(f32[16,512]{1,0:T(8,128)S(1)} %collective-permute-done.refs_1_), channel_id=1, source_target_pairs={{0,3},{1,4},{2,7},{3,0},{4,1},{5,6},{6,5},{7,2},{8,11},{9,12},{10,... | collective-permute-start | bytes 98312 | tf_op jit(solution)/shard_map/ppermute | solution.py:250
  7.6 1.3 %collective-permute-start.6 = (f32[16,512]{1,0:T(8,128)S(1)}, f32[16,512]{1,0:T(8,128)S(1)}, u32[]{:S(2)}, u32[]{:S(2)}) collective-permute-start(f32[16,512]{1,0:T(8,128)S(1)} %collective-permute-done.3.refs_4_), channel_id=1, source_target_pairs={{0,1},{1,0},{2,3},{3,2},{4,5},{5,4},{6,7},{7,6},{8,9},{9,8},{10,11... | collective-permute-start | bytes 98312 | tf_op jit(solution)/shard_map/ppermute | solution.py:250
  8.3 1.2 %collective-permute-start.4 = (f32[16,512]{1,0:T(8,128)S(1)}, f32[16,512]{1,0:T(8,128)S(1)}, u32[]{:S(2)}, u32[]{:S(2)}) collective-permute-start(f32[16,512]{1,0:T(8,128)S(1)} %collective-permute-done.1.refs_2_), channel_id=1, source_target_pairs={{0,1},{1,0},{2,3},{3,2},{4,5},{5,4},{6,7},{7,6},{8,9},{9,8},{10,11... | collective-permute-start | bytes 98312 | tf_op jit(solution)/shard_map/ppermute | solution.py:250
  8.7 1.2 %collective-permute-start.5 = (f32[16,512]{1,0:T(8,128)S(1)}, f32[16,512]{1,0:T(8,128)S(1)}, u32[]{:S(2)}, u32[]{:S(2)}) collective-permute-start(f32[16,512]{1,0:T(8,128)S(1)} %collective-permute-done.2.refs_3_), channel_id=1, source_target_pairs={{0,1},{1,0},{2,3},{3,2},{4,5},{5,4},{6,7},{7,6},{8,9},{9,8},{10,11... | collective-permute-start | bytes 98312 | tf_op jit(solution)/shard_map/ppermute | solution.py:250
  10.5 5.0 %collective-permute-start.7 = (bf16[32,256]{1,0:T(8,128)(2,1)S(1)}, bf16[32,256]{1,0:T(8,128)(2,1)S(1)}, u32[]{:S(2)}, u32[]{:S(2)}) collective-permute-start(bf16[32,256]{1,0:T(8,128)(2,1)S(1)} %get-tuple-element.36), channel_id=1, source_target_pairs={{0,25},{1,24},{2,27},{3,26},{4,29},{5,28},{6,31},{7,30},{8,17},{9,... | collective-permute-start | bytes 49160 | tf_op jit(solution)/shard_map/ppermute | solution.py:250
  13.9 4.1 %collective-permute-start.8 = (bf16[32,256]{1,0:T(8,128)(2,1)S(1)}, bf16[32,256]{1,0:T(8,128)(2,1)S(1)}, u32[]{:S(2)}, u32[]{:S(2)}) collective-permute-start(bf16[32,256]{1,0:T(8,128)(2,1)S(1)} %get-tuple-element.37), channel_id=1, source_target_pairs={{0,17},{1,16},{2,19},{3,18},{4,21},{5,20},{6,23},{7,22},{8,25},{9,... | collective-permute-start | bytes 49160 | tf_op jit(solution)/shard_map/ppermute | solution.py:250
  13.9 4.1 %collective-permute-start.9 = (bf16[32,256]{1,0:T(8,128)(2,1)S(1)}, bf16[32,256]{1,0:T(8,128)(2,1)S(1)}, u32[]{:S(2)}, u32[]{:S(2)}) collective-permute-start(bf16[32,256]{1,0:T(8,128)(2,1)S(1)} %get-tuple-element.38), channel_id=1, source_target_pairs={{0,9},{1,8},{2,11},{3,10},{4,13},{5,12},{6,15},{7,14},{8,1},{9,0},... | collective-permute-start | bytes 49160 | tf_op jit(solution)/shard_map/ppermute | solution.py:250

commit v9 on v7

--- a/solution.py
+++ b/solution.py
@@ -293,7 +293,7 @@
         parts = [
             jnp.concatenate([x[m * rows : (m + 1) * rows] for x in (real, imag)], 0).astype(sent_as[m]) for m in range(outer)
         ]
-    parts, by_templ = lax.optimization_barrier((list(parts), by_templ))
+    parts = list(parts)
     received = [exchange(parts[step], functools.partial(line, step=step)) for step in reversed(range(1, outer))]
     parts = parts[:1] + received
     if tiles_fit:

time: 30.6 us -> 30.6 us (level)
  no operation moved by 1% of the time
where the time goes in v9:
time: 30.6 us; the launch traced here: 30.4 us
  blocking collectives  11 us (36%)
  starting transfers between devices  10.5 us (34%)
  waiting for transfers between devices  4.6 us (15%)
  Pallas kernels  3.61 us (12%)
  between operations  0.68 us (2%)
    all_to_all x1, blocking collectives, local(): lax.all_to_all(outgoing, 'freq', 0, 0, tiled=True).reshape(side, -1)  11 us
    ppermute x10, starting transfers between devices, exchange(): lax.ppermute(value, 'freq', [(i, partner(i)) for i in range(device_count)])  10.5 us
    ppermute x10, waiting for transfers between devices, exchange(): lax.ppermute(value, 'freq', [(i, partner(i)) for i in range(device_count)])  4.6 us
    pallas_call x1, Pallas kernels, local(): pl.pallas_call(prepare_kernel, out_shape=results, in_specs=[hbm] * 6, out...  1.62 us
    pallas_call x1, Pallas kernels, local(): pl.pallas_call(last_kernel, out_shape=(jax.ShapeDtypeStruct((templ_count,...  1.07 us
  transfers between devices with their start and end apart: 10, of which 5 were waited for; matrix products, arithmetic and copies ran while one was open for 0% of the time, Pallas kernels for 5%

profile of v9, /device:TPU:0, one launch (start us, length us, event | category | flops | bytes accessed | tf_op | source)
XLA Modules:
  0.0 30.4 jit_solution(5747099246154314278)
XLA Ops:
  0.6 0.5 %collective-permute-start = (f32[16,512]{1,0:T(8,128)}, f32[16,512]{1,0:T(8,128)S(1)}, u32[]{:S(2)}, u32[]{:S(2)}) collective-permute-start(f32[16,512]{1,0:T(8,128)} %strain.1), channel_id=1, source_target_pairs={{0,1},{1,0},{2,3},{3,2},{4,5},{5,4},{6,7},{7,6},{8,9},{9,8},{10,11... | collective-permute-start | bytes 98312 | tf_op jit(solution)/shard_map/ppermute | solution.py:251
  1.1 3.6 %collective-permute-start.3 = (f32[16,512]{1,0:T(8,128)}, f32[16,512]{1,0:T(8,128)S(1)}, u32[]{:S(2)}, u32[]{:S(2)}) collective-permute-start(f32[16,512]{1,0:T(8,128)} %strain.1), channel_id=1, source_target_pairs={{0,7},{1,6},{2,5},{3,4},{4,3},{5,2},{6,1},{7,0},{8,15},{9,14},{10,... | collective-permute-start | bytes 98312 | tf_op jit(solution)/shard_map/ppermute | solution.py:251
  4.7 0.2 collective-permute-start.1
  4.9 0.0 collective-permute-done.refs_1_
  4.9 1.5 %collective-permute-start.2 = (f32[16,512]{1,0:T(8,128)S(1)}, f32[16,512]{1,0:T(8,128)S(1)}, u32[]{:S(2)}, u32[]{:S(2)}) collective-permute-start(f32[16,512]{1,0:T(8,128)S(1)} %collective-permute-done.refs_1_), channel_id=1, source_target_pairs={{0,3},{1,4},{2,7},{3,0},{4,1},{5,6},{6,5},{7,2},{8,11},{9,12},{10,... | collective-permute-start | bytes 98312 | tf_op jit(solution)/shard_map/ppermute | solution.py:251
  6.5 1.6 %shard_map.86 = (bf16[256,128]{1,0:T(8,128)(2,1)S(1)}, f32[2,64,512]{2,1,0:T(8,128)S(1)}, bf16[512,1536]{1,0:T(8,128)(2,1)S(1)}, f32[16,512]{1,0:T(8,128)S(1)}, ...) custom-call(bf16[32,256,128]{2,1,0:T(8,128)(2,1)} %constant.6.clone.forwards, f32[32,2,64,512]{3,2,1,0:T(8,128)} %constant.7.clone.twists, ...), custom_call_target="tpu_custom_call" | custom-call | bytes 3145728 | tf_op jit(solution)/shard_map/pallas_call | solution.py:267
  8.1 0.0 slice-start
  8.1 0.1 collective-permute-start.6
  8.2 0.0 collective-permute-done.1.refs_2_
  8.3 0.4 %collective-permute-start.4 = (f32[16,512]{1,0:T(8,128)S(1)}, f32[16,512]{1,0:T(8,128)S(1)}, u32[]{:S(2)}, u32[]{:S(2)}) collective-permute-start(f32[16,512]{1,0:T(8,128)S(1)} %collective-permute-done.1.refs_2_), channel_id=1, source_target_pairs={{0,1},{1,0},{2,3},{3,2},{4,5},{5,4},{6,7},{7,6},{8,9},{9,8},{10,11... | collective-permute-start | bytes 98312 | tf_op jit(solution)/shard_map/ppermute | solution.py:251
  8.7 0.0 collective-permute-done.2.refs_3_
  8.7 0.1 collective-permute-start.5
  8.8 0.6 %collective-permute-done.6.refs_7_ = f32[16,512]{1,0:T(8,128)S(1)} collective-permute-done((f32[16,512]{1,0:T(8,128)S(1)}, f32[16,512]{1,0:T(8,128)S(1)}, u32[]{:S(2)}, u32[]{:S(2)}) %collective-permute-start.6) | collective-permute-done | bytes 32800 | tf_op jit(solution)/shard_map/ppermute | solution.py:251
  9.4 0.2 collective-permute-done.4.refs_5_
  9.6 0.4 %collective-permute-done.5.refs_6_ = f32[16,512]{1,0:T(8,128)S(1)} collective-permute-done((f32[16,512]{1,0:T(8,128)S(1)}, f32[16,512]{1,0:T(8,128)S(1)}, u32[]{:S(2)}, u32[]{:S(2)}) %collective-permute-start.5) | collective-permute-done | bytes 32800 | tf_op jit(solution)/shard_map/ppermute | solution.py:251
  9.9 0.6 %shard_map.87 = (f32[32,256]{1,0:T(8,128)S(1)}, bf16[32,256]{1,0:T(8,128)(2,1)S(1)}, bf16[32,256]{1,0:T(8,128)(2,1)S(1)}, bf16[32,256]{1,0:T(8,128)(2,1)S(1)}) custom-call(f32[16,512]{1,0:T(8,128)S(1)} %get-tuple-element.18.refs_0_, f32[16,512]{1,0:T(8,128)S(1)} %collective-permute-done.refs_1_, f32[16,512]{1,0:T(8,128)S(1)} %collective-permute-done.1.refs_2_, ...), custom_call_target="tpu_custom_call" | custom-call | tf_op jit(solution)/shard_map/pallas_call | solution.py:284
  10.5 3.4 %collective-permute-start.7 = (bf16[32,256]{1,0:T(8,128)(2,1)S(1)}, bf16[32,256]{1,0:T(8,128)(2,1)S(1)}, u32[]{:S(2)}, u32[]{:S(2)}) collective-permute-start(bf16[32,256]{1,0:T(8,128)(2,1)S(1)} %get-tuple-element.29), channel_id=1, source_target_pairs={{0,25},{1,24},{2,27},{3,26},{4,29},{5,28},{6,31},{7,30},{8,17},{9,... | collective-permute-start | bytes 49160 | tf_op jit(solution)/shard_map/ppermute | solution.py:251
  13.9 0.0 collective-permute-start.8
  14.0 0.6 %collective-permute-start.9 = (bf16[32,256]{1,0:T(8,128)(2,1)S(1)}, bf16[32,256]{1,0:T(8,128)(2,1)S(1)}, u32[]{:S(2)}, u32[]{:S(2)}) collective-permute-start(bf16[32,256]{1,0:T(8,128)(2,1)S(1)} %get-tuple-element.31), channel_id=1, source_target_pairs={{0,9},{1,8},{2,11},{3,10},{4,13},{5,12},{6,15},{7,14},{8,1},{9,0},... | collective-permute-start | bytes 49160 | tf_op jit(solution)/shard_map/ppermute | solution.py:251
  14.6 1.0 %collective-permute-done.7.refs_1_ = bf16[32,256]{1,0:T(8,128)(2,1)S(1)} collective-permute-done((bf16[32,256]{1,0:T(8,128)(2,1)S(1)}, bf16[32,256]{1,0:T(8,128)(2,1)S(1)}, u32[]{:S(2)}, u32[]{:S(2)}) %collective-permute-start.7) | collective-permute-done | bytes 16416 | tf_op jit(solution)/shard_map/ppermute | solution.py:251
  15.5 2.5 %collective-permute-done.8.refs_2_ = bf16[32,256]{1,0:T(8,128)(2,1)S(1)} collective-permute-done((bf16[32,256]{1,0:T(8,128)(2,1)S(1)}, bf16[32,256]{1,0:T(8,128)(2,1)S(1)}, u32[]{:S(2)}, u32[]{:S(2)}) %collective-permute-start.8) | collective-permute-done | bytes 16416 | tf_op jit(solution)/shard_map/ppermute | solution.py:251
  18.0 0.3 %shard_map.88 = bf16[32,16,128]{2,1,0:T(8,128)(2,1)S(1)} custom-call(f32[32,256]{1,0:T(8,128)S(1)} %get-tuple-element.28.refs_0_, bf16[32,256]{1,0:T(8,128)(2,1)S(1)} %collective-permute-done.7.refs_1_, bf16[32,256]{1,0:T(8,128)(2,1)S(1)} %collective-permute-done.8.refs_2_, bf16[32,256]{1,0:T(8,128)(2,1)S(1)} %collective-permute-done.9.refs_3_, ...), custom_call_target="tpu_custom_call" | custom-call | tf_op jit(solution)/shard_map/pallas_call | solution.py:300
  18.4 11.0 %all_to_all.5 = bf16[32,16,128]{2,1,0:T(8,128)(2,1)S(1)} all-to-all(bf16[32,16,128]{2,1,0:T(8,128)(2,1)S(1)} %shard_map.88), channel_id=1, replica_groups=mesh['tmpl'=1,'freq'=32] {'freq'}, dimensions={0} | all-to-all | bytes 262144 | tf_op jit(solution)/shard_map/all_to_all | solution.py:312
  29.3 1.1 %shard_map.89 = (f32[4,2,16,512]{3,2,1,0:T(8,128)}, f32[16,512]{1,0:T(8,128)}) custom-call(bf16[512,128]{1,0:T(8,128)(2,1)S(1)} %bitcast.4, bf16[512,1536]{1,0:T(8,128)(2,1)S(1)} %get-tuple-element.27.refs_10_.refs_8_.table), custom_call_target="tpu_custom_call" | custom-call | tf_op jit(solution)/shard_map/pallas_call | solution.py:314
  (4 shorter events, 0.0 us)
Async XLA Ops:
  0.6 4.3 %collective-permute-start = (f32[16,512]{1,0:T(8,128)}, f32[16,512]{1,0:T(8,128)S(1)}, u32[]{:S(2)}, u32[]{:S(2)}) collective-permute-start(f32[16,512]{1,0:T(8,128)} %strain.1), channel_id=1, source_target_pairs={{0,1},{1,0},{2,3},{3,2},{4,5},{5,4},{6,7},{7,6},{8,9},{9,8},{10,11... | collective-permute-start | bytes 98312 | tf_op jit(solution)/shard_map/ppermute | solution.py:251
  1.1 7.0 %collective-permute-start.3 = (f32[16,512]{1,0:T(8,128)}, f32[16,512]{1,0:T(8,128)S(1)}, u32[]{:S(2)}, u32[]{:S(2)}) collective-permute-start(f32[16,512]{1,0:T(8,128)} %strain.1), channel_id=1, source_target_pairs={{0,7},{1,6},{2,5},{3,4},{4,3},{5,2},{6,1},{7,0},{8,15},{9,14},{10,... | collective-permute-start | bytes 98312 | tf_op jit(solution)/shard_map/ppermute | solution.py:251
  4.7 3.6 %collective-permute-start.1 = (f32[16,512]{1,0:T(8,128)}, f32[16,512]{1,0:T(8,128)S(1)}, u32[]{:S(2)}, u32[]{:S(2)}) collective-permute-start(f32[16,512]{1,0:T(8,128)} %strain.1), channel_id=1, source_target_pairs={{0,3},{1,4},{2,7},{3,0},{4,1},{5,6},{6,5},{7,2},{8,11},{9,12},{10,... | collective-permute-start | bytes 98312 | tf_op jit(solution)/shard_map/ppermute | solution.py:251
  4.9 3.8 %collective-permute-start.2 = (f32[16,512]{1,0:T(8,128)S(1)}, f32[16,512]{1,0:T(8,128)S(1)}, u32[]{:S(2)}, u32[]{:S(2)}) collective-permute-start(f32[16,512]{1,0:T(8,128)S(1)} %collective-permute-done.refs_1_), channel_id=1, source_target_pairs={{0,3},{1,4},{2,7},{3,0},{4,1},{5,6},{6,5},{7,2},{8,11},{9,12},{10,... | collective-permute-start | bytes 98312 | tf_op jit(solution)/shard_map/ppermute | solution.py:251
  8.1 6.5 %slice-start = ((bf16[16,4,2,512]{3,2,1,0:T(2,128)(2,1)}), bf16[16,4,2,256]{3,2,1,0:T(2,128)(2,1)S(1)}, s32[]{:S(2)}) async-start(bf16[16,4,2,512]{3,2,1,0:T(2,128)(2,1)} %param.9), calls=%async_computation.1 | async-start | bytes 131072 | tf_op jit(solution)/shard_map/slice | solution.py:280
  8.1 1.3 %collective-permute-start.6 = (f32[16,512]{1,0:T(8,128)S(1)}, f32[16,512]{1,0:T(8,128)S(1)}, u32[]{:S(2)}, u32[]{:S(2)}) collective-permute-start(f32[16,512]{1,0:T(8,128)S(1)} %collective-permute-done.3.refs_4_), channel_id=1, source_target_pairs={{0,1},{1,0},{2,3},{3,2},{4,5},{5,4},{6,7},{7,6},{8,9},{9,8},{10,11... | collective-permute-start | bytes 98312 | tf_op jit(solution)/shard_map/ppermute | solution.py:251
  8.3 1.3 %collective-permute-start.4 = (f32[16,512]{1,0:T(8,128)S(1)}, f32[16,512]{1,0:T(8,128)S(1)}, u32[]{:S(2)}, u32[]{:S(2)}) collective-permute-start(f32[16,512]{1,0:T(8,128)S(1)} %collective-permute-done.1.refs_2_), channel_id=1, source_target_pairs={{0,1},{1,0},{2,3},{3,2},{4,5},{5,4},{6,7},{7,6},{8,9},{9,8},{10,11... | collective-permute-start | bytes 98312 | tf_op jit(solution)/shard_map/ppermute | solution.py:251
  8.7 1.2 %collective-permute-start.5 = (f32[16,512]{1,0:T(8,128)S(1)}, f32[16,512]{1,0:T(8,128)S(1)}, u32[]{:S(2)}, u32[]{:S(2)}) collective-permute-start(f32[16,512]{1,0:T(8,128)S(1)} %collective-permute-done.2.refs_3_), channel_id=1, source_target_pairs={{0,1},{1,0},{2,3},{3,2},{4,5},{5,4},{6,7},{7,6},{8,9},{9,8},{10,11... | collective-permute-start | bytes 98312 | tf_op jit(solution)/shard_map/ppermute | solution.py:251
  10.5 5.0 %collective-permute-start.7 = (bf16[32,256]{1,0:T(8,128)(2,1)S(1)}, bf16[32,256]{1,0:T(8,128)(2,1)S(1)}, u32[]{:S(2)}, u32[]{:S(2)}) collective-permute-start(bf16[32,256]{1,0:T(8,128)(2,1)S(1)} %get-tuple-element.29), channel_id=1, source_target_pairs={{0,25},{1,24},{2,27},{3,26},{4,29},{5,28},{6,31},{7,30},{8,17},{9,... | collective-permute-start | bytes 49160 | tf_op jit(solution)/shard_map/ppermute | solution.py:251
  13.9 4.1 %collective-permute-start.8 = (bf16[32,256]{1,0:T(8,128)(2,1)S(1)}, bf16[32,256]{1,0:T(8,128)(2,1)S(1)}, u32[]{:S(2)}, u32[]{:S(2)}) collective-permute-start(bf16[32,256]{1,0:T(8,128)(2,1)S(1)} %get-tuple-element.30), channel_id=1, source_target_pairs={{0,17},{1,16},{2,19},{3,18},{4,21},{5,20},{6,23},{7,22},{8,25},{9,... | collective-permute-start | bytes 49160 | tf_op jit(solution)/shard_map/ppermute | solution.py:251
  14.0 4.1 %collective-permute-start.9 = (bf16[32,256]{1,0:T(8,128)(2,1)S(1)}, bf16[32,256]{1,0:T(8,128)(2,1)S(1)}, u32[]{:S(2)}, u32[]{:S(2)}) collective-permute-start(bf16[32,256]{1,0:T(8,128)(2,1)S(1)} %get-tuple-element.31), channel_id=1, source_target_pairs={{0,9},{1,8},{2,11},{3,10},{4,13},{5,12},{6,15},{7,14},{8,1},{9,0},... | collective-permute-start | bytes 49160 | tf_op jit(solution)/shard_map/ppermute | solution.py:251
